TPU v7x, 32 devices: a whole 2x2x4 slice. The times are simulated.
32 devices in a mesh: ctxouter: 4 (over y, x), ctxinner: 8 (over z, core).
Axes of the slice: x: 2, y: 2, z: 4, core: 2. Of those that a mesh axis runs over, the one named last changes fastest.
Arguments:
- lin_qk: bfloat16 [4096, 512], P(('ctxouter', 'ctxinner')), may hold values from -8 to 8, as said below
- lin_v: bfloat16 [4096, 1024], P(('ctxouter', 'ctxinner')), may hold values from -6 to 6
- conv_w: float32 [3, 1024], replicated, may hold values from -2.5 to 2.5
- swa_qkv: bfloat16 [4096, 3072], P(('ctxouter', 'ctxinner')), may hold values from -8 to 8
Outputs:
- mixed: bfloat16 [4096, 1024], P(('ctxouter', 'ctxinner'))
Inputs may be any that keep to these rules, and one draw needn't show every extreme that they name: `lin_qk`: keys have a scale of their own in each context block and head.
All inputs are finite; a program needn't handle non-finite values.
Results may differ from a plain program's by a relative error of at most 0.0045.
Values may be sent and summed in bfloat16 or wider, within the bound.
No kernel may reach another device: no remote copies, remote signals or barrier semaphores. Data moves between devices by JAX's collectives and lax.ppermute only.
A program may use at most 128 MiB of HBM per device.

v0:
```python
import jax
import jax.numpy as jnp
import numpy as np
from jax import lax
from jax.sharding import PartitionSpec as P

HEADS = 16
FEAT = 16
VHEAD = 64
SWA_HEADS = 8
SWA_HEAD = 128
WINDOW = 64


def passed_along(array, axis, by):
    devices = lax.axis_size(axis)
    pairs = [(i, i + by) for i in range(devices) if 0 <= i + by < devices]
    return lax.ppermute(array, axis, pairs)


def carried_in(part, axis, combine, identity):
    place = lax.axis_index(axis)
    gathered = jax.tree.map(lambda a: lax.all_gather(a, axis), part)
    state = jax.tree.map(lambda a, e: jnp.zeros_like(a) + jnp.asarray(e, a.dtype), part, identity)

    def one(hop, state):
        return combine(
            state, jax.tree.map(lambda a: lax.dynamic_index_in_dim(a, hop, 0, False), gathered)
        )

    return lax.fori_loop(0, place, one, state)


def features(values):
    size = values.shape[1]
    upper, lower = np.triu_indices(size)
    factor = np.where(upper == lower, np.sqrt(0.5), 1.0).astype(np.float32)
    second = values[:, upper, :] * values[:, lower, :] * jnp.asarray(factor)[None, :, None]
    return jnp.concatenate([jnp.ones_like(values[:, :1, :]), values, second], axis=1)


def combine(earlier, later):
    return (earlier[0] + later[0], earlier[1] + later[1])


def shards(lin_qk, lin_v, conv_w, swa_qkv):
    shard_rows = lin_qk.shape[0]
    conv_taps = conv_w.shape[0]
    swa_width = swa_qkv.shape[1] // 3
    reach = WINDOW - 1
    prev_kv, prev_v = passed_along(
        (swa_qkv[shard_rows - reach :, swa_width:], lin_v[shard_rows - (conv_taps - 1) :]),
        ("ctxouter", "ctxinner"),
        1,
    )
    extended_v = jnp.concatenate([prev_v, lin_v], axis=0).astype(jnp.float32)
    conved = conv_w[0] * extended_v[conv_taps - 1 :]
    for conv_lag in range(1, conv_taps):
        conved = (
            conved
            + conv_w[conv_lag]
            * extended_v[conv_taps - 1 - conv_lag : conv_taps - 1 - conv_lag + shard_rows]
        )
    conved = conved.astype(jnp.bfloat16)
    value_heads = conved.reshape(shard_rows, HEADS, VHEAD)
    scaled = lin_qk.astype(jnp.float32).reshape(shard_rows, 2, HEADS, FEAT) * FEAT ** (-0.25)
    query_t = jnp.transpose(scaled[:, 0], (1, 2, 0))
    key_t = jnp.transpose(scaled[:, 1], (1, 2, 0))
    phi_key = features(key_t)
    own_state = jnp.einsum(
        "het,thv->hev", phi_key, value_heads.astype(jnp.float32), precision=lax.Precision.HIGHEST
    )
    own_norm = jnp.sum(phi_key, axis=-1)
    empty = (jnp.zeros_like(own_state), jnp.zeros_like(own_norm))
    all_states, all_norms = (
        lax.all_gather(own_state[None], "ctxinner", axis=0, tiled=True),
        lax.all_gather(own_norm[None], "ctxinner", axis=0, tiled=True),
    )
    member_count = lax.axis_size("ctxinner")
    earlier = (jnp.arange(member_count) < lax.axis_index("ctxinner"))[:, None, None]
    inner_state = jnp.sum(jnp.where(earlier[..., None], all_states, 0.0), axis=0)
    inner_norm = jnp.sum(jnp.where(earlier, all_norms, 0.0), axis=0)
    outer_state, outer_norm = carried_in(
        (jnp.sum(all_states, axis=0), jnp.sum(all_norms, axis=0)), "ctxouter", combine, empty
    )
    past_state = outer_state + inner_state
    past_norm = outer_norm + inner_norm
    phi_query = features(query_t)
    numer = jnp.einsum("het,hev->htv", phi_query, past_state, precision=lax.Precision.HIGHEST)
    denom = jnp.einsum("het,he->ht", phi_query, past_norm, precision=lax.Precision.HIGHEST)
    step_rows = min(512, shard_rows)
    block_num = 0
    finish = (block_num + 1) * step_rows
    score = jnp.einsum("hfq,hfk->hqk", query_t, key_t, precision=lax.Precision.HIGHEST)
    weight = 1.0 + score + 0.5 * score * score
    query_pos = block_num * step_rows + jnp.arange(step_rows)[:, None]
    key_pos = jnp.arange(finish)[None, :]
    weight = jnp.where(key_pos <= query_pos, weight, 0.0).astype(jnp.bfloat16)
    numer_parts = jnp.einsum(
        "hqk,khv->hqv", weight, value_heads, preferred_element_type=jnp.float32
    )
    denom_parts = jnp.sum(weight.astype(jnp.float32), axis=-1)
    numer = numer + numer_parts
    denom = denom + denom_parts
    lin_out = jnp.transpose(numer / denom[..., None], (1, 0, 2)).reshape(shard_rows, HEADS * VHEAD)
    first_block = lax.axis_index(("ctxouter", "ctxinner")) == 0
    extended_kv = jnp.concatenate([prev_kv, swa_qkv[:, swa_width:]], axis=0)
    block_num = 0
    start = block_num * step_rows
    query = swa_qkv[start : start + step_rows, :swa_width].reshape(step_rows, SWA_HEADS, SWA_HEAD)
    keys = extended_kv[:, :swa_width].reshape(step_rows + reach, SWA_HEADS, SWA_HEAD)
    values = extended_kv[:, swa_width:].reshape(step_rows + reach, SWA_HEADS, SWA_HEAD)
    score = jnp.einsum(
        "qhd,khd->hqk", query, keys, preferred_element_type=jnp.float32
    ) * SWA_HEAD ** (-0.5)
    query_pos = jnp.arange(step_rows)[:, None]
    key_pos = jnp.arange(step_rows + reach)[None, :]
    valid = (
        (key_pos >= query_pos)
        & (key_pos <= query_pos + reach)
        & (jnp.logical_not(first_block) | (start + key_pos >= reach))
    )
    score = jnp.where(valid, score, -jnp.inf)
    top = jnp.max(score, axis=-1, keepdims=True)
    expo = jnp.exp(score - top)
    probs = (expo / jnp.sum(expo, axis=-1, keepdims=True)).astype(jnp.bfloat16)
    result = jnp.einsum("hqk,khd->qhd", probs, values, preferred_element_type=jnp.float32)
    swa_parts = result.reshape(step_rows, swa_width)
    return (lin_out + swa_parts).astype(jnp.bfloat16)


def solution(mesh):
    return jax.shard_map(
        shards,
        mesh=mesh,
        in_specs=(
            P(("ctxouter", "ctxinner"), None),
            P(("ctxouter", "ctxinner"), None),
            P(),
            P(("ctxouter", "ctxinner"), None),
        ),
        out_specs=P(("ctxouter", "ctxinner"), None),
        check_vma=False,
    )
```

profile of v0, /device:TPU:6, one launch (start us, length us, event | category | flops | bytes accessed | tf_op | source)
XLA Modules:
  0.0 197.1 jit_solution(9481247151884933903)
XLA Ops:
  6.5 0.0 all-gather.7.cloned.1.call-start
  6.5 0.7 slice.45
  7.3 0.9 copy.70
  8.1 1.9 collective-permute-start
  10.1 0.7 pad_clamp_fusion.1
  10.8 0.7 pad_clamp_fusion
  11.4 0.9 convert_multiply_fusion
  12.4 0.1 copy.61
  12.6 0.7 copy-done.4
  13.3 0.8 gather_fusion.3
  14.1 1.8 gather_fusion.2
  15.9 1.8 gather_fusion
  17.7 1.8 gather_fusion.1
  19.4 3.2 %fusion.10 = (f32[16,136,128]{2,1,0:T(8,128)S(1)}, f32[16,136,128]{2,1,0:T(8,128)S(1)}) fusion(f32[136,16,128]{2,1,0:T(8,128)} %gather_fusion.1, f32[136,16,128]{2,1,0:T(8,128)} %gather_fusion, f32[136]{0:T(256)S(1)} %copy-done.13, f32[136,16,128]{2,1,0:T(8,128)S(1)} %gather_fusion.3, f32[136,16,128]{2,1,0:T(8,128)} %gather_fusion.2), kind=kLoop, calls=%fused_computation.25 | loop fusion | flops 1114112 | bytes 6685216 | tf_op jit(solution)/shard_map/mul | solution.py:38
  22.6 1.1 copy.71
  23.8 0.0 collective-permute-done
  23.8 1.2 maximum_convert_fusion
  25.0 0.7 fusion.22
  25.7 2.5 %fusion.16 = f32[16,153,64]{1,2,0:T(8,128)} fusion(bf16[128,16,64]{0,2,1:T(8,128)(2,1)S(1)} %bitcast.73, f32[16,136,128]{2,1,0:T(8,128)S(1)} %get-tuple-element.77, f32[16,16,128]{2,1,0:T(8,128)S(1)} %get-tuple-element.72, f32[153]{0:T(256)S(1)} %pad.7.clone), kind=kOutput, calls=%fused_computation.32 | convolution fusion | flops 241274880 | bytes 2134628 | tf_op jit(solution)/shard_map/het,thv->hev/dot_general | solution.py:70
  28.3 0.0 all-gather.7.cloned.1.call-update
  28.3 0.0 all-gather.9.cloned.1.call-start
  28.4 83.7 %all-gather.7.cloned.1.call-done = f32[128,153,64]{1,2,0:T(8,128)} async-done(((f32[16,153,64]{1,2,0:T(8,128)}), f32[128,153,64]{1,2,0:T(8,128)}) %all-gather.7.cloned.1.call-update) | async-done | bytes 5013520 | tf_op jit(solution)/shard_map/all_gather | solution.py:76
  112.1 6.3 %select_reduce_fusion = (f32[16,153,64]{1,2,0:T(8,128)}, f32[16,153,64]{1,2,0:T(8,128)}) fusion(f32[8,16,153,64]{2,3,1,0:T(8,128)} %bitcast.71, pred[8]{0:T(512)(128)(4,1)S(1)} %iota_compare_fusion.3), kind=kLoop, calls=%fused_computation.8 | loop fusion | flops 3446784 | bytes 6266888 | tf_op jit(solution)/shard_map/reduce_sum | solution.py:81
  118.4 0.0 all-gather.9.cloned.1.call-update
  118.4 0.0 copy-done.2
  118.4 0.8 slice.51
  119.2 2.1 %collective-permute-start.1 = (bf16[63,2048]{1,0:T(8,128)(2,1)}, bf16[63,2048]{1,0:T(8,128)(2,1)}, u32[]{:S(2)}, u32[]{:S(2)}) collective-permute-start(bf16[63,2048]{1,0:T(8,128)(2,1)} %slice.51), channel_id=1, source_target_pairs={{0,1},{1,2},{2,3},{3,4},{4,5},{5,6},{6,7},{7,8},{8,9},{9,10},{10,1... | collective-permute-start | bytes 774152 | tf_op jit(solution)/shard_map/ppermute | solution.py:18
  121.4 0.8 fusion.15
  122.2 14.0 %all-gather.2 = f32[128,153]{1,0:T(8,128)S(1)} all-gather(f32[16,153]{1,0:T(8,128)S(1)} %fusion.15), channel_id=4, replica_groups=mesh['ctxouter'=4,'ctxinner'=8] {'ctxinner'}, dimensions={0}, use_global_device_ids=true | all-gather | bytes 88128 | tf_op jit(solution)/shard_map/all_gather | solution.py:77
  136.2 0.7 select_reduce_fusion.1
  136.9 0.1 fusion.29
  137.0 3.2 %convert_reduce_fusion = (f32[16,128]{1,0:T(8,128)}, bf16[16,128,128]{1,2,0:T(8,128)(2,1)}) fusion(f32[128,2,16,16]{0,3,2,1:T(8,128)S(1)} %bitcast.81, pred[128,128]{0,1:T(8,128)(4,1)S(1)} %iota_compare_fusion.2), kind=kOutput, calls=%fused_computation.29 | convolution fusion | flops 52426752 | bytes 811008 | tf_op jit(solution)/shard_map/hfq,hfk->hqk/dot_general | solution.py:94
  140.2 8.9 %all-gather.3 = f32[64,153]{1,0:T(8,128)S(1)} all-gather(f32[16,153]{1,0:T(8,128)S(1)} %get-tuple-element.56), channel_id=5, replica_groups=mesh['ctxouter'=4,'ctxinner'=8] {'ctxouter'}, dimensions={0}, use_global_device_ids=true | all-gather | bytes 48960 | tf_op jit(solution)/shard_map/all_gather | solution.py:23
  149.2 0.2 copy.86
  149.3 2.1 %fusion.43 = f32[16,128,64]{1,2,0:T(8,128)} fusion(bf16[128,16,64]{0,2,1:T(8,128)(2,1)S(1)} %bitcast.74, bf16[16,128,128]{1,2,0:T(8,128)(2,1)} %get-tuple-element.79), kind=kOutput, calls=%fused_computation.78 | convolution fusion | flops 33554432 | bytes 1310720 | tf_op jit(solution)/shard_map/hqk,khv->hqv/dot_general | solution.py:99
  151.4 0.0 collective-permute-done.1
  151.4 0.0 slice-done.1
  151.4 1.1 pad_maximum_fusion.5
  152.6 0.1 copy.88
  152.7 0.1 copy.87
  152.8 0.4 fusion.40
  153.2 0.3 fusion.4
  153.4 0.4 fusion.25
  153.9 1.0 copy.80
  154.9 14.3 %all-gather.9.cloned.1.call-done = f32[64,153,64]{1,2,0:T(8,128)} async-done(((f32[16,153,64]{1,2,0:T(8,128)}), f32[64,153,64]{1,2,0:T(8,128)}) %all-gather.9.cloned.1.call-update) | async-done | bytes 2506768 | tf_op jit(solution)/shard_map/all_gather | solution.py:23
  169.2 1.2 broadcast_in_dim.76
  170.4 13.0 %while.12 = (s32[]{:T(128)}, f32[16,153,64]{2,1,0:T(8,128)}, f32[16,153]{1,0:T(8,128)S(1)}, s32[]{:T(128)}, f32[4,16,153,64]{2,3,1,0:T(8,128)}, /*index=5*/f32[4...) while((s32[]{:T(128)}, f32[16,153,64]{2,1,0:T(8,128)}, f32[16,153]{1,0:T(8,128)S(1)}, s32[]{:T(128)}, ...), condition=%wide.region_4.5_spmd, body=%wide.region_3.4_spmd.sunk | while | flops 159125 | bytes 4416335 | solution.py:31
  170.4 1.3 constant_dynamic-slice_fusion.2
  171.7 0.5 copy.112
  172.2 2.5 %bitcast_add_fusion.4 = f32[16,153,64]{2,1,0:T(8,128)} fusion(f32[16,153,64]{2,1,0:T(8,128)} %get-tuple-element.128, f32[1,16,153,64]{3,2,1,0:T(8,128)S(1)} %copy.112), kind=kLoop, calls=%fused_computation.4.clone.1 | loop fusion | flops 156672 | bytes 1880064 | tf_op jit(solution)/shard_map/while/body/add | solution.py:43
  174.8 1.3 constant_dynamic-slice_fusion.2
  176.1 0.5 copy.112
  176.6 2.5 %bitcast_add_fusion.4 = f32[16,153,64]{2,1,0:T(8,128)} fusion(f32[16,153,64]{2,1,0:T(8,128)} %get-tuple-element.128, f32[1,16,153,64]{3,2,1,0:T(8,128)S(1)} %copy.112), kind=kLoop, calls=%fused_computation.4.clone.1 | loop fusion | flops 156672 | bytes 1880064 | tf_op jit(solution)/shard_map/while/body/add | solution.py:43
  179.1 1.3 constant_dynamic-slice_fusion.2
  180.4 0.5 copy.112
  180.9 2.5 %bitcast_add_fusion.4 = f32[16,153,64]{2,1,0:T(8,128)} fusion(f32[16,153,64]{2,1,0:T(8,128)} %get-tuple-element.128, f32[1,16,153,64]{3,2,1,0:T(8,128)S(1)} %copy.112), kind=kLoop, calls=%fused_computation.4.clone.1 | loop fusion | flops 156672 | bytes 1880064 | tf_op jit(solution)/shard_map/while/body/add | solution.py:43
  183.5 1.9 copy.73
  185.5 1.4 fusion.17
  186.9 0.0 copy-done
  186.9 1.6 fusion.6
  188.5 0.0 copy-start.3
  188.5 0.2 copy.79
  188.7 0.8 copy-done.3
  189.5 0.8 add_convert_fusion
  (43 shorter events, 0.3 us)
Async XLA Ops:
  6.5 105.5 %all-gather.7.cloned.1.call-start = ((), (), s32[]{:S(2)}) async-start(), calls=%async_computation | async-start | bytes 9437184 | tf_op jit(solution)/shard_map/all_gather | solution.py:76
  8.1 15.6 %collective-permute-start = (bf16[2,1024]{0,1:T(8,128)(2,1)}, bf16[2,1024]{0,1:T(8,128)(2,1)}, u32[]{:S(2)}, u32[]{:S(2)}) collective-permute-start(bf16[2,1024]{0,1:T(8,128)(2,1)} %copy.70), channel_id=1, source_target_pairs={{0,1},{1,2},{2,3},{3,4},{4,5},{5,6},{6,7},{7,8},{8,9},{9,10},{10,1... | collective-permute-start | bytes 12296 | tf_op jit(solution)/shard_map/ppermute | solution.py:18
  12.5 1.6 copy-start.6
  12.5 0.7 copy-start.4
  17.7 1.8 copy-start.13
  19.4 3.2 %copy-start.11 = (f32[3,1024]{1,0:T(4,128)S(1)}, f32[3,1024]{1,0:T(4,128)}, u32[]{:S(2)}) copy-start(f32[3,1024]{1,0:T(4,128)} %param.18) | copy-start | bytes 36868
  23.8 97.6 %copy-start.9 = (f32[153]{0:T(256)}, f32[153]{0:T(256)S(1)}, u32[]{:S(2)}) copy-start(f32[153]{0:T(256)S(1)} %pad.7.clone) | copy-start | bytes 1840
  28.3 140.9 %all-gather.9.cloned.1.call-start = ((), (), s32[]{:S(2)}) async-start(), calls=%async_computation.1 | async-start | bytes 5242880 | tf_op jit(solution)/shard_map/all_gather | solution.py:23
  112.1 6.4 %copy-start.2 = (bf16[128,3072]{1,0:T(8,128)(2,1)S(1)}, bf16[128,3072]{1,0:T(8,128)(2,1)}, u32[]{:S(2)}) copy-start(bf16[128,3072]{1,0:T(8,128)(2,1)} %param.19) | copy-start | bytes 2359300
  119.2 32.2 %collective-permute-start.1 = (bf16[63,2048]{1,0:T(8,128)(2,1)}, bf16[63,2048]{1,0:T(8,128)(2,1)}, u32[]{:S(2)}, u32[]{:S(2)}) collective-permute-start(bf16[63,2048]{1,0:T(8,128)(2,1)} %slice.51), channel_id=1, source_target_pairs={{0,1},{1,2},{2,3},{3,4},{4,5},{5,6},{6,7},{7,8},{8,9},{9,10},{10,1... | collective-permute-start | bytes 774152 | tf_op jit(solution)/shard_map/ppermute | solution.py:18
  121.4 15.6 %copy-start.7 = (f32[128,512]{0,1:T(8,128)S(1)}, f32[128,512]{0,1:T(8,128)}, u32[]{:S(2)}) copy-start(f32[128,512]{0,1:T(8,128)} %copy-done.6) | copy-start | bytes 786436
  140.2 8.9 %slice-start = ((bf16[128,3072]{1,0:T(8,128)(2,1)}), bf16[128,1024]{1,0:T(8,128)(2,1)S(1)}, s32[]{:S(2)}) async-start(bf16[128,3072]{1,0:T(8,128)(2,1)} %param.19), calls=%async_computation.2 | async-start | bytes 524288 | tf_op jit(solution)/shard_map/slice | solution.py:110
  149.1 2.3 %slice-start.1 = ((bf16[128,3072]{1,0:T(8,128)(2,1)}), bf16[128,2048]{1,0:T(8,128)(2,1)S(1)}, s32[]{:S(2)}) async-start(bf16[128,3072]{1,0:T(8,128)(2,1)} %param.19), calls=%async_computation.3 | async-start | bytes 1048576 | tf_op jit(solution)/shard_map/slice | solution.py:107
  183.4 2.0 %copy-start.8 = (f32[16,153]{1,0:T(8,128)S(1)}, f32[16,153]{1,0:T(8,128)}, u32[]{:S(2)}) copy-start(f32[16,153]{1,0:T(8,128)} %get-tuple-element.55) | copy-start | bytes 29380
  183.5 2.0 %copy-start.5 = (f32[16,16,128]{2,1,0:T(8,128)S(1)}, f32[16,16,128]{2,1,0:T(8,128)}, u32[]{:S(2)}) copy-start(f32[16,16,128]{2,1,0:T(8,128)} %copy-done.4) | copy-start | bytes 393220
  183.5 2.0 %copy-start.10 = (f32[153]{0:T(256)S(1)}, f32[153]{0:T(256)}, u32[]{:S(2)}) copy-start(f32[153]{0:T(256)} %copy-done.9) | copy-start | bytes 1840
  185.4 1.5 copy-start.12
  185.4 1.5 copy-start
  185.4 1.5 copy-start.1
  188.5 1.0 copy-start.3
Sparse Core Ops, SparseCore 0:
  28.4 83.5 all-gather.6
  118.6 50.6 all-gather.8
where the time goes:
time: 198 us; the launch traced here: 197 us
  waiting for transfers between devices  98 us (49%)
  other arithmetic  24.8 us (13%)
  blocking collectives  22.9 us (12%)
  local copies, waits for them, and re-layouts  21.5 us (11%)
  between operations  13.8 us (7%)
  matrix products  12 us (6%)
  starting transfers between devices  4.1 us (2%)
    all_gather x1, waiting for transfers between devices, shards(): lax.all_gather(own_state[None], 'ctxinner', axis=0, tiled=True)  83.7 us
    all_gather x1, waiting for transfers between devices, carried_in(): gathered = jax.tree.map(lambda a: lax.all_gather(a, axis), part)  14.3 us
    all_gather x1, blocking collectives, shards(): lax.all_gather(own_norm[None], 'ctxinner', axis=0, tiled=True)  14 us
    all_gather x1, blocking collectives, carried_in(): gathered = jax.tree.map(lambda a: lax.all_gather(a, axis), part)  8.91 us
    add x6, other arithmetic, combine(): return (earlier[0] + later[0], earlier[1] + later[1])  7.6 us
    reduce_sum x1, other arithmetic, shards(): jnp.sum(jnp.where(earlier[..., None], all_states, 0.0), axis=0)  6.35 us
    dynamic_slice x6, local copies, waits for them, and re-layouts, one(): lax.dynamic_index_in_dim(a, hop, 0, False)  5.4 us
    ppermute x2, starting transfers between devices, passed_along(): return lax.ppermute(array, axis, pairs)  4.06 us
  transfers between devices with their start and end apart: 4, of which 2 were waited for; matrix products, arithmetic and copies ran while one was open for 12% of the time, Pallas kernels for 0%

commit v1 on v0

v1 whole, which is shorter than its diff:
```python
import functools

import jax
import jax.numpy as jnp
import numpy as np
from jax import lax
from jax.experimental import pallas as pl
from jax.experimental.pallas import tpu as pltpu
from jax.sharding import PartitionSpec as P

HEADS = 16
FEAT = 16
VHEAD = 64
SWA_HEADS = 8
SWA_HEAD = 128
WINDOW = 64

AXES = ("ctxouter", "ctxinner")
LANES = 128
PAIRS = HEADS // 2
QUADS = FEAT * (FEAT + 1) // 2
CONST = QUADS + FEAT
ROWS = 160
TAIL = 16
VMEM_LIMIT = 48 * 1024 * 1024

NT = (((1,), (1,)), ((), ()))
NN = (((1,), (0,)), ((), ()))


def dot(a, b, dims=NN):
    return lax.dot_general(a, b, dims, preferred_element_type=jnp.float32)


def selectors():
    upper, lower = np.triu_indices(FEAT)
    scale = FEAT ** (-0.25)
    first = np.zeros((FEAT, ROWS), np.float32)
    second = np.zeros((FEAT, ROWS), np.float32)
    first[upper, np.arange(QUADS)] = scale
    second[lower, np.arange(QUADS)] = scale
    first[np.arange(FEAT), QUADS + np.arange(FEAT)] = scale
    halved = first.copy()
    halved[:, np.arange(QUADS)[upper == lower]] *= 0.5
    add_first = np.zeros((8, ROWS), np.float32)
    add_first[:, CONST] = 1.0
    add_second = np.zeros((8, ROWS), np.float32)
    add_second[:, QUADS : CONST + 1] = 1.0
    return first, second, halved, add_first, add_second


def split_hi_lo(values):
    high = values.astype(jnp.bfloat16)
    return high, (values - high.astype(jnp.float32)).astype(jnp.bfloat16)


def head_mask(head, shape):
    place = lax.broadcasted_iota(jnp.int32, shape, 1)
    return (place >= head * FEAT) & (place < (head + 1) * FEAT)


def state_kernel(first_ref, second_ref, qk_ref, v_ref, tail_ref, conv_ref, cv_ref, state_ref):
    rows = v_ref.shape[0]
    taps = conv_ref.shape[0]
    width = HEADS * FEAT
    key = qk_ref[:, width : 2 * width]
    row_id = lax.broadcasted_iota(jnp.int32, (rows, LANES), 0)
    lane_id = lax.broadcasted_iota(jnp.int32, (ROWS, LANES), 1)
    low_row = lax.broadcasted_iota(jnp.int32, (8, LANES), 0)
    const_rows = jnp.where(lax.broadcasted_iota(jnp.int32, (8, rows), 0) == 0, 1.0, 0.0)
    ones = jnp.ones((8, rows), jnp.bfloat16)
    for pair in range(PAIRS):
        lanes = slice(pair * LANES, (pair + 1) * LANES)
        value = v_ref[:, lanes].astype(jnp.float32)
        tail = tail_ref[:, lanes].astype(jnp.float32)
        conved = conv_ref[0:1, lanes] * value
        for lag in range(1, taps):
            shifted = pltpu.roll(value, lag, 0)
            for row in range(lag):
                source = TAIL - lag + row
                shifted = jnp.where(row_id == row, tail[source : source + 1], shifted)
            conved = conved + conv_ref[lag : lag + 1, lanes] * shifted
        conved = conved.astype(jnp.bfloat16)
        cv_ref[:, lanes] = conved
        states = []
        norms = []
        for head in (2 * pair, 2 * pair + 1):
            own = jnp.where(head_mask(head, key.shape), key, jnp.zeros_like(key))
            one = dot(first_ref[...], own, NT)
            two = dot(second_ref[...], own, NT)
            phi = jnp.concatenate(
                [one[:QUADS] * two[:QUADS], one[QUADS:CONST], const_rows], axis=0
            )
            high, low = split_hi_lo(phi)
            states.append(dot(high, conved) + dot(low, conved))
            norm = dot(ones, high, NT) + dot(ones, low, NT)
            norms.append(norm[:, :LANES])
            norms.append(
                jnp.concatenate(
                    [norm[:, LANES:], jnp.zeros((8, 2 * LANES - ROWS), jnp.float32)], axis=1
                )
            )
        state = jnp.where(lane_id < VHEAD, states[0], states[1])
        last = state[CONST:]
        for place, norm in enumerate(norms):
            last = jnp.where(low_row == 1 + place, norm, last)
        state = jnp.concatenate([state[:CONST], last], axis=0)
        state_ref[pair * ROWS : (pair + 1) * ROWS, :] = state.astype(jnp.bfloat16)


def local_kernel(first_ref, qk_ref, cv_ref, swa_ref, kv_ref, numer_ref, denom_ref, swa_out_ref):
    rows = cv_ref.shape[0]
    width = HEADS * FEAT
    query = qk_ref[:, :width]
    key = qk_ref[:, width : 2 * width]
    lane_id = lax.broadcasted_iota(jnp.int32, (rows, LANES), 1)
    causal = lax.broadcasted_iota(jnp.int32, (rows, rows), 1) <= lax.broadcasted_iota(
        jnp.int32, (rows, rows), 0
    )
    ones = jnp.ones((rows, LANES), jnp.bfloat16)
    for pair in range(PAIRS):
        lanes = slice(pair * LANES, (pair + 1) * LANES)
        conved = cv_ref[:, lanes]
        numers = []
        denoms = []
        for head in (2 * pair, 2 * pair + 1):
            own = jnp.where(head_mask(head, query.shape), query, jnp.zeros_like(query))
            score = dot(own, key, NT) * FEAT ** (-0.5)
            weight = 1.0 + score + 0.5 * score * score
            weight = jnp.where(causal, weight, 0.0).astype(jnp.bfloat16)
            numers.append(dot(weight, conved))
            denoms.append(dot(weight, ones))
        numer_ref[:, lanes] = jnp.where(lane_id < VHEAD, numers[0], numers[1])
        denom_ref[:, lanes] = jnp.where(lane_id < VHEAD, denoms[0], denoms[1])
    swa_width = SWA_HEADS * SWA_HEAD
    not_before = jnp.where(first_ref[0] == 0, WINDOW, 0)
    span = 2 * WINDOW
    place = lax.broadcasted_iota(jnp.int32, (WINDOW, span), 1)
    row = lax.broadcasted_iota(jnp.int32, (WINDOW, span), 0)
    inside = (place > row) & (place <= row + WINDOW)
    inside_first = inside & (place >= not_before)
    for head in range(SWA_HEADS):
        at = head * SWA_HEAD
        for step in range(rows // WINDOW):
            mine = slice(step * WINDOW, (step + 1) * WINDOW)
            query = swa_ref[mine, at : at + SWA_HEAD]
            both = []
            for start in (swa_width + at, 2 * swa_width + at):
                if step == 0:
                    before = kv_ref[:, start - swa_width : start - swa_width + SWA_HEAD]
                    both.append(
                        jnp.concatenate([before, swa_ref[mine, start : start + SWA_HEAD]], axis=0)
                    )
                else:
                    both.append(
                        swa_ref[(step - 1) * WINDOW : (step + 1) * WINDOW, start : start + SWA_HEAD]
                    )
            score = dot(query, both[0], NT) * SWA_HEAD ** (-0.5)
            score = jnp.where(inside_first if step == 0 else inside, score, -jnp.inf)
            expo = jnp.exp(score - jnp.max(score, axis=-1, keepdims=True))
            probs = (expo / jnp.sum(expo, axis=-1, keepdims=True)).astype(jnp.bfloat16)
            swa_out_ref[mine, at : at + SWA_HEAD] = dot(probs, both[1])


def readout_kernel(
    first_ref, second_ref, add_first_ref, add_second_ref,
    qk_ref, past_ref, numer_ref, denom_ref, swa_ref, out_ref,
):
    rows = qk_ref.shape[0]
    query = qk_ref[:, : HEADS * FEAT]
    lane_id = lax.broadcasted_iota(jnp.int32, (rows, LANES), 1)
    for pair in range(PAIRS):
        lanes = slice(pair * LANES, (pair + 1) * LANES)
        past = past_ref[pair * ROWS : (pair + 1) * ROWS, :]
        last = past[ROWS - 16 :].astype(jnp.float32)
        numers = []
        denoms = []
        for place, head in enumerate((2 * pair, 2 * pair + 1)):
            own = jnp.where(head_mask(head, query.shape), query, jnp.zeros_like(query))
            one = dot(own, first_ref[...]) + add_first_ref[0:1]
            two = dot(own, second_ref[...]) + add_second_ref[0:1]
            high, low = split_hi_lo(one * two)
            numers.append(dot(high, past) + dot(low, past))
            at = 16 - (ROWS - CONST) + 1 + 2 * place
            norm = jnp.concatenate([last[at : at + 1], last[at + 1 : at + 2, : ROWS - LANES]], axis=1)
            norm = jnp.broadcast_to(norm, (LANES, ROWS)).astype(jnp.bfloat16)
            denoms.append(dot(high, norm, NT) + dot(low, norm, NT))
        numer = jnp.where(lane_id < VHEAD, numers[0], numers[1]) + numer_ref[:, lanes]
        denom = jnp.where(lane_id < VHEAD, denoms[0], denoms[1]) + denom_ref[:, lanes]
        out_ref[:, lanes] = (numer / denom + swa_ref[:, lanes]).astype(out_ref.dtype)


def call(kernel, outs, args, specs=None):
    whole = pl.BlockSpec(memory_space=pltpu.VMEM)
    return pl.pallas_call(
        kernel,
        out_shape=outs,
        in_specs=specs or [whole] * len(args),
        out_specs=jax.tree.map(lambda _: whole, outs),
        compiler_params=pltpu.CompilerParams(vmem_limit_bytes=VMEM_LIMIT),
    )(*args)


def shards(lin_qk, lin_v, conv_w, swa_qkv):
    rows = lin_qk.shape[0]
    devices = lax.axis_size("ctxouter") * lax.axis_size("ctxinner")
    swa_width = swa_qkv.shape[1] // 3
    shift = [(i, i + 1) for i in range(devices - 1)]
    bf16 = jnp.bfloat16
    first, second, halved, add_first, add_second = selectors()
    stacked = lambda a: jnp.asarray(np.tile(a, (HEADS, 1)), bf16)
    stacked_t = lambda a: jnp.asarray(np.tile(a, (HEADS, 1)).T, bf16)

    tail_v = lax.ppermute(lin_v[rows - TAIL :], AXES, shift)
    conved, state = call(
        state_kernel,
        [
            jax.ShapeDtypeStruct(lin_v.shape, bf16),
            jax.ShapeDtypeStruct((PAIRS * ROWS, LANES), bf16),
        ],
        [stacked_t(first), stacked_t(second), lin_qk, lin_v, tail_v, conv_w],
    )
    tail_kv = lax.ppermute(swa_qkv[rows - WINDOW :, swa_width:], AXES, shift)
    parts = lax.all_to_all(state.reshape(devices, -1, LANES), AXES, 0, 0, tiled=True)
    before = jnp.asarray(np.tril(np.ones((devices, devices), np.float32), -1), bf16)
    past = jnp.einsum("ij,jrl->irl", before, parts, preferred_element_type=jnp.float32).astype(bf16)
    past = lax.all_to_all(past, AXES, 0, 0, tiled=True).reshape(PAIRS * ROWS, LANES)
    whole = pl.BlockSpec(memory_space=pltpu.VMEM)
    numer, denom, swa = call(
        local_kernel,
        [jax.ShapeDtypeStruct(lin_v.shape, jnp.float32)] * 3,
        [lax.axis_index(AXES).reshape(1), lin_qk, conved, swa_qkv, tail_kv],
        [pl.BlockSpec(memory_space=pltpu.SMEM)] + [whole] * 4,
    )
    return call(
        readout_kernel,
        jax.ShapeDtypeStruct(lin_v.shape, bf16),
        [
            stacked(halved),
            stacked(second),
            jnp.asarray(add_first),
            jnp.asarray(add_second),
            lin_qk,
            past,
            numer,
            denom,
            swa,
        ],
    )


def solution(mesh):
    return jax.shard_map(
        shards,
        mesh=mesh,
        in_specs=(P(AXES, None), P(AXES, None), P(), P(AXES, None)),
        out_specs=P(AXES, None),
        check_vma=False,
    )
```

time: 198 us -> 60.2 us (0.30)
  the two profiles are of different devices: /device:TPU:6 before, /device:TPU:4 now
where the time goes in v1:
time: 60.2 us; the launch traced here: 59.8 us
  waiting for transfers between devices  18.3 us (30%)
  Pallas kernels  14.1 us (23%)
  blocking collectives  13.2 us (22%)
  starting transfers between devices  7.81 us (13%)
  local copies, waits for them, and re-layouts  6.05 us (10%)
    pallas_call x3, Pallas kernels, call(): pl.pallas_call(kernel, out_shape=outs, in_specs=specs or [whole] * len(ar...  14.1 us
    all_to_all x1, blocking collectives, shards(): lax.all_to_all(state.reshape(devices, -1, LANES), AXES, 0, 0, tiled=True)  13.2 us
    ppermute x1, waiting for transfers between devices, shards(): tail_kv = lax.ppermute(swa_qkv[rows - WINDOW:, swa_width:], AXES, shift)  11.4 us
    ppermute x1, waiting for transfers between devices, shards(): tail_v = lax.ppermute(lin_v[rows - TAIL:], AXES, shift)  6.9 us
    unnamed x24, local copies, waits for them, and re-layouts  4.39 us
    all_to_all x1, starting transfers between devices, shards(): lax.all_to_all(past, AXES, 0, 0, tiled=True).reshape(PAIRS * ROWS, LANES)  3.71 us
    ppermute x1, starting transfers between devices, shards(): tail_kv = lax.ppermute(swa_qkv[rows - WINDOW:, swa_width:], AXES, shift)  2.19 us
    ppermute x1, starting transfers between devices, shards(): tail_v = lax.ppermute(lin_v[rows - TAIL:], AXES, shift)  1.91 us
  transfers between devices with their start and end apart: 3, of which 2 were waited for; matrix products, arithmetic and copies ran while one was open for 0% of the time, Pallas kernels for 10%

profile of v1, /device:TPU:4, one launch (start us, length us, event | category | flops | bytes accessed | tf_op | source)
XLA Modules:
  0.0 59.8 jit_solution(15969928728397023151)
XLA Ops:
  0.0 0.0 copy-start.6
  0.0 0.8 %slice.6 = bf16[16,1024]{1,0:T(8,128)(2,1)S(1)} slice(bf16[128,1024]{1,0:T(8,128)(2,1)} %v_ref.1), slice={[112:128], [0:1024]} | slice | bytes 65536 | tf_op jit(solution)/shard_map/slice | solution.py:214
  0.8 1.9 %collective-permute-start = (bf16[16,1024]{1,0:T(8,128)(2,1)S(1)}, bf16[16,1024]{1,0:T(8,128)(2,1)S(1)}, u32[]{:S(2)}, u32[]{:S(2)}) collective-permute-start(bf16[16,1024]{1,0:T(8,128)(2,1)S(1)} %slice.6), channel_id=1, source_target_pairs={{0,1},{1,2},{2,3},{3,4},{4,5},{5,6},{6,7},{7,8},{8,9},{9,10},{10,1... | collective-permute-start | bytes 98312 | tf_op jit(solution)/shard_map/ppermute | solution.py:214
  2.7 6.9 %collective-permute-done.tail_ref = bf16[16,1024]{1,0:T(8,128)(2,1)S(1)} collective-permute-done((bf16[16,1024]{1,0:T(8,128)(2,1)S(1)}, bf16[16,1024]{1,0:T(8,128)(2,1)S(1)}, u32[]{:S(2)}, u32[]{:S(2)}) %collective-permute-start) | collective-permute-done | bytes 32800 | tf_op jit(solution)/shard_map/ppermute | solution.py:214
  9.6 0.0 copy-done.6
  9.6 0.0 copy-start.1
  9.6 0.9 %copy-done.1 = bf16[128,512]{1,0:T(8,128)(2,1)S(1)} copy-done((bf16[128,512]{1,0:T(8,128)(2,1)S(1)}, bf16[128,512]{1,0:T(8,128)(2,1)}, u32[]{:S(2)}) %copy-start.1) | copy-done | bytes 131096
  10.5 0.0 copy-start.3
  10.5 0.9 %copy-done.3 = bf16[128,1024]{1,0:T(8,128)(2,1)S(1)} copy-done((bf16[128,1024]{1,0:T(8,128)(2,1)S(1)}, bf16[128,1024]{1,0:T(8,128)(2,1)}, u32[]{:S(2)}) %copy-start.3) | copy-done | bytes 262168
  11.5 0.0 copy-start.7
  11.5 0.9 %copy-done.7 = bf16[160,256]{1,0:T(8,128)(2,1)S(1)} copy-done((bf16[160,256]{1,0:T(8,128)(2,1)S(1)}, bf16[160,256]{1,0:T(8,128)(2,1)}, u32[]{:S(2)}) %copy-start.7) | copy-done | bytes 81944
  12.4 0.0 copy-start.8
  12.4 0.7 %copy-done.8 = f32[3,1024]{1,0:T(4,128)S(1)} copy-done((f32[3,1024]{1,0:T(4,128)S(1)}, f32[3,1024]{1,0:T(4,128)}, u32[]{:S(2)}) %copy-start.8) | copy-done | bytes 12312
  13.1 4.0 %shard_map.109 = (bf16[128,1024]{1,0:T(8,128)(2,1)S(1)}, bf16[1280,128]{1,0:T(8,128)(2,1)S(1)}) custom-call(bf16[160,256]{1,0:T(8,128)(2,1)S(1)} %copy-done.7, bf16[160,256]{1,0:T(8,128)(2,1)S(1)} %copy-done.6, bf16[128,512]{1,0:T(8,128)(2,1)S(1)} %copy-done.1, bf16[128,1024]{1,0:T(8,128)(2,1)S(1)} %copy-done.3, ...), custom_call_target="tpu_custom_call" | custom-call | tf_op jit(solution)/shard_map/pallas_call | solution.py:195
  17.1 0.0 copy-start.11
  17.1 13.2 %all_to_all.10 = bf16[32,40,128]{2,1,0:T(8,128)(2,1)S(1)} all-to-all(bf16[32,40,128]{2,1,0:T(8,128)(2,1)S(1)} %bitcast.8), channel_id=1, replica_groups=mesh['ctxouter'=4,'ctxinner'=8] {'ctxouter','ctxinner'}, dimensions={0} | all-to-all | bytes 655360 | tf_op jit(solution)/shard_map/all_to_all | solution.py:224
  30.3 0.0 copy-done.11
  30.3 0.2 fusion
  30.5 0.0 copy-start
  30.5 0.8 %copy.15 = bf16[32,40,128]{2,1,0:T(8,128)(2,1)} copy(bf16[32,40,128]{2,0,1:T(8,128)(2,1)S(1)} %fusion) | data formatting | bytes 655360 | tf_op jit(solution)/shard_map/convert_element_type | solution.py:226
  31.4 3.7 %all-to-all-start.1 = ((bf16[32,40,128]{2,1,0:T(8,128)(2,1)}), bf16[32,40,128]{2,1,0:T(8,128)(2,1)S(1)}, u32[]{:S(2)}, u32[]{:S(2)}) async-start(bf16[32,40,128]{2,1,0:T(8,128)(2,1)} %copy.15), calls=%async_computation.1 | async-start | bytes 655360 | tf_op jit(solution)/shard_map/all_to_all | solution.py:227
  35.1 0.0 copy-done
  35.1 0.0 copy-start.2
  35.1 2.2 %collective-permute-start.1 = (bf16[64,2048]{1,0:T(8,128)(2,1)S(1)}, bf16[64,2048]{1,0:T(8,128)(2,1)S(1)}, u32[]{:S(2)}, u32[]{:S(2)}) collective-permute-start(bf16[64,2048]{1,0:T(8,128)(2,1)S(1)} %slice.7), channel_id=1, source_target_pairs={{0,1},{1,2},{2,3},{3,4},{4,5},{5,6},{6,7},{7,8},{8,9},{9,10},{10,1... | collective-permute-start | bytes 786440 | tf_op jit(solution)/shard_map/ppermute | solution.py:223
  37.3 11.4 %collective-permute-done.1.kv_ref = bf16[64,2048]{1,0:T(8,128)(2,1)S(1)} collective-permute-done((bf16[64,2048]{1,0:T(8,128)(2,1)S(1)}, bf16[64,2048]{1,0:T(8,128)(2,1)S(1)}, u32[]{:S(2)}, u32[]{:S(2)}) %collective-permute-start.1) | collective-permute-done | bytes 262176 | tf_op jit(solution)/shard_map/ppermute | solution.py:223
  48.7 0.0 copy-done.2
  48.7 0.0 copy-start.4
  48.7 0.0 copy-start.9
  48.7 0.0 copy-start.10
  48.7 5.8 %shard_map.110 = (f32[128,1024]{1,0:T(8,128)S(1)}, f32[128,1024]{1,0:T(8,128)S(1)}, f32[128,1024]{1,0:T(8,128)S(1)}) custom-call(s32[1]{0:T(128)} %bitcast.4.first_ref, bf16[128,512]{1,0:T(8,128)(2,1)S(1)} %copy-done.2, bf16[128,1024]{1,0:T(8,128)(2,1)S(1)} %get-tuple-element.11.cv_ref, bf16[128,3072]{1,0:T(8,128)(2,1)S(1)} %copy-done, ...), custom_call_target="tpu_custom_call" | custom-call | tf_op jit(solution)/shard_map/pallas_call | solution.py:195
  54.5 0.0 all-to-all-done.1
  54.5 0.0 copy-done.4
  54.5 0.0 copy-done.9
  54.5 0.0 copy-done.10
  54.5 0.0 copy-start.5
  54.5 0.9 %copy-done.5 = bf16[256,160]{1,0:T(8,128)(2,1)S(1)} copy-done((bf16[256,160]{1,0:T(8,128)(2,1)S(1)}, bf16[256,160]{1,0:T(8,128)(2,1)}, u32[]{:S(2)}) %copy-start.5) | copy-done | bytes 81944
  55.4 4.4 %shard_map.111 = bf16[128,1024]{1,0:T(8,128)(2,1)} custom-call(bf16[256,160]{1,0:T(8,128)(2,1)S(1)} %copy-done.5, bf16[256,160]{1,0:T(8,128)(2,1)S(1)} %copy-done.4, f32[8,160]{1,0:T(8,128)S(1)} %copy-done.10, f32[8,160]{1,0:T(8,128)S(1)} %copy-done.9, bf16[128,512]{1,0:T(8,128)(2,1)S(1)} %copy-done.2, bf16[1280,128]{1,0:T(8,128)(2,1)S(1)} %bitcast.7, ...), custom_call_target="tpu_custom_call" | custom-call | tf_op jit(solution)/shard_map/pallas_call | solution.py:195
  (1 shorter events, 0.0 us)
Async XLA Ops:
  0.0 9.6 %copy-start.6 = (bf16[160,256]{1,0:T(8,128)(2,1)S(1)}, bf16[160,256]{1,0:T(8,128)(2,1)}, u32[]{:S(2)}) copy-start(bf16[160,256]{1,0:T(8,128)(2,1)} %constant.25.clone.second_ref) | copy-start | bytes 245764
  0.8 8.8 %collective-permute-start = (bf16[16,1024]{1,0:T(8,128)(2,1)S(1)}, bf16[16,1024]{1,0:T(8,128)(2,1)S(1)}, u32[]{:S(2)}, u32[]{:S(2)}) collective-permute-start(bf16[16,1024]{1,0:T(8,128)(2,1)S(1)} %slice.6), channel_id=1, source_target_pairs={{0,1},{1,2},{2,3},{3,4},{4,5},{5,6},{6,7},{7,8},{8,9},{9,10},{10,1... | collective-permute-start | bytes 98312 | tf_op jit(solution)/shard_map/ppermute | solution.py:214
  9.6 0.9 %copy-start.1 = (bf16[128,512]{1,0:T(8,128)(2,1)S(1)}, bf16[128,512]{1,0:T(8,128)(2,1)}, u32[]{:S(2)}) copy-start(bf16[128,512]{1,0:T(8,128)(2,1)} %qk_ref.5) | copy-start | bytes 393220
  10.5 0.9 %copy-start.3 = (bf16[128,1024]{1,0:T(8,128)(2,1)S(1)}, bf16[128,1024]{1,0:T(8,128)(2,1)}, u32[]{:S(2)}) copy-start(bf16[128,1024]{1,0:T(8,128)(2,1)} %v_ref.1) | copy-start | bytes 786436
  11.5 0.9 %copy-start.7 = (bf16[160,256]{1,0:T(8,128)(2,1)S(1)}, bf16[160,256]{1,0:T(8,128)(2,1)}, u32[]{:S(2)}) copy-start(bf16[160,256]{1,0:T(8,128)(2,1)} %constant.24.clone.first_ref) | copy-start | bytes 245764
  12.4 0.7 %copy-start.8 = (f32[3,1024]{1,0:T(4,128)S(1)}, f32[3,1024]{1,0:T(4,128)}, u32[]{:S(2)}) copy-start(f32[3,1024]{1,0:T(4,128)} %conv_ref.1) | copy-start | bytes 36868
  17.1 13.2 %copy-start.11 = (bf16[32,32,1]{1,0,2:T(8,128)(2,1)S(1)}, bf16[32,32,1]{1,0,2:T(8,128)(2,1)}, u32[]{:S(2)}) copy-start(bf16[32,32,1]{1,0,2:T(8,128)(2,1)} %constant.31) | copy-start | bytes 6148
  30.5 4.6 %copy-start = (bf16[128,3072]{1,0:T(8,128)(2,1)S(1)}, bf16[128,3072]{1,0:T(8,128)(2,1)}, u32[]{:S(2)}) copy-start(bf16[128,3072]{1,0:T(8,128)(2,1)} %swa_ref.1) | copy-start | bytes 2359300
  31.4 23.1 %all-to-all-start.1 = ((bf16[32,40,128]{2,1,0:T(8,128)(2,1)}), bf16[32,40,128]{2,1,0:T(8,128)(2,1)S(1)}, u32[]{:S(2)}, u32[]{:S(2)}) async-start(bf16[32,40,128]{2,1,0:T(8,128)(2,1)} %copy.15), calls=%async_computation.1 | async-start | bytes 655360 | tf_op jit(solution)/shard_map/all_to_all | solution.py:227
  35.1 13.6 %copy-start.2 = (bf16[128,512]{1,0:T(8,128)(2,1)S(1)}, bf16[128,512]{1,0:T(8,128)(2,1)}, u32[]{:S(2)}) copy-start(bf16[128,512]{1,0:T(8,128)(2,1)} %qk_ref.5) | copy-start | bytes 393220
  35.1 13.6 %collective-permute-start.1 = (bf16[64,2048]{1,0:T(8,128)(2,1)S(1)}, bf16[64,2048]{1,0:T(8,128)(2,1)S(1)}, u32[]{:S(2)}, u32[]{:S(2)}) collective-permute-start(bf16[64,2048]{1,0:T(8,128)(2,1)S(1)} %slice.7), channel_id=1, source_target_pairs={{0,1},{1,2},{2,3},{3,4},{4,5},{5,6},{6,7},{7,8},{8,9},{9,10},{10,1... | collective-permute-start | bytes 786440 | tf_op jit(solution)/shard_map/ppermute | solution.py:223
  48.7 5.8 %copy-start.4 = (bf16[256,160]{1,0:T(8,128)(2,1)S(1)}, bf16[256,160]{1,0:T(8,128)(2,1)}, u32[]{:S(2)}) copy-start(bf16[256,160]{1,0:T(8,128)(2,1)} %constant.28.clone.second_ref) | copy-start | bytes 245764
  48.7 5.8 %copy-start.9 = (f32[8,160]{1,0:T(8,128)S(1)}, f32[8,160]{1,0:T(8,128)}, u32[]{:S(2)}) copy-start(f32[8,160]{1,0:T(8,128)} %constant.30.clone.add_second_ref) | copy-start | bytes 15364
  48.7 5.8 %copy-start.10 = (f32[8,160]{1,0:T(8,128)S(1)}, f32[8,160]{1,0:T(8,128)}, u32[]{:S(2)}) copy-start(f32[8,160]{1,0:T(8,128)} %constant.29.clone.add_first_ref) | copy-start | bytes 15364
  54.5 0.9 %copy-start.5 = (bf16[256,160]{1,0:T(8,128)(2,1)S(1)}, bf16[256,160]{1,0:T(8,128)(2,1)}, u32[]{:S(2)}) copy-start(bf16[256,160]{1,0:T(8,128)(2,1)} %constant.27.clone.first_ref) | copy-start | bytes 245764

commit v2 on v1

v2 whole, which is shorter than its diff:
```python
import functools

import jax
import jax.numpy as jnp
import numpy as np
from jax import lax
from jax.experimental import pallas as pl
from jax.experimental.pallas import tpu as pltpu
from jax.sharding import PartitionSpec as P

HEADS = 16
FEAT = 16
VHEAD = 64
SWA_HEADS = 8
SWA_HEAD = 128
WINDOW = 64

AXES = ("ctxouter", "ctxinner")
LANES = 128
PAIRS = HEADS // 2
QUADS = FEAT * (FEAT + 1) // 2
CONST = QUADS + FEAT
ROWS = 160
TAIL = 16
EXTRA = 8
VMEM_LIMIT = 48 * 1024 * 1024


NT = (((1,), (1,)), ((), ()))
NN = (((1,), (0,)), ((), ()))
BF16 = jnp.bfloat16


def dot(a, b, dims=NN):
    return lax.dot_general(a, b, dims, preferred_element_type=jnp.float32)


def iota(shape, dim):
    return lax.broadcasted_iota(jnp.int32, shape, dim)


def selector(feature, lane, second, halved=False):
    scale = FEAT ** (-0.25)
    quad = feature < QUADS
    entry = feature % FEAT
    if second:
        wanted = (feature + feature // FEAT) % FEAT
        return jnp.where((lane % FEAT == wanted) & quad, scale, 0.0)
    linear = (feature >= QUADS) & (feature < CONST)
    wanted = jnp.where(quad, entry, (feature - QUADS) % FEAT)
    weight = jnp.where((feature < FEAT) & halved, 0.5 * scale, scale)
    return jnp.where((lane % FEAT == wanted) & (quad | linear), weight, 0.0)


def adders(feature):
    first = jnp.where(feature == CONST, 1.0, 0.0)
    second = jnp.where((feature >= QUADS) & (feature <= CONST), 1.0, 0.0)
    return first, second


def head_mask(head, shape):
    place = iota(shape, 1)
    return (place >= head * FEAT) & (place < (head + 1) * FEAT)


def hi_lo(values):
    high = values.astype(BF16)
    return high, (values - high.astype(jnp.float32)).astype(BF16)


def convolved(value, tail, conv_ref, lanes):
    row_id = iota(value.shape, 0)
    result = conv_ref[0:1, lanes] * value
    for lag in range(1, conv_ref.shape[0]):
        shifted = pltpu.roll(value, lag, 0)
        for row in range(lag):
            source = TAIL - lag + row
            before = 0.0 if tail is None else tail[source : source + 1]
            shifted = jnp.where(row_id == row, before, shifted)
        result = result + conv_ref[lag : lag + 1, lanes] * shifted
    return result.astype(BF16)


def state_kernel(part, qk_hbm, v_hbm, conv_hbm, out_ref, key_ref, v_ref, conv_ref, sems):
    rows = v_ref.shape[0]
    taps = conv_ref.shape[0]
    width = HEADS * FEAT
    copies = [
        pltpu.make_async_copy(qk_hbm.at[:, width : 2 * width], key_ref, sems.at[0]),
        pltpu.make_async_copy(conv_hbm, conv_ref, sems.at[1]),
        pltpu.make_async_copy(v_hbm, v_ref, sems.at[2]),
    ]
    for copy in copies:
        copy.start()
    for copy in copies:
        copy.wait()
    key_t = (key_ref[...].astype(jnp.float32) * FEAT ** (-0.25)).T
    const_rows = jnp.where(iota((EXTRA, rows), 0) == 0, 1.0, 0.0)
    lane_id = iota((ROWS, LANES), 1)
    low_row = iota((EXTRA, LANES), 0)
    ones = jnp.ones((rows, LANES), BF16)
    half = FEAT // 2
    padded = (part + 7) // 8 * 8
    states = []
    norms = jnp.zeros((ROWS, LANES), jnp.float32)
    extras = []
    for pair in range(PAIRS):
        lanes = slice(pair * LANES, (pair + 1) * LANES)
        value = v_ref[:, lanes].astype(jnp.float32)
        conved = convolved(value, None, conv_ref, lanes)
        right = jnp.concatenate([conved, ones], axis=1)
        right = jnp.concatenate([right, right], axis=0)
        both = []
        for head in (2 * pair, 2 * pair + 1):
            x = key_t[head * FEAT : (head + 1) * FEAT]
            blocks = [x * x]
            for by in range(1, half):
                blocks.append(x * jnp.concatenate([x[by:], x[:by]], axis=0))
            blocks += [x[:half] * x[half:], x, const_rows]
            left = jnp.concatenate(hi_lo(jnp.concatenate(blocks, axis=0)), axis=1)
            result = dot(left, right)
            both.append(result[:, :LANES])
            norms = jnp.where(lane_id // 8 == head, result[:, LANES:], norms)
        states.append(jnp.where(lane_id < VHEAD, both[0], both[1]))
        group = pair * 2 * FEAT // LANES * LANES
        extra = jnp.zeros((EXTRA, LANES), jnp.float32)
        for row in range(taps - 1):
            share = jnp.zeros((1, LANES), jnp.float32)
            for lag in range(row + 1, taps):
                share = share + conv_ref[lag : lag + 1, lanes] * value[rows + row - lag : rows + row - lag + 1]
            extra = jnp.where(low_row == row, share, extra)
            first = key_ref[0:16, group : group + LANES].astype(jnp.float32)[row : row + 1]
            extra = jnp.where(low_row == taps - 1 + row, first, extra)
        extras.append(extra)
    norms_t = norms.T
    for pair in range(PAIRS):
        last = states[pair][CONST:]
        for place in range(2):
            at = 8 * (2 * pair + place)
            norm = norms_t[at : at + 8]
            rest = jnp.concatenate(
                [norm[:, LANES:], jnp.zeros((8, 2 * LANES - ROWS), jnp.float32)], axis=1
            )
            last = jnp.where(low_row == 1 + 2 * place, norm[:, :LANES], last)
            last = jnp.where(low_row == 2 + 2 * place, rest, last)
        state = jnp.concatenate([states[pair][:CONST], last], axis=0)
        for piece in range(ROWS // part):
            rows_of = [state[piece * part : (piece + 1) * part]]
            if padded != part:
                rows_of.append(jnp.zeros((padded - part, LANES), jnp.float32))
            message = jnp.concatenate(rows_of + [extras[pair]], axis=0)
            out_ref[pair * (ROWS // part) + piece] = message.astype(BF16)


def prefix_kernel(taps, place_ref, parts_ref, out_ref):
    blocks, held, _ = parts_ref.shape
    part = out_ref.shape[1]
    padded = held - EXTRA
    start = place_ref[0] * part
    head = start // ROWS * 2 % (LANES // FEAT)
    feature = start % ROWS + iota((padded, LANES), 0)
    lane = iota((padded, LANES), 1)
    one = selector(feature, lane, False)
    two = selector(feature, lane, True)
    add_one, add_two = adders(feature[:, 0:1])
    extras = parts_ref[:, padded:, :].astype(jnp.float32).reshape(blocks * EXTRA, LANES)
    extras_low = extras.astype(BF16)
    lefts = []
    rights = []
    for place in range(2):
        mine = lane // FEAT == head + place
        first = dot(jnp.where(mine, one, 0.0).astype(BF16), extras_low, NT) + add_one
        second = dot(jnp.where(mine, two, 0.0).astype(BF16), extras_low, NT) + add_two
        width = blocks * EXTRA
        shift = width - EXTRA - (taps - 1)
        lefts.append(pltpu.roll(first * second, shift, 1))
        upper = iota((width, LANES), 1) >= VHEAD
        rights.append(jnp.where(upper == (place == 1), extras, 0.0).astype(BF16))
    left = jnp.concatenate(lefts, axis=1)
    right = jnp.concatenate(rights, axis=0)
    column = iota(left.shape, 1) % (blocks * EXTRA)
    from_block = jnp.where(column % EXTRA < taps - 1, column // EXTRA + 1, blocks)

    def one_block(block, total):
        seen = jnp.where(from_block < block, left, 0.0).astype(BF16)
        result = total + dot(seen, right)
        out_ref[block] = result[:part].astype(BF16)
        return total + parts_ref[block].astype(jnp.float32)[:padded]

    total = jnp.zeros((padded, LANES), jnp.float32)
    if blocks <= 32:
        for block in range(blocks):
            total = one_block(block, total)
    else:
        lax.fori_loop(0, blocks, one_block, total)


def local_kernel(
    place_ref, qk_ref, v_ref, conv_ref, swa_ref, kv_ref, tail_ref, numer_ref, denom_ref, swa_out_ref, phi_ref
):
    rows = v_ref.shape[0]
    width = HEADS * FEAT
    query = qk_ref[:, :width]
    key = qk_ref[:, width : 2 * width]
    lane_id = iota((rows, LANES), 1)
    causal = iota((rows, rows), 1) <= iota((rows, rows), 0)
    ones = jnp.ones((rows, LANES), BF16)
    feature = iota((width, ROWS), 1)
    lane = iota((width, ROWS), 0)
    one = selector(feature, lane, False, halved=True).astype(BF16)
    two = selector(feature, lane, True).astype(BF16)
    add_one, add_two = adders(iota((8, ROWS), 1)[0:1])
    for pair in range(PAIRS):
        lanes = slice(pair * LANES, (pair + 1) * LANES)
        tail = tail_ref[:, lanes].astype(jnp.float32)
        tail = jnp.where(place_ref[0] == 0, 0.0, tail)
        conved = convolved(v_ref[:, lanes].astype(jnp.float32), tail, conv_ref, lanes)
        right = jnp.concatenate([conved, ones], axis=1)
        results = []
        for head in (2 * pair, 2 * pair + 1):
            own = jnp.where(head_mask(head, query.shape), query, jnp.zeros_like(query))
            score = dot(own, key, NT) * FEAT ** (-0.5)
            weight = 1.0 + score + 0.5 * score * score
            weight = jnp.where(causal, weight, 0.0).astype(BF16)
            results.append(dot(weight, right))
            high, low = hi_lo((dot(own, one) + add_one) * (dot(own, two) + add_two))
            phi_ref[head, :rows, :] = high
            phi_ref[head, rows:, :] = low
        lower = lane_id < VHEAD
        numer_ref[:, lanes] = jnp.where(lower, results[0][:, :LANES], results[1][:, :LANES])
        denom_ref[:, lanes] = jnp.where(lower, results[0][:, LANES:], results[1][:, LANES:])
    swa_width = SWA_HEADS * SWA_HEAD
    not_before = jnp.where(place_ref[0] == 0, WINDOW, 0)
    span = 2 * WINDOW
    place = iota((WINDOW, span), 1)
    row = iota((WINDOW, span), 0)
    inside = (place > row) & (place <= row + WINDOW)
    inside_first = inside & (place >= not_before)
    for head in range(SWA_HEADS):
        at = head * SWA_HEAD
        for step in range(rows // WINDOW):
            mine = slice(step * WINDOW, (step + 1) * WINDOW)
            window = slice((step - 1) * WINDOW, (step + 1) * WINDOW)
            both = []
            for start in (swa_width + at, 2 * swa_width + at):
                here = slice(start, start + SWA_HEAD)
                there = slice(start - swa_width, start - swa_width + SWA_HEAD)
                if step == 0:
                    both.append(jnp.concatenate([kv_ref[:, there], swa_ref[mine, here]], axis=0))
                else:
                    both.append(swa_ref[window, here])
            score = dot(swa_ref[mine, at : at + SWA_HEAD], both[0], NT) * SWA_HEAD ** (-0.5)
            score = jnp.where(inside_first if step == 0 else inside, score, -jnp.inf)
            expo = jnp.exp(score - jnp.max(score, axis=-1, keepdims=True))
            probs = (expo / jnp.sum(expo, axis=-1, keepdims=True)).astype(BF16)
            swa_out_ref[mine, at : at + SWA_HEAD] = dot(probs, both[1])


def readout_kernel(phi_ref, past_ref, numer_ref, denom_ref, swa_ref, out_ref):
    rows = out_ref.shape[0]
    lower = iota((rows, LANES), 1) < VHEAD
    norms = []
    for pair in range(PAIRS):
        last = past_ref[(pair + 1) * ROWS - 16 : (pair + 1) * ROWS, :].astype(jnp.float32)
        for place in range(2):
            at = 16 - (ROWS - CONST) + 1 + 2 * place
            norm = jnp.concatenate([last[at : at + 1], last[at + 1 : at + 2, : ROWS - LANES]], axis=1)
            norms.append(jnp.broadcast_to(norm, (8, ROWS)))
    norms = jnp.concatenate(norms, axis=0).T.astype(BF16)
    source = iota((LANES, LANES), 0)
    target = iota((LANES, LANES), 1)
    for pair in range(PAIRS):
        lanes = slice(pair * LANES, (pair + 1) * LANES)
        wanted = jnp.where(target < VHEAD, 16 * pair, 16 * pair + 8)
        spread = dot(norms, jnp.where(source == wanted, 1.0, 0.0).astype(BF16)).astype(BF16)
        right = jnp.concatenate([past_ref[pair * ROWS : (pair + 1) * ROWS, :], spread], axis=1)
        results = []
        for head in (2 * pair, 2 * pair + 1):
            result = dot(phi_ref[head], right)
            results.append(result[:rows] + result[rows:])
        numer = jnp.where(lower, results[0][:, :LANES], results[1][:, :LANES]) + numer_ref[:, lanes]
        denom = jnp.where(lower, results[0][:, LANES:], results[1][:, LANES:]) + denom_ref[:, lanes]
        out_ref[:, lanes] = (numer / denom + swa_ref[:, lanes]).astype(out_ref.dtype)


IN_VMEM = pl.BlockSpec(memory_space=pltpu.VMEM)
IN_SMEM = pl.BlockSpec(memory_space=pltpu.SMEM)
IN_PLACE = pl.BlockSpec(memory_space=pl.ANY)


def call(kernel, outs, args, specs, scratch=()):
    return pl.pallas_call(
        kernel,
        out_shape=outs,
        in_specs=specs,
        out_specs=jax.tree.map(lambda _: IN_VMEM, outs),
        scratch_shapes=scratch,
        compiler_params=pltpu.CompilerParams(vmem_limit_bytes=VMEM_LIMIT),
    )(*args)


def shards(lin_qk, lin_v, conv_w, swa_qkv):
    rows = lin_qk.shape[0]
    devices = lax.axis_size("ctxouter") * lax.axis_size("ctxinner")
    place = lax.axis_index(AXES).reshape(1)
    swa_width = swa_qkv.shape[1] // 3
    shift = [(i, i + 1) for i in range(devices - 1)]
    part = PAIRS * ROWS // devices
    held = (part + 7) // 8 * 8 + EXTRA
    shape = jax.ShapeDtypeStruct

    messages = call(
        functools.partial(state_kernel, part),
        shape((devices, held, LANES), BF16),
        [lin_qk, lin_v, conv_w],
        [IN_PLACE] * 3,
        [
            pltpu.VMEM((rows, HEADS * FEAT), BF16),
            pltpu.VMEM(lin_v.shape, BF16),
            pltpu.VMEM(conv_w.shape, jnp.float32),
            pltpu.SemaphoreType.DMA((3,)),
        ],
    )
    messages, lin_v, swa_qkv = lax.optimization_barrier((messages, lin_v, swa_qkv))
    parts = lax.all_to_all(messages, AXES, 0, 0, tiled=True)
    tail_kv = lax.ppermute(swa_qkv[rows - WINDOW :, swa_width:], AXES, shift)
    tail_v = lax.ppermute(lin_v[rows - TAIL :], AXES, shift)
    parts, tail_kv, tail_v = lax.optimization_barrier((parts, tail_kv, tail_v))
    past = call(
        functools.partial(prefix_kernel, conv_w.shape[0]),
        shape((devices, part, LANES), BF16),
        [place, parts],
        [IN_SMEM, IN_VMEM],
    )
    past, tail_kv, tail_v = lax.optimization_barrier((past, tail_kv, tail_v))
    past = lax.all_to_all(past, AXES, 0, 0, tiled=True).reshape(PAIRS * ROWS, LANES)
    numer, denom, swa, phi = call(
        local_kernel,
        [shape(lin_v.shape, jnp.float32)] * 3 + [shape((HEADS, 2 * rows, ROWS), BF16)],
        [place, lin_qk, lin_v, conv_w, swa_qkv, tail_kv, tail_v],
        [IN_SMEM] + [IN_VMEM] * 6,
    )
    return call(
        readout_kernel,
        shape(lin_v.shape, BF16),
        [phi, past, numer, denom, swa],
        [IN_VMEM] * 5,
    )


def solution(mesh):
    return jax.shard_map(
        shards,
        mesh=mesh,
        in_specs=(P(AXES, None), P(AXES, None), P(), P(AXES, None)),
        out_specs=P(AXES, None),
        check_vma=False,
    )
```

time: 60.2 us -> 49.8 us (0.83)
  the two profiles are of different devices: /device:TPU:4 before, /device:TPU:0 now
where the time goes in v2:
time: 49.8 us; the launch traced here: 49.2 us
  starting transfers between devices  16.6 us (33%)
  Pallas kernels  12.3 us (25%)
  local copies, waits for them, and re-layouts  10.9 us (22%)
  waiting for transfers between devices  9.3 us (19%)
    pallas_call x4, Pallas kernels, call(): pl.pallas_call(kernel, out_shape=outs, in_specs=specs, out_specs=jax.tree...  12.3 us
    unnamed x30, local copies, waits for them, and re-layouts  9.95 us
    all_to_all x1, starting transfers between devices, shards(): parts = lax.all_to_all(messages, AXES, 0, 0, tiled=True)  7.3 us
    all_to_all x1, waiting for transfers between devices, shards(): parts = lax.all_to_all(messages, AXES, 0, 0, tiled=True)  6.95 us
    all_to_all x1, starting transfers between devices, shards(): lax.all_to_all(past, AXES, 0, 0, tiled=True).reshape(PAIRS * ROWS, LANES)  3.58 us
    ppermute x1, starting transfers between devices, shards(): tail_v = lax.ppermute(lin_v[rows - TAIL:], AXES, shift)  3.53 us
    ppermute x1, starting transfers between devices, shards(): tail_kv = lax.ppermute(swa_qkv[rows - WINDOW:, swa_width:], AXES, shift)  2.17 us
    all_to_all x1, waiting for transfers between devices, shards(): lax.all_to_all(past, AXES, 0, 0, tiled=True).reshape(PAIRS * ROWS, LANES)  1.51 us
  transfers between devices with their start and end apart: 4, of which 3 were waited for; matrix products, arithmetic and copies ran while one was open for 2% of the time, Pallas kernels for 13%

profile of v2, /device:TPU:0, one launch (start us, length us, event | category | flops | bytes accessed | tf_op | source)
XLA Modules:
  0.0 49.2 jit_solution(16206024244916723751)
XLA Ops:
  0.0 0.0 copy-start.1
  0.0 0.9 %copy-done.1 = bf16[128,1024]{1,0:T(8,128)(2,1)S(1)} copy-done((bf16[128,1024]{1,0:T(8,128)(2,1)S(1)}, bf16[128,1024]{1,0:T(8,128)(2,1)}, u32[]{:S(2)}) %copy-start.1) | copy-done | bytes 262168
  1.0 0.0 copy-start.3
  1.0 0.9 %copy-done.3 = bf16[128,512]{1,0:T(8,128)(2,1)S(1)} copy-done((bf16[128,512]{1,0:T(8,128)(2,1)S(1)}, bf16[128,512]{1,0:T(8,128)(2,1)}, u32[]{:S(2)}) %copy-start.3) | copy-done | bytes 131096
  1.9 0.0 copy-start.13
  1.9 0.7 %copy-done.13 = f32[3,1024]{1,0:T(4,128)S(1)} copy-done((f32[3,1024]{1,0:T(4,128)S(1)}, f32[3,1024]{1,0:T(4,128)}, u32[]{:S(2)}) %copy-start.13) | copy-done | bytes 12312
  2.6 0.0 copy-start.2
  2.6 0.0 copy-start
  2.6 0.0 copy-start.14
  2.6 1.6 %shard_map.46 = bf16[32,48,128]{2,1,0:T(8,128)(2,1)} custom-call(bf16[128,512]{1,0:T(8,128)(2,1)S(1)} %copy-done.3, bf16[128,1024]{1,0:T(8,128)(2,1)S(1)} %copy-done.1, f32[3,1024]{1,0:T(4,128)S(1)} %copy-done.13), custom_call_target="tpu_custom_call" | custom-call | tf_op jit(solution)/shard_map/pallas_call | solution.py:292
  4.2 7.3 %all-to-all-start = ((bf16[32,48,128]{2,1,0:T(8,128)(2,1)}), bf16[32,48,128]{2,1,0:T(8,128)(2,1)S(1)}, u32[]{:S(2)}, u32[]{:S(2)}) async-start(bf16[32,48,128]{2,1,0:T(8,128)(2,1)} %shard_map.46), calls=%async_computation | async-start | bytes 786432 | tf_op jit(solution)/shard_map/all_to_all | solution.py:325
  11.5 1.0 %slice.6 = bf16[64,2048]{1,0:T(8,128)(2,1)S(1)} slice(bf16[128,3072]{1,0:T(8,128)(2,1)} %swa_ref), slice={[64:128], [1024:3072]} | slice | bytes 524288 | tf_op jit(solution)/shard_map/slice | solution.py:326
  12.5 2.2 %collective-permute-start = (bf16[64,2048]{1,0:T(8,128)(2,1)S(1)}, bf16[64,2048]{1,0:T(8,128)(2,1)S(1)}, u32[]{:S(2)}, u32[]{:S(2)}) collective-permute-start(bf16[64,2048]{1,0:T(8,128)(2,1)S(1)} %slice.6), channel_id=1, source_target_pairs={{0,1},{1,2},{2,3},{3,4},{4,5},{5,6},{6,7},{7,8},{8,9},{9,10},{10,1... | collective-permute-start | bytes 786440 | tf_op jit(solution)/shard_map/ppermute | solution.py:326
  14.7 0.0 copy-done.2
  14.7 3.5 %collective-permute-start.1 = (bf16[16,1024]{1,0:T(8,128)(2,1)S(1)}, bf16[16,1024]{1,0:T(8,128)(2,1)S(1)}, u32[]{:S(2)}, u32[]{:S(2)}) collective-permute-start(bf16[16,1024]{1,0:T(8,128)(2,1)S(1)} %slice.7), channel_id=1, source_target_pairs={{0,1},{1,2},{2,3},{3,4},{4,5},{5,6},{6,7},{7,8},{8,9},{9,10},{10,1... | collective-permute-start | bytes 98312 | tf_op jit(solution)/shard_map/ppermute | solution.py:327
  18.2 0.8 %collective-permute-done.1.tail_ref = bf16[16,1024]{1,0:T(8,128)(2,1)S(1)} collective-permute-done((bf16[16,1024]{1,0:T(8,128)(2,1)S(1)}, bf16[16,1024]{1,0:T(8,128)(2,1)S(1)}, u32[]{:S(2)}, u32[]{:S(2)}) %collective-permute-start.1) | collective-permute-done | bytes 32800 | tf_op jit(solution)/shard_map/ppermute | solution.py:327
  19.1 0.0 collective-permute-done.kv_ref
  19.1 0.0 copy-start.11
  19.1 6.9 %all-to-all-done.parts_ref = bf16[32,48,128]{2,1,0:T(8,128)(2,1)S(1)} async-done(((bf16[32,48,128]{2,1,0:T(8,128)(2,1)}), bf16[32,48,128]{2,1,0:T(8,128)(2,1)S(1)}, u32[]{:S(2)}, u32[]{:S(2)}) %all-to-all-start) | async-done | bytes 393248 | tf_op jit(solution)/shard_map/all_to_all | solution.py:325
  26.0 1.7 %shard_map.47 = bf16[32,40,128]{2,1,0:T(8,128)(2,1)} custom-call(s32[1]{0:T(128)} %bitcast.place_ref, bf16[32,48,128]{2,1,0:T(8,128)(2,1)S(1)} %all-to-all-done.parts_ref), custom_call_target="tpu_custom_call" | custom-call | tf_op jit(solution)/shard_map/pallas_call | solution.py:292
  27.7 0.0 copy-done.11
  27.7 3.6 %all-to-all-start.1 = ((bf16[32,40,128]{2,1,0:T(8,128)(2,1)}), bf16[32,40,128]{2,1,0:T(8,128)(2,1)S(1)}, u32[]{:S(2)}, u32[]{:S(2)}) async-start(bf16[32,40,128]{2,1,0:T(8,128)(2,1)} %shard_map.47), calls=%async_computation.1 | async-start | bytes 655360 | tf_op jit(solution)/shard_map/all_to_all | solution.py:336
  31.3 0.0 copy-done
  31.3 0.0 copy-done.14
  31.3 0.0 copy-start.4
  31.3 0.9 %copy-done.4 = bf16[128,512]{1,0:T(8,128)(2,1)S(1)} copy-done((bf16[128,512]{1,0:T(8,128)(2,1)S(1)}, bf16[128,512]{1,0:T(8,128)(2,1)}, u32[]{:S(2)}) %copy-start.4) | copy-done | bytes 131096
  32.2 0.0 copy-start.12
  32.2 0.9 %copy-done.12 = bf16[64,2048]{1,0:T(8,128)(2,1)S(1)} copy-done((bf16[64,2048]{1,0:T(8,128)(2,1)S(1)}, bf16[64,2048]{1,0:T(8,128)(2,1)}, u32[]{:S(2)}) %copy-start.12) | copy-done | bytes 262168
  33.1 6.4 %shard_map.48 = (f32[128,1024]{1,0:T(8,128)S(1)}, f32[128,1024]{1,0:T(8,128)S(1)}, f32[128,1024]{1,0:T(8,128)S(1)}, bf16[16,256,160]{2,1,0:T(8,128)(2,1)S(1)}) custom-call(s32[1]{0:T(128)} %bitcast.place_ref, bf16[128,512]{1,0:T(8,128)(2,1)S(1)} %copy-done.4, bf16[128,1024]{1,0:T(8,128)(2,1)S(1)} %copy-done.2, f32[3,1024]{1,0:T(4,128)S(1)} %copy-done.14, ...), custom_call_target="tpu_custom_call" | custom-call | tf_op jit(solution)/shard_map/pallas_call | solution.py:292
  39.5 0.0 copy-start.5
  39.5 0.8 %copy-done.5 = f32[128,1024]{1,0:T(8,128)} copy-done((f32[128,1024]{1,0:T(8,128)}, f32[128,1024]{1,0:T(8,128)S(1)}, u32[]{:S(2)}) %copy-start.5) | copy-done | bytes 524312
  40.3 0.0 copy-start.7
  40.3 0.8 %copy-done.7 = f32[128,1024]{1,0:T(8,128)} copy-done((f32[128,1024]{1,0:T(8,128)}, f32[128,1024]{1,0:T(8,128)S(1)}, u32[]{:S(2)}) %copy-start.7) | copy-done | bytes 524312
  41.1 0.0 copy-start.9
  41.1 0.8 %copy-done.9 = f32[128,1024]{1,0:T(8,128)} copy-done((f32[128,1024]{1,0:T(8,128)}, f32[128,1024]{1,0:T(8,128)S(1)}, u32[]{:S(2)}) %copy-start.9) | copy-done | bytes 524312
  41.9 1.5 %all-to-all-done.1 = bf16[32,40,128]{2,1,0:T(8,128)(2,1)S(1)} async-done(((bf16[32,40,128]{2,1,0:T(8,128)(2,1)}), bf16[32,40,128]{2,1,0:T(8,128)(2,1)S(1)}, u32[]{:S(2)}, u32[]{:S(2)}) %all-to-all-start.1) | async-done | bytes 327712 | tf_op jit(solution)/shard_map/all_to_all | solution.py:336
  43.4 0.0 copy-start.6
  43.4 1.0 %copy-done.6 = f32[128,1024]{1,0:T(8,128)S(1)} copy-done((f32[128,1024]{1,0:T(8,128)S(1)}, f32[128,1024]{1,0:T(8,128)}, u32[]{:S(2)}) %copy-start.6) | copy-done | bytes 524312
  44.4 0.0 copy-start.8
  44.5 1.0 %copy-done.8 = f32[128,1024]{1,0:T(8,128)S(1)} copy-done((f32[128,1024]{1,0:T(8,128)S(1)}, f32[128,1024]{1,0:T(8,128)}, u32[]{:S(2)}) %copy-start.8) | copy-done | bytes 524312
  45.5 0.0 copy-start.10
  45.5 1.0 %copy-done.10 = f32[128,1024]{1,0:T(8,128)S(1)} copy-done((f32[128,1024]{1,0:T(8,128)S(1)}, f32[128,1024]{1,0:T(8,128)}, u32[]{:S(2)}) %copy-start.10) | copy-done | bytes 524312
  46.5 2.7 %shard_map.49 = bf16[128,1024]{1,0:T(8,128)(2,1)} custom-call(bf16[16,256,160]{2,1,0:T(8,128)(2,1)S(1)} %get-tuple-element.26.phi_ref, bf16[1280,128]{1,0:T(8,128)(2,1)S(1)} %bitcast.2, f32[128,1024]{1,0:T(8,128)S(1)} %copy-done.6, f32[128,1024]{1,0:T(8,128)S(1)} %copy-done.8, f32[128,1024]{1,0:T(8,128)S(1)} %copy-done.10), custom_call_target="tpu_custom_call" | custom-call | tf_op jit(solution)/shard_map/pallas_call | solution.py:292
  (1 shorter events, 0.0 us)
Async XLA Ops:
  0.0 0.9 %copy-start.1 = (bf16[128,1024]{1,0:T(8,128)(2,1)S(1)}, bf16[128,1024]{1,0:T(8,128)(2,1)}, u32[]{:S(2)}) copy-start(bf16[128,1024]{1,0:T(8,128)(2,1)} %v_ref) | copy-start | bytes 786436
  1.0 0.9 %copy-start.3 = (bf16[128,512]{1,0:T(8,128)(2,1)S(1)}, bf16[128,512]{1,0:T(8,128)(2,1)}, u32[]{:S(2)}) copy-start(bf16[128,512]{1,0:T(8,128)(2,1)} %qk_ref.1) | copy-start | bytes 393220
  1.9 0.7 %copy-start.13 = (f32[3,1024]{1,0:T(4,128)S(1)}, f32[3,1024]{1,0:T(4,128)}, u32[]{:S(2)}) copy-start(f32[3,1024]{1,0:T(4,128)} %conv_ref.1) | copy-start | bytes 36868
  2.6 12.1 %copy-start.2 = (bf16[128,1024]{1,0:T(8,128)(2,1)S(1)}, bf16[128,1024]{1,0:T(8,128)(2,1)}, u32[]{:S(2)}) copy-start(bf16[128,1024]{1,0:T(8,128)(2,1)} %v_ref) | copy-start | bytes 786436
  2.6 28.7 %copy-start = (bf16[128,3072]{1,0:T(8,128)(2,1)S(1)}, bf16[128,3072]{1,0:T(8,128)(2,1)}, u32[]{:S(2)}) copy-start(bf16[128,3072]{1,0:T(8,128)(2,1)} %swa_ref) | copy-start | bytes 2359300
  2.6 28.7 %copy-start.14 = (f32[3,1024]{1,0:T(4,128)S(1)}, f32[3,1024]{1,0:T(4,128)}, u32[]{:S(2)}) copy-start(f32[3,1024]{1,0:T(4,128)} %conv_ref.1) | copy-start | bytes 36868
  4.2 21.8 %all-to-all-start = ((bf16[32,48,128]{2,1,0:T(8,128)(2,1)}), bf16[32,48,128]{2,1,0:T(8,128)(2,1)S(1)}, u32[]{:S(2)}, u32[]{:S(2)}) async-start(bf16[32,48,128]{2,1,0:T(8,128)(2,1)} %shard_map.46), calls=%async_computation | async-start | bytes 786432 | tf_op jit(solution)/shard_map/all_to_all | solution.py:325
  12.5 6.6 %collective-permute-start = (bf16[64,2048]{1,0:T(8,128)(2,1)S(1)}, bf16[64,2048]{1,0:T(8,128)(2,1)S(1)}, u32[]{:S(2)}, u32[]{:S(2)}) collective-permute-start(bf16[64,2048]{1,0:T(8,128)(2,1)S(1)} %slice.6), channel_id=1, source_target_pairs={{0,1},{1,2},{2,3},{3,4},{4,5},{5,6},{6,7},{7,8},{8,9},{9,10},{10,1... | collective-permute-start | bytes 786440 | tf_op jit(solution)/shard_map/ppermute | solution.py:326
  14.7 4.4 %collective-permute-start.1 = (bf16[16,1024]{1,0:T(8,128)(2,1)S(1)}, bf16[16,1024]{1,0:T(8,128)(2,1)S(1)}, u32[]{:S(2)}, u32[]{:S(2)}) collective-permute-start(bf16[16,1024]{1,0:T(8,128)(2,1)S(1)} %slice.7), channel_id=1, source_target_pairs={{0,1},{1,2},{2,3},{3,4},{4,5},{5,6},{6,7},{7,8},{8,9},{9,10},{10,1... | collective-permute-start | bytes 98312 | tf_op jit(solution)/shard_map/ppermute | solution.py:327
  19.1 8.6 %copy-start.11 = (bf16[64,2048]{1,0:T(8,128)(2,1)}, bf16[64,2048]{1,0:T(8,128)(2,1)S(1)}, u32[]{:S(2)}) copy-start(bf16[64,2048]{1,0:T(8,128)(2,1)S(1)} %collective-permute-done.kv_ref) | copy-start | bytes 786436
  27.7 15.7 %all-to-all-start.1 = ((bf16[32,40,128]{2,1,0:T(8,128)(2,1)}), bf16[32,40,128]{2,1,0:T(8,128)(2,1)S(1)}, u32[]{:S(2)}, u32[]{:S(2)}) async-start(bf16[32,40,128]{2,1,0:T(8,128)(2,1)} %shard_map.47), calls=%async_computation.1 | async-start | bytes 655360 | tf_op jit(solution)/shard_map/all_to_all | solution.py:336
  31.3 0.9 %copy-start.4 = (bf16[128,512]{1,0:T(8,128)(2,1)S(1)}, bf16[128,512]{1,0:T(8,128)(2,1)}, u32[]{:S(2)}) copy-start(bf16[128,512]{1,0:T(8,128)(2,1)} %qk_ref.1) | copy-start | bytes 393220
  32.2 0.9 %copy-start.12 = (bf16[64,2048]{1,0:T(8,128)(2,1)S(1)}, bf16[64,2048]{1,0:T(8,128)(2,1)}, u32[]{:S(2)}) copy-start(bf16[64,2048]{1,0:T(8,128)(2,1)} %copy-done.11) | copy-start | bytes 786436
  39.5 0.8 %copy-start.5 = (f32[128,1024]{1,0:T(8,128)}, f32[128,1024]{1,0:T(8,128)S(1)}, u32[]{:S(2)}) copy-start(f32[128,1024]{1,0:T(8,128)S(1)} %get-tuple-element.28.numer_ref) | copy-start | bytes 1572868
  40.3 0.8 %copy-start.7 = (f32[128,1024]{1,0:T(8,128)}, f32[128,1024]{1,0:T(8,128)S(1)}, u32[]{:S(2)}) copy-start(f32[128,1024]{1,0:T(8,128)S(1)} %get-tuple-element.29.denom_ref) | copy-start | bytes 1572868
  41.1 0.8 %copy-start.9 = (f32[128,1024]{1,0:T(8,128)}, f32[128,1024]{1,0:T(8,128)S(1)}, u32[]{:S(2)}) copy-start(f32[128,1024]{1,0:T(8,128)S(1)} %get-tuple-element.30.swa_ref) | copy-start | bytes 1572868
  43.4 1.0 %copy-start.6 = (f32[128,1024]{1,0:T(8,128)S(1)}, f32[128,1024]{1,0:T(8,128)}, u32[]{:S(2)}) copy-start(f32[128,1024]{1,0:T(8,128)} %copy-done.5) | copy-start | bytes 1572868
  44.4 1.0 %copy-start.8 = (f32[128,1024]{1,0:T(8,128)S(1)}, f32[128,1024]{1,0:T(8,128)}, u32[]{:S(2)}) copy-start(f32[128,1024]{1,0:T(8,128)} %copy-done.7) | copy-start | bytes 1572868
  45.5 1.0 %copy-start.10 = (f32[128,1024]{1,0:T(8,128)S(1)}, f32[128,1024]{1,0:T(8,128)}, u32[]{:S(2)}) copy-start(f32[128,1024]{1,0:T(8,128)} %copy-done.9) | copy-start | bytes 1572868

commit v3 on v2

--- a/solution.py
+++ b/solution.py
@@ -23,7 +23,6 @@
 ROWS = 160
 TAIL = 16
 EXTRA = 8
-VMEM_LIMIT = 48 * 1024 * 1024
 
 
 NT = (((1,), (1,)), ((), ()))
@@ -196,8 +195,27 @@
 
 
 def local_kernel(
-    place_ref, qk_ref, v_ref, conv_ref, swa_ref, kv_ref, tail_ref, numer_ref, denom_ref, swa_out_ref, phi_ref
+    place_ref, qk_hbm, v_hbm, conv_hbm, swa_hbm, kv_hbm, tail_hbm,
+    numer_hbm, denom_hbm, swa_out_hbm, phi_hbm,
+    qk_ref, v_ref, conv_ref, swa_ref, kv_ref, tail_ref,
+    numer_ref, denom_ref, swa_out_ref, phi_ref, sems_in, sems_out,
 ):
+    pairs = (
+        (qk_hbm, qk_ref), (v_hbm, v_ref), (conv_hbm, conv_ref), (tail_hbm, tail_ref),
+        (swa_hbm, swa_ref), (kv_hbm, kv_ref),
+    )
+    copies = [pltpu.make_async_copy(a, b, sems_in.at[i]) for i, (a, b) in enumerate(pairs)]
+    for copy in copies:
+        copy.start()
+    for copy in copies[:4]:
+        copy.wait()
+    results_out = []
+
+    def send(here, there):
+        copy = pltpu.make_async_copy(here, there, sems_out.at[len(results_out)])
+        copy.start()
+        results_out.append(copy)
+
     rows = v_ref.shape[0]
     width = HEADS * FEAT
     query = qk_ref[:, :width]
@@ -229,6 +247,11 @@
         lower = lane_id < VHEAD
         numer_ref[:, lanes] = jnp.where(lower, results[0][:, :LANES], results[1][:, :LANES])
         denom_ref[:, lanes] = jnp.where(lower, results[0][:, LANES:], results[1][:, LANES:])
+        send(phi_ref.at[2 * pair : 2 * pair + 2], phi_hbm.at[2 * pair : 2 * pair + 2])
+    send(numer_ref, numer_hbm)
+    send(denom_ref, denom_hbm)
+    for copy in copies[4:]:
+        copy.wait()
     swa_width = SWA_HEADS * SWA_HEAD
     not_before = jnp.where(place_ref[0] == 0, WINDOW, 0)
     span = 2 * WINDOW
@@ -254,9 +277,26 @@
             expo = jnp.exp(score - jnp.max(score, axis=-1, keepdims=True))
             probs = (expo / jnp.sum(expo, axis=-1, keepdims=True)).astype(BF16)
             swa_out_ref[mine, at : at + SWA_HEAD] = dot(probs, both[1])
-
-
-def readout_kernel(phi_ref, past_ref, numer_ref, denom_ref, swa_ref, out_ref):
+    send(swa_out_ref, swa_out_hbm)
+    for copy in results_out:
+        copy.wait()
+
+
+def readout_kernel(
+    past_hbm, phi_hbm, numer_hbm, denom_hbm, swa_hbm, out_ref,
+    past_ref, phi_ref, numer_ref, denom_ref, swa_ref, sems,
+):
+    copies = [
+        pltpu.make_async_copy(
+            phi_hbm.at[2 * pair : 2 * pair + 2], phi_ref.at[2 * pair : 2 * pair + 2], sems.at[pair]
+        )
+        for pair in range(PAIRS)
+    ]
+    shares = ((past_hbm, past_ref), (numer_hbm, numer_ref), (denom_hbm, denom_ref), (swa_hbm, swa_ref))
+    rest = [pltpu.make_async_copy(a, b, sems.at[PAIRS + i]) for i, (a, b) in enumerate(shares)]
+    for copy in rest[:1] + copies[:1] + rest[1:] + copies[1:]:
+        copy.start()
+    rest[0].wait()
     rows = out_ref.shape[0]
     lower = iota((rows, LANES), 1) < VHEAD
     norms = []
@@ -275,6 +315,9 @@
         spread = dot(norms, jnp.where(source == wanted, 1.0, 0.0).astype(BF16)).astype(BF16)
         right = jnp.concatenate([past_ref[pair * ROWS : (pair + 1) * ROWS, :], spread], axis=1)
         results = []
+        copies[pair].wait()
+        for copy in rest[1:] if pair == 0 else ():
+            copy.wait()
         for head in (2 * pair, 2 * pair + 1):
             result = dot(phi_ref[head], right)
             results.append(result[:rows] + result[rows:])
@@ -285,18 +328,22 @@
 
 IN_VMEM = pl.BlockSpec(memory_space=pltpu.VMEM)
 IN_SMEM = pl.BlockSpec(memory_space=pltpu.SMEM)
-IN_PLACE = pl.BlockSpec(memory_space=pl.ANY)
-
-
-def call(kernel, outs, args, specs, scratch=()):
+IN_HBM = pl.BlockSpec(memory_space=pltpu.HBM)
+
+
+def call(kernel, outs, args, specs, out_spec, scratch=(), grant=60):
     return pl.pallas_call(
         kernel,
         out_shape=outs,
         in_specs=specs,
-        out_specs=jax.tree.map(lambda _: IN_VMEM, outs),
+        out_specs=jax.tree.map(lambda _: out_spec, outs),
         scratch_shapes=scratch,
-        compiler_params=pltpu.CompilerParams(vmem_limit_bytes=VMEM_LIMIT),
+        compiler_params=pltpu.CompilerParams(vmem_limit_bytes=grant * 1024 * 1024),
     )(*args)
+
+
+def like(*arrays):
+    return [pltpu.VMEM(a.shape, a.dtype) for a in arrays]
 
 
 def shards(lin_qk, lin_v, conv_w, swa_qkv):
@@ -308,18 +355,15 @@
     part = PAIRS * ROWS // devices
     held = (part + 7) // 8 * 8 + EXTRA
     shape = jax.ShapeDtypeStruct
+    sems = pltpu.SemaphoreType.DMA
 
     messages = call(
         functools.partial(state_kernel, part),
         shape((devices, held, LANES), BF16),
         [lin_qk, lin_v, conv_w],
-        [IN_PLACE] * 3,
-        [
-            pltpu.VMEM((rows, HEADS * FEAT), BF16),
-            pltpu.VMEM(lin_v.shape, BF16),
-            pltpu.VMEM(conv_w.shape, jnp.float32),
-            pltpu.SemaphoreType.DMA((3,)),
-        ],
+        [IN_HBM] * 3,
+        IN_VMEM,
+        [pltpu.VMEM((rows, HEADS * FEAT), BF16)] + like(lin_v, conv_w) + [sems((3,))],
     )
     messages, lin_v, swa_qkv = lax.optimization_barrier((messages, lin_v, swa_qkv))
     parts = lax.all_to_all(messages, AXES, 0, 0, tiled=True)
@@ -331,20 +375,29 @@
         shape((devices, part, LANES), BF16),
         [place, parts],
         [IN_SMEM, IN_VMEM],
+        IN_VMEM,
+        grant=16,
     )
     past, tail_kv, tail_v = lax.optimization_barrier((past, tail_kv, tail_v))
     past = lax.all_to_all(past, AXES, 0, 0, tiled=True).reshape(PAIRS * ROWS, LANES)
+    wide = shape(lin_v.shape, jnp.float32)
+    phis = shape((HEADS, 2 * rows, ROWS), BF16)
     numer, denom, swa, phi = call(
         local_kernel,
-        [shape(lin_v.shape, jnp.float32)] * 3 + [shape((HEADS, 2 * rows, ROWS), BF16)],
+        [wide, wide, wide, phis],
         [place, lin_qk, lin_v, conv_w, swa_qkv, tail_kv, tail_v],
-        [IN_SMEM] + [IN_VMEM] * 6,
+        [IN_SMEM] + [IN_HBM] * 6,
+        IN_HBM,
+        like(lin_qk, lin_v, conv_w, swa_qkv, tail_kv, tail_v, wide, wide, wide, phis)
+        + [sems((6,)), sems((PAIRS + 3,))],
     )
     return call(
         readout_kernel,
         shape(lin_v.shape, BF16),
-        [phi, past, numer, denom, swa],
-        [IN_VMEM] * 5,
+        [past, phi, numer, denom, swa],
+        [IN_HBM] * 5,
+        IN_VMEM,
+        like(past, phis, wide, wide, wide) + [sems((PAIRS + 4,))],
     )
 
 

time: 49.8 us -> 47.2 us (0.948)
  local copies, waits for them, and re-layouts: 10.9 us -> 2.48 us
  Pallas kernels: 12.3 us -> 17 us
  waiting for transfers between devices: 9.3 us -> 10.6 us
    unnamed x30 -> x6, local copies, waits for them, and re-layouts: 9.95 us -> 0.74 us
    pallas_call x4, Pallas kernels: 12.3 us -> 17 us  [call(): pl.pallas_call(kernel, out_shape=outs, in_specs=specs, out_specs=jax.tree...]
    all_to_all x1, waiting for transfers between devices: 1.51 us -> 3.54 us  [shards(): lax.all_to_all(past, AXES, 0, 0, tiled=True).reshape(PAIRS * ROWS, LANES)]
    slice x1, local copies, waits for them, and re-layouts: 0.01 us -> 0.76 us  [shards(): tail_v = lax.ppermute(lin_v[rows - TAIL:], AXES, shift)]
    all_to_all x1, waiting for transfers between devices: 6.95 us -> 6.22 us  [shards(): parts = lax.all_to_all(messages, AXES, 0, 0, tiled=True)]
  transfers between devices with their start and end apart: 4 -> 4, of which waited for: 3 -> 3; matrix products, arithmetic and copies ran while one was open for 2% -> 4% of each run, Pallas kernels for 13% -> 18%
where the time goes in v3:
time: 47.2 us; the launch traced here: 46.8 us
  Pallas kernels  17 us (36%)
  starting transfers between devices  16.6 us (35%)
  waiting for transfers between devices  10.6 us (22%)
  local copies, waits for them, and re-layouts  2.48 us (5%)
    pallas_call x4, Pallas kernels, call(): pl.pallas_call(kernel, out_shape=outs, in_specs=specs, out_specs=jax.tree...  17 us
    all_to_all x1, starting transfers between devices, shards(): parts = lax.all_to_all(messages, AXES, 0, 0, tiled=True)  7.31 us
    all_to_all x1, waiting for transfers between devices, shards(): parts = lax.all_to_all(messages, AXES, 0, 0, tiled=True)  6.22 us
    all_to_all x1, starting transfers between devices, shards(): lax.all_to_all(past, AXES, 0, 0, tiled=True).reshape(PAIRS * ROWS, LANES)  3.58 us
    all_to_all x1, waiting for transfers between devices, shards(): lax.all_to_all(past, AXES, 0, 0, tiled=True).reshape(PAIRS * ROWS, LANES)  3.54 us
    ppermute x1, starting transfers between devices, shards(): tail_v = lax.ppermute(lin_v[rows - TAIL:], AXES, shift)  3.52 us
    ppermute x1, starting transfers between devices, shards(): tail_kv = lax.ppermute(swa_qkv[rows - WINDOW:, swa_width:], AXES, shift)  2.17 us
    slice x1, local copies, waits for them, and re-layouts, shards(): tail_kv = lax.ppermute(swa_qkv[rows - WINDOW:, swa_width:], AXES, shift)  0.97 us
  transfers between devices with their start and end apart: 4, of which 3 were waited for; matrix products, arithmetic and copies ran while one was open for 4% of the time, Pallas kernels for 18%

profile of v3, /device:TPU:0, one launch (start us, length us, event | category | flops | bytes accessed | tf_op | source)
XLA Modules:
  0.0 46.8 jit_solution(12923025386215760993)
XLA Ops:
  0.0 2.5 %shard_map.46 = bf16[32,48,128]{2,1,0:T(8,128)(2,1)} custom-call(bf16[128,512]{1,0:T(8,128)(2,1)} %qk_hbm.3, bf16[128,1024]{1,0:T(8,128)(2,1)} %v_hbm.2, f32[3,1024]{1,0:T(4,128)} %conv_hbm.3), custom_call_target="tpu_custom_call" | custom-call | tf_op jit(solution)/shard_map/pallas_call | solution.py:335
  2.6 7.3 %all-to-all-start = ((bf16[32,48,128]{2,1,0:T(8,128)(2,1)}), bf16[32,48,128]{2,1,0:T(8,128)(2,1)S(1)}, u32[]{:S(2)}, u32[]{:S(2)}) async-start(bf16[32,48,128]{2,1,0:T(8,128)(2,1)} %shard_map.46), calls=%async_computation | async-start | bytes 786432 | tf_op jit(solution)/shard_map/all_to_all | solution.py:369
  9.9 1.0 %slice.6 = bf16[64,2048]{1,0:T(8,128)(2,1)S(1)} slice(bf16[128,3072]{1,0:T(8,128)(2,1)} %swa_hbm), slice={[64:128], [1024:3072]} | slice | bytes 524288 | tf_op jit(solution)/shard_map/slice | solution.py:370
  10.8 2.2 %collective-permute-start = (bf16[64,2048]{1,0:T(8,128)(2,1)S(1)}, bf16[64,2048]{1,0:T(8,128)(2,1)S(1)}, u32[]{:S(2)}, u32[]{:S(2)}) collective-permute-start(bf16[64,2048]{1,0:T(8,128)(2,1)S(1)} %slice.6), channel_id=1, source_target_pairs={{0,1},{1,2},{2,3},{3,4},{4,5},{5,6},{6,7},{7,8},{8,9},{9,10},{10,1... | collective-permute-start | bytes 786440 | tf_op jit(solution)/shard_map/ppermute | solution.py:370
  13.0 0.8 %slice.7 = bf16[16,1024]{1,0:T(8,128)(2,1)S(1)} slice(bf16[128,1024]{1,0:T(8,128)(2,1)} %v_hbm.2), slice={[112:128], [0:1024]} | slice | bytes 65536 | tf_op jit(solution)/shard_map/slice | solution.py:371
  13.8 3.5 %collective-permute-start.1 = (bf16[16,1024]{1,0:T(8,128)(2,1)S(1)}, bf16[16,1024]{1,0:T(8,128)(2,1)S(1)}, u32[]{:S(2)}, u32[]{:S(2)}) collective-permute-start(bf16[16,1024]{1,0:T(8,128)(2,1)S(1)} %slice.7), channel_id=1, source_target_pairs={{0,1},{1,2},{2,3},{3,4},{4,5},{5,6},{6,7},{7,8},{8,9},{9,10},{10,1... | collective-permute-start | bytes 98312 | tf_op jit(solution)/shard_map/ppermute | solution.py:371
  17.3 0.8 %collective-permute-done.1.tail_hbm = bf16[16,1024]{1,0:T(8,128)(2,1)S(1)} collective-permute-done((bf16[16,1024]{1,0:T(8,128)(2,1)S(1)}, bf16[16,1024]{1,0:T(8,128)(2,1)S(1)}, u32[]{:S(2)}, u32[]{:S(2)}) %collective-permute-start.1) | collective-permute-done | bytes 32800 | tf_op jit(solution)/shard_map/ppermute | solution.py:371
  18.2 0.0 copy-start.2
  18.2 0.0 collective-permute-done.kv_hbm
  18.2 0.0 copy-start.1
  18.2 6.2 %all-to-all-done.parts_ref = bf16[32,48,128]{2,1,0:T(8,128)(2,1)S(1)} async-done(((bf16[32,48,128]{2,1,0:T(8,128)(2,1)}), bf16[32,48,128]{2,1,0:T(8,128)(2,1)S(1)}, u32[]{:S(2)}, u32[]{:S(2)}) %all-to-all-start) | async-done | bytes 393248 | tf_op jit(solution)/shard_map/all_to_all | solution.py:369
  24.4 1.7 %shard_map.47 = bf16[32,40,128]{2,1,0:T(8,128)(2,1)} custom-call(s32[1]{0:T(128)} %bitcast.place_ref, bf16[32,48,128]{2,1,0:T(8,128)(2,1)S(1)} %all-to-all-done.parts_ref), custom_call_target="tpu_custom_call" | custom-call | tf_op jit(solution)/shard_map/pallas_call | solution.py:335
  26.0 3.6 %all-to-all-start.1 = ((bf16[32,40,128]{2,1,0:T(8,128)(2,1)}), bf16[32,40,128]{2,1,0:T(8,128)(2,1)S(1)}, u32[]{:S(2)}, u32[]{:S(2)}) async-start(bf16[32,40,128]{2,1,0:T(8,128)(2,1)} %shard_map.47), calls=%async_computation.1 | async-start | bytes 655360 | tf_op jit(solution)/shard_map/all_to_all | solution.py:382
  29.6 0.0 copy-done.2
  29.6 0.0 copy-done.1
  29.7 8.6 %shard_map.48 = (f32[128,1024]{1,0:T(8,128)}, f32[128,1024]{1,0:T(8,128)}, f32[128,1024]{1,0:T(8,128)}, bf16[16,256,160]{2,1,0:T(8,128)(2,1)}) custom-call(s32[1]{0:T(128)} %bitcast.place_ref, bf16[128,512]{1,0:T(8,128)(2,1)} %qk_hbm.3, bf16[128,1024]{1,0:T(8,128)(2,1)} %v_hbm.2, f32[3,1024]{1,0:T(4,128)} %conv_hbm.3, bf16[128,3072]{1,0:T(8,128)(2,1)} %swa_hbm, ...), custom_call_target="tpu_custom_call" | custom-call | tf_op jit(solution)/shard_map/pallas_call | solution.py:335
  38.2 3.5 %all-to-all-done.1 = bf16[32,40,128]{2,1,0:T(8,128)(2,1)S(1)} async-done(((bf16[32,40,128]{2,1,0:T(8,128)(2,1)}), bf16[32,40,128]{2,1,0:T(8,128)(2,1)S(1)}, u32[]{:S(2)}, u32[]{:S(2)}) %all-to-all-start.1) | async-done | bytes 327712 | tf_op jit(solution)/shard_map/all_to_all | solution.py:382
  41.8 0.0 copy-start
  41.8 0.7 %copy-done = bf16[32,40,128]{2,1,0:T(8,128)(2,1)} copy-done((bf16[32,40,128]{2,1,0:T(8,128)(2,1)}, bf16[32,40,128]{2,1,0:T(8,128)(2,1)S(1)}, u32[]{:S(2)}) %copy-start) | copy-done | bytes 327704
  42.5 4.2 %shard_map.49 = bf16[128,1024]{1,0:T(8,128)(2,1)} custom-call(bf16[1280,128]{1,0:T(8,128)(2,1)} %bitcast.2, bf16[16,256,160]{2,1,0:T(8,128)(2,1)} %get-tuple-element.27.phi_hbm, f32[128,1024]{1,0:T(8,128)} %get-tuple-element.28.numer_hbm, f32[128,1024]{1,0:T(8,128)} %get-tuple-element.29.denom_hbm, f32[128,1024]{1,0:T(8,128)} %get-tuple-element.30.swa_hbm), custom_call_target="tpu_custom_call" | custom-call | tf_op jit(solution)/shard_map/pallas_call | solution.py:335
Async XLA Ops:
  2.6 21.8 %all-to-all-start = ((bf16[32,48,128]{2,1,0:T(8,128)(2,1)}), bf16[32,48,128]{2,1,0:T(8,128)(2,1)S(1)}, u32[]{:S(2)}, u32[]{:S(2)}) async-start(bf16[32,48,128]{2,1,0:T(8,128)(2,1)} %shard_map.46), calls=%async_computation | async-start | bytes 786432 | tf_op jit(solution)/shard_map/all_to_all | solution.py:369
  10.8 7.3 %collective-permute-start = (bf16[64,2048]{1,0:T(8,128)(2,1)S(1)}, bf16[64,2048]{1,0:T(8,128)(2,1)S(1)}, u32[]{:S(2)}, u32[]{:S(2)}) collective-permute-start(bf16[64,2048]{1,0:T(8,128)(2,1)S(1)} %slice.6), channel_id=1, source_target_pairs={{0,1},{1,2},{2,3},{3,4},{4,5},{5,6},{6,7},{7,8},{8,9},{9,10},{10,1... | collective-permute-start | bytes 786440 | tf_op jit(solution)/shard_map/ppermute | solution.py:370
  13.8 4.4 %collective-permute-start.1 = (bf16[16,1024]{1,0:T(8,128)(2,1)S(1)}, bf16[16,1024]{1,0:T(8,128)(2,1)S(1)}, u32[]{:S(2)}, u32[]{:S(2)}) collective-permute-start(bf16[16,1024]{1,0:T(8,128)(2,1)S(1)} %slice.7), channel_id=1, source_target_pairs={{0,1},{1,2},{2,3},{3,4},{4,5},{5,6},{6,7},{7,8},{8,9},{9,10},{10,1... | collective-permute-start | bytes 98312 | tf_op jit(solution)/shard_map/ppermute | solution.py:371
  18.2 11.5 %copy-start.2 = (bf16[16,1024]{1,0:T(8,128)(2,1)}, bf16[16,1024]{1,0:T(8,128)(2,1)S(1)}, u32[]{:S(2)}) copy-start(bf16[16,1024]{1,0:T(8,128)(2,1)S(1)} %collective-permute-done.1.tail_hbm) | copy-start | bytes 98308
  18.2 11.5 %copy-start.1 = (bf16[64,2048]{1,0:T(8,128)(2,1)}, bf16[64,2048]{1,0:T(8,128)(2,1)S(1)}, u32[]{:S(2)}) copy-start(bf16[64,2048]{1,0:T(8,128)(2,1)S(1)} %collective-permute-done.kv_hbm) | copy-start | bytes 786436
  26.0 15.7 %all-to-all-start.1 = ((bf16[32,40,128]{2,1,0:T(8,128)(2,1)}), bf16[32,40,128]{2,1,0:T(8,128)(2,1)S(1)}, u32[]{:S(2)}, u32[]{:S(2)}) async-start(bf16[32,40,128]{2,1,0:T(8,128)(2,1)} %shard_map.47), calls=%async_computation.1 | async-start | bytes 655360 | tf_op jit(solution)/shard_map/all_to_all | solution.py:382
  41.8 0.7 %copy-start = (bf16[32,40,128]{2,1,0:T(8,128)(2,1)}, bf16[32,40,128]{2,1,0:T(8,128)(2,1)S(1)}, u32[]{:S(2)}) copy-start(bf16[32,40,128]{2,1,0:T(8,128)(2,1)S(1)} %all-to-all-done.1) | copy-start | bytes 983044

commit v4 on v2

v4 whole, which is shorter than its diff:
```python
import functools

import jax
import jax.numpy as jnp
import numpy as np
from jax import lax
from jax.experimental import pallas as pl
from jax.experimental.pallas import tpu as pltpu
from jax.sharding import PartitionSpec as P

HEADS = 16
FEAT = 16
VHEAD = 64
SWA_HEADS = 8
SWA_HEAD = 128
WINDOW = 64

AXES = ("ctxouter", "ctxinner")
SPLIT = ("outer", "z", "core")
CHIPS = ("outer", "z")
LANES = 128
PAIRS = HEADS // 2
QUADS = FEAT * (FEAT + 1) // 2
CONST = QUADS + FEAT
ROWS = 160
TAIL = 16
EXTRA = 8


NT = (((1,), (1,)), ((), ()))
NN = (((1,), (0,)), ((), ()))
BF16 = jnp.bfloat16


def dot(a, b, dims=NN):
    return lax.dot_general(a, b, dims, preferred_element_type=jnp.float32)


def iota(shape, dim):
    return lax.broadcasted_iota(jnp.int32, shape, dim)


def selector(feature, lane, second, halved=False):
    scale = FEAT ** (-0.25)
    quad = feature < QUADS
    entry = feature % FEAT
    if second:
        wanted = (feature + feature // FEAT) % FEAT
        return jnp.where((lane % FEAT == wanted) & quad, scale, 0.0)
    linear = (feature >= QUADS) & (feature < CONST)
    wanted = jnp.where(quad, entry, (feature - QUADS) % FEAT)
    weight = jnp.where((feature < FEAT) & halved, 0.5 * scale, scale)
    return jnp.where((lane % FEAT == wanted) & (quad | linear), weight, 0.0)


def adders(feature):
    first = jnp.where(feature == CONST, 1.0, 0.0)
    second = jnp.where((feature >= QUADS) & (feature <= CONST), 1.0, 0.0)
    return first, second


def head_mask(head, shape):
    place = iota(shape, 1)
    return (place >= head * FEAT) & (place < (head + 1) * FEAT)


def hi_lo(values):
    high = values.astype(BF16)
    return high, (values - high.astype(jnp.float32)).astype(BF16)


def convolved(value, tail, conv_ref, lanes):
    row_id = iota(value.shape, 0)
    result = conv_ref[0:1, lanes] * value
    for lag in range(1, conv_ref.shape[0]):
        shifted = pltpu.roll(value, lag, 0)
        for row in range(lag):
            source = TAIL - lag + row
            before = 0.0 if tail is None else tail[source : source + 1]
            shifted = jnp.where(row_id == row, before, shifted)
        result = result + conv_ref[lag : lag + 1, lanes] * shifted
    return result.astype(BF16)


def state_kernel(
    part, qk_hbm, v_hbm, other_qk_hbm, other_v_hbm, conv_hbm, swa_hbm, out_ref, tails_ref,
    key_ref, v_ref, conv_ref, sems,
):
    rows, wide = v_hbm.shape
    taps = conv_ref.shape[0]
    core = lax.axis_index("core")
    mine = pl.ds(pl.multiple_of(core * (wide // 2), wide // 2), wide // 2)
    keys = pl.ds(pl.multiple_of(HEADS * FEAT + core * LANES, LANES), LANES)
    here = pl.ds(pl.multiple_of(core * rows, rows), rows)
    there = pl.ds(pl.multiple_of((1 - core) * rows, rows), rows)
    copies = [
        pltpu.make_async_copy(qk_hbm.at[:, keys], key_ref.at[here, :], sems.at[0]),
        pltpu.make_async_copy(other_qk_hbm.at[:, keys], key_ref.at[there, :], sems.at[1]),
        pltpu.make_async_copy(conv_hbm.at[:, mine], conv_ref, sems.at[2]),
        pltpu.make_async_copy(v_hbm.at[:, mine], v_ref.at[here, :], sems.at[3]),
        pltpu.make_async_copy(other_v_hbm.at[:, mine], v_ref.at[there, :], sems.at[4]),
        pltpu.make_async_copy(
            swa_hbm.at[rows - WINDOW :, tails_ref.shape[1] // 2 :], tails_ref.at[:WINDOW, :], sems.at[5]
        ),
        pltpu.make_async_copy(v_hbm.at[rows - TAIL :, :], tails_ref.at[WINDOW:, :wide], sems.at[6]),
    ]
    for copy in copies:
        copy.start()
    for copy in copies[:2]:
        copy.wait()
    tokens = 2 * rows
    key_t = (key_ref[...].astype(jnp.float32) * FEAT ** (-0.25)).T
    const_rows = jnp.where(iota((EXTRA, tokens), 0) == 0, 1.0, 0.0)
    lane_id = iota((ROWS, LANES), 1)
    low_row = iota((EXTRA, LANES), 0)
    ones = jnp.ones((tokens, LANES), BF16)
    half = FEAT // 2
    padded = (part + 7) // 8 * 8
    lefts = []
    for head in range(HEADS // 2):
        x = key_t[head * FEAT : (head + 1) * FEAT]
        blocks = [x * x]
        for by in range(1, half):
            blocks.append(x * jnp.concatenate([x[by:], x[:by]], axis=0))
        blocks += [x[:half] * x[half:], x, const_rows]
        lefts.append(jnp.concatenate(hi_lo(jnp.concatenate(blocks, axis=0)), axis=1))
    first_keys = key_ref[0:16].astype(jnp.float32)
    for copy in copies[2:5]:
        copy.wait()
    states = []
    extras = []
    norms = jnp.zeros((ROWS, LANES), jnp.float32)
    for pair in range(PAIRS // 2):
        lanes = slice(pair * LANES, (pair + 1) * LANES)
        value = v_ref[:, lanes].astype(jnp.float32)
        conved = convolved(value, None, conv_ref, lanes)
        right = jnp.concatenate([conved, ones], axis=1)
        right = jnp.concatenate([right, right], axis=0)
        both = []
        for head in (2 * pair, 2 * pair + 1):
            result = dot(lefts[head], right)
            both.append(result[:, :LANES])
            norms = jnp.where(lane_id // 8 == head, result[:, LANES:], norms)
        states.append(jnp.where(lane_id < VHEAD, both[0], both[1]))
        extra = jnp.zeros((EXTRA, LANES), jnp.float32)
        for row in range(taps - 1):
            share = jnp.zeros((1, LANES), jnp.float32)
            for lag in range(row + 1, taps):
                at = tokens + row - lag
                share = share + conv_ref[lag : lag + 1, lanes] * value[at : at + 1]
            extra = jnp.where(low_row == row, share, extra)
            extra = jnp.where(low_row == taps - 1 + row, first_keys[row : row + 1], extra)
        extras.append(extra)
    norms_t = norms.T
    for pair in range(PAIRS // 2):
        last = states[pair][CONST:]
        for place in range(2):
            at = 8 * (2 * pair + place)
            norm = norms_t[at : at + 8]
            rest = jnp.concatenate(
                [norm[:, LANES:], jnp.zeros((8, 2 * LANES - ROWS), jnp.float32)], axis=1
            )
            last = jnp.where(low_row == 1 + 2 * place, norm[:, :LANES], last)
            last = jnp.where(low_row == 2 + 2 * place, rest, last)
        state = jnp.concatenate([states[pair][:CONST], last], axis=0)
        for piece in range(ROWS // part):
            rows_of = [state[piece * part : (piece + 1) * part]]
            if padded != part:
                rows_of.append(jnp.zeros((padded - part, LANES), jnp.float32))
            message = jnp.concatenate(rows_of + [extras[pair]], axis=0)
            out_ref[pair * (ROWS // part) + piece] = message.astype(BF16)
    for copy in copies[5:]:
        copy.wait()


def prefix_kernel(taps, parts_ref, out_ref):
    chips, held, _ = parts_ref.shape
    part = out_ref.shape[1]
    padded = held - EXTRA
    width = chips * EXTRA
    chip, core = lax.axis_index(CHIPS), lax.axis_index("core")
    start = core * (ROWS * PAIRS // 2) + chip * part
    head = start // ROWS * 2 % (LANES // FEAT)
    feature = start % ROWS + iota((padded, LANES), 0)
    lane = iota((padded, LANES), 1)
    one = selector(feature, lane, False)
    two = selector(feature, lane, True)
    add_one, add_two = adders(feature[:, 0:1])
    extras = parts_ref[:, padded:, :].astype(jnp.float32).reshape(width, LANES)
    extras_low = extras.astype(BF16)
    upper = iota((width, LANES), 1) >= VHEAD
    lefts = []
    rights = []
    for place in range(2):
        mine = lane // FEAT == head + place
        first = dot(jnp.where(mine, one, 0.0).astype(BF16), extras_low, NT) + add_one
        second = dot(jnp.where(mine, two, 0.0).astype(BF16), extras_low, NT) + add_two
        lefts.append(pltpu.roll(first * second, width - EXTRA - (taps - 1), 1))
        rights.append(jnp.where(upper == (place == 1), extras, 0.0).astype(BF16))
    left = jnp.concatenate(lefts, axis=1)
    right = jnp.concatenate(rights, axis=0)
    column = iota(left.shape, 1) % width
    to_chip = jnp.where(column % EXTRA < taps - 1, column // EXTRA + 1, chips)

    def one_chip(chip, total):
        seen = jnp.where(to_chip <= chip, left, 0.0).astype(BF16)
        result = total + dot(seen, right)
        out_ref[chip] = result[:part].astype(BF16)
        return total + parts_ref[chip].astype(jnp.float32)[:padded]

    total = jnp.zeros((padded, LANES), jnp.float32)
    if chips <= 32:
        for chip in range(chips):
            total = one_chip(chip, total)
    else:
        lax.fori_loop(0, chips, one_chip, total)


def local_kernel(
    qk_ref, v_ref, conv_ref, swa_ref, tails_ref, other_qk_ref, other_v_ref,
    numer_ref, denom_ref, swa_out_ref,
):
    rows = v_ref.shape[0]
    taps = conv_ref.shape[0]
    width = HEADS * FEAT
    core = lax.axis_index("core")
    second = core == 1
    first_block = (lax.axis_index(CHIPS) == 0) & (core == 0)
    query = qk_ref[:, :width]
    key = qk_ref[:, width : 2 * width]
    lower = iota((rows, LANES), 1) < VHEAD
    causal = iota((rows, rows), 1) <= iota((rows, rows), 0)
    row_id = iota((rows, LANES), 0)
    ones = jnp.ones((rows, LANES), BF16)
    counted = jnp.where(second, ones, jnp.zeros_like(ones))
    more_key = jnp.where(second, other_qk_ref[:, width : 2 * width], key)
    all_keys = jnp.concatenate([key, more_key], axis=0)
    allowed = jnp.concatenate([causal, causal | True], axis=1)
    group_heads = 4
    for group in range(0, HEADS, group_heads):
        own = jnp.concatenate(
            [
                jnp.where(head_mask(head, query.shape), query, jnp.zeros_like(query))
                for head in range(group, group + group_heads)
            ],
            axis=0,
        )
        score = dot(own, all_keys, NT) * FEAT ** (-0.5)
        weight = 1.0 + score + 0.5 * score * score
        weight = jnp.where(jnp.concatenate([allowed] * group_heads, axis=0), weight, 0.0).astype(BF16)
        for at in range(group_heads // 2):
            pair = group // 2 + at
            lanes = slice(pair * LANES, (pair + 1) * LANES)
            tail = jnp.where(first_block, 0.0, tails_ref[WINDOW:, lanes].astype(jnp.float32))
            conved = convolved(v_ref[:, lanes].astype(jnp.float32), tail, conv_ref, lanes)
            before = convolved(other_v_ref[:, lanes].astype(jnp.float32), None, conv_ref, lanes)
            shares = jnp.zeros((rows, LANES), jnp.float32)
            for row in range(taps - 1):
                share = jnp.zeros((1, LANES), jnp.float32)
                for lag in range(row + 1, taps):
                    at_row = TAIL + row - lag
                    share = share + conv_ref[lag : lag + 1, lanes] * tail[at_row : at_row + 1]
                shares = jnp.where(row_id == row, -share, shares)
            before = jnp.where(second, before, shares.astype(BF16))
            right = jnp.concatenate([conved, ones], axis=1)
            right = jnp.concatenate([right, jnp.concatenate([before, counted], axis=1)], axis=0)
            result = dot(weight[2 * at * rows : (2 * at + 2) * rows], right)
            top, bottom = result[:rows], result[rows:]
            numer_ref[:, lanes] = jnp.where(lower, top[:, :LANES], bottom[:, :LANES])
            denom_ref[:, lanes] = jnp.where(lower, top[:, LANES:], bottom[:, LANES:])
    swa_width = SWA_HEADS * SWA_HEAD
    not_before = jnp.where(first_block, WINDOW, 0)
    span = 2 * WINDOW
    place = iota((WINDOW, span), 1)
    row = iota((WINDOW, span), 0)
    inside = (place > row) & (place <= row + WINDOW)
    inside_first = inside & (place >= not_before)
    for step in range(rows // WINDOW):
        mine = slice(step * WINDOW, (step + 1) * WINDOW)
        window = slice((step - 1) * WINDOW, (step + 1) * WINDOW)

        def around(head, start):
            here = slice(start + head * SWA_HEAD, start + (head + 1) * SWA_HEAD)
            if step:
                return swa_ref[window, here]
            there = slice(here.start - swa_width, here.stop - swa_width)
            return jnp.concatenate([tails_ref[:WINDOW, there], swa_ref[mine, here]], axis=0)

        scores = []
        for head in range(SWA_HEADS):
            own = swa_ref[mine, head * SWA_HEAD : (head + 1) * SWA_HEAD]
            score = dot(own, around(head, swa_width), NT) * SWA_HEAD ** (-0.5)
            scores.append(jnp.where(inside if step else inside_first, score, -jnp.inf))
        scores = jnp.concatenate(scores, axis=0)
        expo = jnp.exp(scores - jnp.max(scores, axis=-1, keepdims=True))
        probs = (expo / jnp.sum(expo, axis=-1, keepdims=True)).astype(BF16)
        for head in range(SWA_HEADS):
            own = probs[head * WINDOW : (head + 1) * WINDOW]
            swa_out_ref[mine, head * SWA_HEAD : (head + 1) * SWA_HEAD] = dot(
                own, around(head, 2 * swa_width)
            )


def readout_kernel(qk_ref, numer_ref, denom_ref, swa_ref, here_ref, there_ref, out_ref, past_ref):
    core = lax.axis_index("core")
    rows = out_ref.shape[0]
    half = PAIRS // 2 * ROWS
    past_ref[pl.ds(pl.multiple_of(core * half, half), half), :] = here_ref[...]
    past_ref[pl.ds(pl.multiple_of((1 - core) * half, half), half), :] = there_ref[...]
    lower = iota((rows, LANES), 1) < VHEAD
    query = qk_ref[:, : HEADS * FEAT]
    feature = iota((HEADS * FEAT, ROWS), 1)
    lane = iota((HEADS * FEAT, ROWS), 0)
    one = selector(feature, lane, False, halved=True).astype(BF16)
    two = selector(feature, lane, True).astype(BF16)
    add_one, add_two = adders(iota((8, ROWS), 1)[0:1])
    norms = []
    for pair in range(PAIRS):
        last = past_ref[(pair + 1) * ROWS - 16 : (pair + 1) * ROWS, :].astype(jnp.float32)
        for place in range(2):
            at = 16 - (ROWS - CONST) + 1 + 2 * place
            norm = jnp.concatenate([last[at : at + 1], last[at + 1 : at + 2, : ROWS - LANES]], axis=1)
            norms.append(jnp.broadcast_to(norm, (8, ROWS)))
    norms = jnp.concatenate(norms, axis=0).T.astype(BF16)
    source = iota((LANES, LANES), 0)
    target = iota((LANES, LANES), 1)
    group_heads = 8
    for group in range(0, HEADS, group_heads):
        own = jnp.concatenate(
            [
                jnp.where(head_mask(head, query.shape), query, jnp.zeros_like(query))
                for head in range(group, group + group_heads)
            ],
            axis=0,
        )
        high, low = hi_lo((dot(own, one) + add_one) * (dot(own, two) + add_two))
        for at in range(group_heads // 2):
            pair = group // 2 + at
            lanes = slice(pair * LANES, (pair + 1) * LANES)
            wanted = jnp.where(target < VHEAD, 16 * pair, 16 * pair + 8)
            spread = dot(norms, jnp.where(source == wanted, 1.0, 0.0).astype(BF16)).astype(BF16)
            right = jnp.concatenate([past_ref[pair * ROWS : (pair + 1) * ROWS, :], spread], axis=1)
            mine = slice(2 * at * rows, (2 * at + 2) * rows)
            result = dot(high[mine], right) + dot(low[mine], right)
            numer = jnp.where(lower, result[:rows, :LANES], result[rows:, :LANES]) + numer_ref[:, lanes]
            denom = jnp.where(lower, result[:rows, LANES:], result[rows:, LANES:]) + denom_ref[:, lanes]
            out_ref[:, lanes] = (numer / denom + swa_ref[:, lanes]).astype(out_ref.dtype)


IN_VMEM = pl.BlockSpec(memory_space=pltpu.VMEM)
IN_HBM = pl.BlockSpec(memory_space=pltpu.HBM)


def call(kernel, outs, args, specs, out_specs, scratch=(), grant=16):
    return pl.pallas_call(
        kernel,
        out_shape=outs,
        in_specs=specs,
        out_specs=out_specs,
        scratch_shapes=scratch,
        compiler_params=pltpu.CompilerParams(vmem_limit_bytes=grant * 1024 * 1024),
    )(*args)


def shards(lin_qk, lin_v, conv_w, swa_qkv):
    rows = lin_qk.shape[0]
    taps = conv_w.shape[0]
    chips = lax.axis_size("outer") * lax.axis_size("z")
    part = PAIRS // 2 * ROWS // chips
    held = (part + 7) // 8 * 8 + EXTRA
    shape = jax.ShapeDtypeStruct

    def swap(array):
        return lax.ppermute(array, "core", [(0, 1), (1, 0)])

    other_qk, other_v = swap(lin_qk), swap(lin_v)
    tokens = 2 * rows
    sums, tails = call(
        functools.partial(state_kernel, part),
        [
            shape((chips, held, LANES), BF16),
            shape((WINDOW + TAIL, swa_qkv.shape[1] // 3 * 2), BF16),
        ],
        [lin_qk, lin_v, other_qk, other_v, conv_w, swa_qkv],
        [IN_HBM] * 6,
        [IN_VMEM] * 2,
        [
            pltpu.VMEM((tokens, LANES), BF16),
            pltpu.VMEM((tokens, lin_v.shape[1] // 2), BF16),
            pltpu.VMEM((taps, lin_v.shape[1] // 2), jnp.float32),
            pltpu.SemaphoreType.DMA((7,)),
        ],
        grant=60,
    )
    sums, tails = lax.optimization_barrier((sums, tails))
    parts = lax.all_to_all(sums, CHIPS, 0, 0, tiled=True)
    tails = lax.ppermute(tails, SPLIT, [(i, i + 1) for i in range(2 * chips - 1)])
    past = call(
        functools.partial(prefix_kernel, taps),
        shape((chips, part, LANES), BF16),
        [parts],
        [IN_VMEM],
        IN_VMEM,
    )
    here = lax.all_to_all(past, CHIPS, 0, 0, tiled=True).reshape(chips * part, LANES)
    wide = shape(lin_v.shape, jnp.float32)
    numer, denom, swa = call(
        local_kernel,
        [wide, wide, wide],
        [lin_qk, lin_v, conv_w, swa_qkv, tails, other_qk, other_v],
        [IN_VMEM] * 7,
        [IN_VMEM] * 3,
    )
    here, numer, denom, swa = lax.optimization_barrier((here, numer, denom, swa))
    there = swap(here)
    return call(
        readout_kernel,
        shape(lin_v.shape, BF16),
        [lin_qk, numer, denom, swa, here, there],
        [IN_VMEM] * 6,
        IN_VMEM,
        [pltpu.VMEM((PAIRS * ROWS, LANES), BF16)],
    )


def solution(mesh):
    outer, inner = mesh.shape["ctxouter"], mesh.shape["ctxinner"]
    split = jax.sharding.Mesh(mesh.devices.reshape(outer, inner // 2, 2), SPLIT)
    return jax.shard_map(
        shards,
        mesh=split,
        in_specs=(P(SPLIT, None), P(SPLIT, None), P(), P(SPLIT, None)),
        out_specs=P(SPLIT, None),
        check_vma=False,
    )
```

time: 49.8 us -> 40.7 us (0.82)
  local copies, waits for them, and re-layouts: 10.9 us -> 2.31 us
  waiting for transfers between devices: 9.3 us -> 15.1 us
  Pallas kernels: 12.3 us -> 8.51 us
  starting transfers between devices: 16.6 us -> 14.3 us
    unnamed x30 -> x16, local copies, waits for them, and re-layouts: 9.95 us -> 2.31 us
    pallas_call x4, Pallas kernels: 12.3 us -> 8.51 us  [call(): pl.pallas_call(kernel, out_shape=outs, in_specs=specs, out_specs=out_spec...]
    all_to_all x2, waiting for transfers between devices: 8.46 us -> 12.2 us  [the longest x1 7.68 us: shards(): parts = lax.all_to_all(sums, CHIPS, 0, 0, tiled=True)]
    ppermute x2 -> x4, starting transfers between devices: 5.7 us -> 2.29 us  [the longest x1 1.78 us: shards(): lax.ppermute(tails, SPLIT, [(i, i + 1) for i in range(2 * chips - 1)])]
    ppermute x2 -> x4, waiting for transfers between devices: 0.84 us -> 2.9 us  [the longest x3 2.9 us: swap(): return lax.ppermute(array, 'core', [(0, 1), (1, 0)])]
    all_to_all x2, starting transfers between devices: 10.9 us -> 12 us  [the longest x1 8.38 us: shards(): parts = lax.all_to_all(sums, CHIPS, 0, 0, tiled=True)]
    slice x2 -> x0, local copies, waits for them, and re-layouts: 0.98 us -> none  [the longest x1 0.97 us: shards(): tail_kv = lax.ppermute(swa_qkv[rows - WINDOW:, swa_width:], AXES, shift)]
  transfers between devices with their start and end apart: 4 -> 6, of which waited for: 3 -> 4; matrix products, arithmetic and copies ran while one was open for 2% -> 0% of each run, Pallas kernels for 13% -> 8%
where the time goes in v4:
time: 40.7 us; the launch traced here: 40.4 us
  waiting for transfers between devices  15.1 us (37%)
  starting transfers between devices  14.3 us (35%)
  Pallas kernels  8.51 us (21%)
  local copies, waits for them, and re-layouts  2.31 us (6%)
    pallas_call x4, Pallas kernels, call(): pl.pallas_call(kernel, out_shape=outs, in_specs=specs, out_specs=out_spec...  8.51 us
    all_to_all x1, starting transfers between devices, shards(): parts = lax.all_to_all(sums, CHIPS, 0, 0, tiled=True)  8.38 us
    all_to_all x1, waiting for transfers between devices, shards(): parts = lax.all_to_all(sums, CHIPS, 0, 0, tiled=True)  7.68 us
    all_to_all x1, waiting for transfers between devices, shards(): lax.all_to_all(past, CHIPS, 0, 0, tiled=True).reshape(chips * part, LANES)  4.54 us
    all_to_all x1, starting transfers between devices, shards(): lax.all_to_all(past, CHIPS, 0, 0, tiled=True).reshape(chips * part, LANES)  3.65 us
    ppermute x3, waiting for transfers between devices, swap(): return lax.ppermute(array, 'core', [(0, 1), (1, 0)])  2.9 us
    unnamed x16, local copies, waits for them, and re-layouts  2.31 us
    ppermute x1, starting transfers between devices, shards(): lax.ppermute(tails, SPLIT, [(i, i + 1) for i in range(2 * chips - 1)])  1.78 us
  transfers between devices with their start and end apart: 6, of which 4 were waited for; matrix products, arithmetic and copies ran while one was open for 0% of the time, Pallas kernels for 8%

profile of v4, /device:TPU:0, one launch (start us, length us, event | category | flops | bytes accessed | tf_op | source)
XLA Modules:
  0.0 40.4 jit_solution(16683329633468757544)
XLA Ops:
  0.0 0.5 %collective-permute-start.1 = (bf16[128,1024]{1,0:T(8,128)(2,1)}, bf16[128,1024]{1,0:T(8,128)(2,1)S(1)}, u32[]{:S(2)}, u32[]{:S(2)}) collective-permute-start(bf16[128,1024]{1,0:T(8,128)(2,1)} %v_ref.1), channel_id=1, source_target_pairs={{0,1},{1,0},{2,3},{3,2},{4,5},{5,4},{6,7},{7,6},{8,9},{9,8},{10,11... | collective-permute-start | bytes 786440 | tf_op jit(solution)/shard_map/ppermute | solution.py:374
  0.5 0.1 collective-permute-start
  0.5 1.5 %collective-permute-done.other_qk_hbm.other_qk_ref = bf16[128,512]{1,0:T(8,128)(2,1)S(1)} collective-permute-done((bf16[128,512]{1,0:T(8,128)(2,1)}, bf16[128,512]{1,0:T(8,128)(2,1)S(1)}, u32[]{:S(2)}, u32[]{:S(2)}) %collective-permute-start) | collective-permute-done | bytes 131104 | tf_op jit(solution)/shard_map/ppermute | solution.py:374
  2.0 0.0 copy-start.5
  2.0 0.0 collective-permute-done.1.other_v_hbm.other_v_ref
  2.0 0.6 %copy-done.5 = bf16[128,512]{1,0:T(8,128)(2,1)} copy-done((bf16[128,512]{1,0:T(8,128)(2,1)}, bf16[128,512]{1,0:T(8,128)(2,1)S(1)}, u32[]{:S(2)}) %copy-start.5) | copy-done | bytes 131096
  2.7 0.0 copy-start.3
  2.7 0.7 %copy-done.3 = bf16[128,1024]{1,0:T(8,128)(2,1)} copy-done((bf16[128,1024]{1,0:T(8,128)(2,1)}, bf16[128,1024]{1,0:T(8,128)(2,1)S(1)}, u32[]{:S(2)}) %copy-start.3) | copy-done | bytes 262168
  3.4 0.0 copy-start.2
  3.4 2.6 %shard_map.46 = (bf16[16,48,128]{2,1,0:T(8,128)(2,1)}, bf16[80,2048]{1,0:T(8,128)(2,1)}) custom-call(bf16[128,512]{1,0:T(8,128)(2,1)} %qk_ref.3, bf16[128,1024]{1,0:T(8,128)(2,1)} %v_ref.1, bf16[128,512]{1,0:T(8,128)(2,1)} %copy-done.5, bf16[128,1024]{1,0:T(8,128)(2,1)} %copy-done.3, f32[3,1024]{1,0:T(4,128)} %conv_ref.1, bf16[128,3072]{1,0:T(8,128)(2,1)} %swa_ref.1), custom_call_target="tpu_custom_call" | custom-call | tf_op jit(solution)/shard_map/pallas_call | solution.py:355
  6.0 0.0 copy-start
  6.0 8.4 %all-to-all-start = ((bf16[16,48,128]{2,1,0:T(8,128)(2,1)}), bf16[16,48,128]{2,1,0:T(8,128)(2,1)S(1)}, u32[]{:S(2)}, u32[]{:S(2)}) async-start(bf16[16,48,128]{2,1,0:T(8,128)(2,1)} %get-tuple-element.14), calls=%async_computation | async-start | bytes 393216 | tf_op jit(solution)/shard_map/all_to_all | solution.py:396
  14.4 1.8 %collective-permute-start.2 = (bf16[80,2048]{1,0:T(8,128)(2,1)}, bf16[80,2048]{1,0:T(8,128)(2,1)S(1)}, u32[]{:S(2)}, u32[]{:S(2)}) collective-permute-start(bf16[80,2048]{1,0:T(8,128)(2,1)} %get-tuple-element.15), channel_id=1, source_target_pairs={{0,1},{1,2},{2,3},{3,4},{4,5},{5,6},{6,7},{7,8},{8,9},{9,10},{10,1... | collective-permute-start | bytes 983048 | tf_op jit(solution)/shard_map/ppermute | solution.py:397
  16.1 7.7 %all-to-all-done.parts_ref = bf16[16,48,128]{2,1,0:T(8,128)(2,1)S(1)} async-done(((bf16[16,48,128]{2,1,0:T(8,128)(2,1)}), bf16[16,48,128]{2,1,0:T(8,128)(2,1)S(1)}, u32[]{:S(2)}, u32[]{:S(2)}) %all-to-all-start) | async-done | bytes 196640 | tf_op jit(solution)/shard_map/all_to_all | solution.py:396
  23.8 1.2 %shard_map.47 = bf16[16,40,128]{2,1,0:T(8,128)(2,1)} custom-call(bf16[16,48,128]{2,1,0:T(8,128)(2,1)S(1)} %all-to-all-done.parts_ref), custom_call_target="tpu_custom_call" | custom-call | tf_op jit(solution)/shard_map/pallas_call | solution.py:355
  25.0 0.0 copy-start.1
  25.0 0.0 copy-start.6
  25.0 0.0 copy-start.7
  25.0 3.6 %all-to-all-start.1 = ((bf16[16,40,128]{2,1,0:T(8,128)(2,1)}), bf16[16,40,128]{2,1,0:T(8,128)(2,1)S(1)}, u32[]{:S(2)}, u32[]{:S(2)}) async-start(bf16[16,40,128]{2,1,0:T(8,128)(2,1)} %shard_map.47), calls=%async_computation.1 | async-start | bytes 327680 | tf_op jit(solution)/shard_map/all_to_all | solution.py:405
  28.7 0.0 collective-permute-done.2.tails_ref
  28.7 0.0 copy-done.2
  28.7 0.0 copy-done
  28.7 0.0 copy-done.1
  28.7 0.0 copy-done.6
  28.7 0.0 copy-done.7
  28.7 0.0 copy-start.4
  28.8 0.9 %copy-done.4 = bf16[128,1024]{1,0:T(8,128)(2,1)S(1)} copy-done((bf16[128,1024]{1,0:T(8,128)(2,1)S(1)}, bf16[128,1024]{1,0:T(8,128)(2,1)}, u32[]{:S(2)}) %copy-start.4) | copy-done | bytes 262168
  29.7 2.1 %shard_map.48 = (f32[128,1024]{1,0:T(8,128)S(1)}, f32[128,1024]{1,0:T(8,128)S(1)}, f32[128,1024]{1,0:T(8,128)S(1)}) custom-call(bf16[128,512]{1,0:T(8,128)(2,1)S(1)} %copy-done.1, bf16[128,1024]{1,0:T(8,128)(2,1)S(1)} %copy-done.2, f32[3,1024]{1,0:T(4,128)S(1)} %copy-done.7, bf16[128,3072]{1,0:T(8,128)(2,1)S(1)} %copy-done, ...), custom_call_target="tpu_custom_call" | custom-call | tf_op jit(solution)/shard_map/pallas_call | solution.py:355
  31.8 4.5 %all-to-all-done.1 = bf16[16,40,128]{2,1,0:T(8,128)(2,1)S(1)} async-done(((bf16[16,40,128]{2,1,0:T(8,128)(2,1)}), bf16[16,40,128]{2,1,0:T(8,128)(2,1)S(1)}, u32[]{:S(2)}, u32[]{:S(2)}) %all-to-all-start.1) | async-done | bytes 163872 | tf_op jit(solution)/shard_map/all_to_all | solution.py:405
  36.4 0.0 collective-permute-start.3
  36.4 1.4 %collective-permute-done.3.there_ref = bf16[640,128]{1,0:T(8,128)(2,1)S(1)} collective-permute-done((bf16[640,128]{1,0:T(8,128)(2,1)S(1)}, bf16[640,128]{1,0:T(8,128)(2,1)S(1)}, u32[]{:S(2)}, u32[]{:S(2)}) %collective-permute-start.3) | collective-permute-done | bytes 163872 | tf_op jit(solution)/shard_map/ppermute | solution.py:374
  37.8 2.6 %shard_map.49 = bf16[128,1024]{1,0:T(8,128)(2,1)} custom-call(bf16[128,512]{1,0:T(8,128)(2,1)S(1)} %copy-done.1, f32[128,1024]{1,0:T(8,128)S(1)} %get-tuple-element.19.numer_ref, f32[128,1024]{1,0:T(8,128)S(1)} %get-tuple-element.20.denom_ref, f32[128,1024]{1,0:T(8,128)S(1)} %get-tuple-element.21.swa_ref, bf16[640,128]{1,0:T(8,128)(2,1)S(1)} %bitcast.2, ...), custom_call_target="tpu_custom_call" | custom-call | tf_op jit(solution)/shard_map/pallas_call | solution.py:355
Async XLA Ops:
  0.0 2.0 %collective-permute-start.1 = (bf16[128,1024]{1,0:T(8,128)(2,1)}, bf16[128,1024]{1,0:T(8,128)(2,1)S(1)}, u32[]{:S(2)}, u32[]{:S(2)}) collective-permute-start(bf16[128,1024]{1,0:T(8,128)(2,1)} %v_ref.1), channel_id=1, source_target_pairs={{0,1},{1,0},{2,3},{3,2},{4,5},{5,4},{6,7},{7,6},{8,9},{9,8},{10,11... | collective-permute-start | bytes 786440 | tf_op jit(solution)/shard_map/ppermute | solution.py:374
  0.5 1.6 %collective-permute-start = (bf16[128,512]{1,0:T(8,128)(2,1)}, bf16[128,512]{1,0:T(8,128)(2,1)S(1)}, u32[]{:S(2)}, u32[]{:S(2)}) collective-permute-start(bf16[128,512]{1,0:T(8,128)(2,1)} %qk_ref.3), channel_id=1, source_target_pairs={{0,1},{1,0},{2,3},{3,2},{4,5},{5,4},{6,7},{7,6},{8,9},{9,8},{10,11... | collective-permute-start | bytes 393224 | tf_op jit(solution)/shard_map/ppermute | solution.py:374
  2.0 0.7 %copy-start.5 = (bf16[128,512]{1,0:T(8,128)(2,1)}, bf16[128,512]{1,0:T(8,128)(2,1)S(1)}, u32[]{:S(2)}) copy-start(bf16[128,512]{1,0:T(8,128)(2,1)S(1)} %collective-permute-done.other_qk_hbm.other_qk_ref) | copy-start | bytes 393220
  2.7 0.7 %copy-start.3 = (bf16[128,1024]{1,0:T(8,128)(2,1)}, bf16[128,1024]{1,0:T(8,128)(2,1)S(1)}, u32[]{:S(2)}) copy-start(bf16[128,1024]{1,0:T(8,128)(2,1)S(1)} %collective-permute-done.1.other_v_hbm.other_v_ref) | copy-start | bytes 786436
  3.4 25.3 %copy-start.2 = (bf16[128,1024]{1,0:T(8,128)(2,1)S(1)}, bf16[128,1024]{1,0:T(8,128)(2,1)}, u32[]{:S(2)}) copy-start(bf16[128,1024]{1,0:T(8,128)(2,1)} %v_ref.1) | copy-start | bytes 786436
  6.0 22.7 %copy-start = (bf16[128,3072]{1,0:T(8,128)(2,1)S(1)}, bf16[128,3072]{1,0:T(8,128)(2,1)}, u32[]{:S(2)}) copy-start(bf16[128,3072]{1,0:T(8,128)(2,1)} %swa_ref.1) | copy-start | bytes 2359300
  6.0 17.9 %all-to-all-start = ((bf16[16,48,128]{2,1,0:T(8,128)(2,1)}), bf16[16,48,128]{2,1,0:T(8,128)(2,1)S(1)}, u32[]{:S(2)}, u32[]{:S(2)}) async-start(bf16[16,48,128]{2,1,0:T(8,128)(2,1)} %get-tuple-element.14), calls=%async_computation | async-start | bytes 393216 | tf_op jit(solution)/shard_map/all_to_all | solution.py:396
  14.4 14.3 %collective-permute-start.2 = (bf16[80,2048]{1,0:T(8,128)(2,1)}, bf16[80,2048]{1,0:T(8,128)(2,1)S(1)}, u32[]{:S(2)}, u32[]{:S(2)}) collective-permute-start(bf16[80,2048]{1,0:T(8,128)(2,1)} %get-tuple-element.15), channel_id=1, source_target_pairs={{0,1},{1,2},{2,3},{3,4},{4,5},{5,6},{6,7},{7,8},{8,9},{9,10},{10,1... | collective-permute-start | bytes 983048 | tf_op jit(solution)/shard_map/ppermute | solution.py:397
  25.0 3.7 %copy-start.1 = (bf16[128,512]{1,0:T(8,128)(2,1)S(1)}, bf16[128,512]{1,0:T(8,128)(2,1)}, u32[]{:S(2)}) copy-start(bf16[128,512]{1,0:T(8,128)(2,1)} %qk_ref.3) | copy-start | bytes 393220
  25.0 3.7 %copy-start.6 = (bf16[128,512]{1,0:T(8,128)(2,1)S(1)}, bf16[128,512]{1,0:T(8,128)(2,1)}, u32[]{:S(2)}) copy-start(bf16[128,512]{1,0:T(8,128)(2,1)} %copy-done.5) | copy-start | bytes 393220
  25.0 3.7 %copy-start.7 = (f32[3,1024]{1,0:T(4,128)S(1)}, f32[3,1024]{1,0:T(4,128)}, u32[]{:S(2)}) copy-start(f32[3,1024]{1,0:T(4,128)} %conv_ref.1) | copy-start | bytes 36868
  25.0 11.3 %all-to-all-start.1 = ((bf16[16,40,128]{2,1,0:T(8,128)(2,1)}), bf16[16,40,128]{2,1,0:T(8,128)(2,1)S(1)}, u32[]{:S(2)}, u32[]{:S(2)}) async-start(bf16[16,40,128]{2,1,0:T(8,128)(2,1)} %shard_map.47), calls=%async_computation.1 | async-start | bytes 327680 | tf_op jit(solution)/shard_map/all_to_all | solution.py:405
  28.7 1.0 %copy-start.4 = (bf16[128,1024]{1,0:T(8,128)(2,1)S(1)}, bf16[128,1024]{1,0:T(8,128)(2,1)}, u32[]{:S(2)}) copy-start(bf16[128,1024]{1,0:T(8,128)(2,1)} %copy-done.3) | copy-start | bytes 786436
  36.4 1.4 %collective-permute-start.3 = (bf16[640,128]{1,0:T(8,128)(2,1)S(1)}, bf16[640,128]{1,0:T(8,128)(2,1)S(1)}, u32[]{:S(2)}, u32[]{:S(2)}) collective-permute-start(bf16[640,128]{1,0:T(8,128)(2,1)S(1)} %bitcast.1), channel_id=1, source_target_pairs={{0,1},{1,0},{2,3},{3,2},{4,5},{5,4},{6,7},{7,6},{8,9},{9,8},{10,11... | collective-permute-start | bytes 491528 | tf_op jit(solution)/shard_map/ppermute | solution.py:374

commit v5 on v4

--- a/solution.py
+++ b/solution.py
@@ -25,6 +25,7 @@
 ROWS = 160
 TAIL = 16
 EXTRA = 8
+BLOCK_EXTRA = 4
 
 
 NT = (((1,), (1,)), ((), ()))
@@ -82,38 +83,38 @@
     return result.astype(BF16)
 
 
-def state_kernel(
-    part, qk_hbm, v_hbm, other_qk_hbm, other_v_hbm, conv_hbm, swa_hbm, out_ref, tails_ref,
-    key_ref, v_ref, conv_ref, sems,
-):
-    rows, wide = v_hbm.shape
+def state_kernel(part, own, *refs):
+    core = lax.axis_index("core")
+    if own:
+        qk_hbm, v_hbm, conv_hbm, swa_hbm, out_ref, tails_ref, conv_ref, key_ref, v_ref, sems = refs
+        rows, wide = v_hbm.shape
+    else:
+        qk_ref, v_ref, conv_ref, own_ref, out_ref = refs
+        rows, wide = v_ref.shape
     taps = conv_ref.shape[0]
-    core = lax.axis_index("core")
     mine = pl.ds(pl.multiple_of(core * (wide // 2), wide // 2), wide // 2)
     keys = pl.ds(pl.multiple_of(HEADS * FEAT + core * LANES, LANES), LANES)
-    here = pl.ds(pl.multiple_of(core * rows, rows), rows)
-    there = pl.ds(pl.multiple_of((1 - core) * rows, rows), rows)
-    copies = [
-        pltpu.make_async_copy(qk_hbm.at[:, keys], key_ref.at[here, :], sems.at[0]),
-        pltpu.make_async_copy(other_qk_hbm.at[:, keys], key_ref.at[there, :], sems.at[1]),
-        pltpu.make_async_copy(conv_hbm.at[:, mine], conv_ref, sems.at[2]),
-        pltpu.make_async_copy(v_hbm.at[:, mine], v_ref.at[here, :], sems.at[3]),
-        pltpu.make_async_copy(other_v_hbm.at[:, mine], v_ref.at[there, :], sems.at[4]),
-        pltpu.make_async_copy(
-            swa_hbm.at[rows - WINDOW :, tails_ref.shape[1] // 2 :], tails_ref.at[:WINDOW, :], sems.at[5]
-        ),
-        pltpu.make_async_copy(v_hbm.at[rows - TAIL :, :], tails_ref.at[WINDOW:, :wide], sems.at[6]),
-    ]
-    for copy in copies:
-        copy.start()
-    for copy in copies[:2]:
-        copy.wait()
-    tokens = 2 * rows
-    key_t = (key_ref[...].astype(jnp.float32) * FEAT ** (-0.25)).T
-    const_rows = jnp.where(iota((EXTRA, tokens), 0) == 0, 1.0, 0.0)
+    if own:
+        pieces = [
+            (qk_hbm.at[:, keys], key_ref),
+            (conv_hbm.at[:, mine], conv_ref),
+            (v_hbm.at[:, mine], v_ref),
+            (swa_hbm.at[rows - WINDOW :, tails_ref.shape[1] // 2 :], tails_ref.at[:WINDOW, :]),
+            (v_hbm.at[rows - TAIL :, :], tails_ref.at[WINDOW:, :wide]),
+        ]
+        copies = [pltpu.make_async_copy(a, b, sems.at[i]) for i, (a, b) in enumerate(pieces)]
+        for copy in copies:
+            copy.start()
+        copies[0].wait()
+        key = key_ref[...]
+    else:
+        copies = []
+        key = qk_ref[:, keys]
+    key_t = (key.astype(jnp.float32) * FEAT ** (-0.25)).T
+    const_rows = jnp.where(iota((EXTRA, rows), 0) == 0, 1.0, 0.0)
     lane_id = iota((ROWS, LANES), 1)
     low_row = iota((EXTRA, LANES), 0)
-    ones = jnp.ones((tokens, LANES), BF16)
+    ones = jnp.ones((rows, LANES), BF16)
     half = FEAT // 2
     padded = (part + 7) // 8 * 8
     lefts = []
@@ -124,15 +125,17 @@
             blocks.append(x * jnp.concatenate([x[by:], x[:by]], axis=0))
         blocks += [x[:half] * x[half:], x, const_rows]
         lefts.append(jnp.concatenate(hi_lo(jnp.concatenate(blocks, axis=0)), axis=1))
-    first_keys = key_ref[0:16].astype(jnp.float32)
-    for copy in copies[2:5]:
+    first_keys = key[:16].astype(jnp.float32)
+    slot = low_row - BLOCK_EXTRA * (core if own else 1 - core)
+    for copy in copies[1:3]:
         copy.wait()
     states = []
     extras = []
     norms = jnp.zeros((ROWS, LANES), jnp.float32)
     for pair in range(PAIRS // 2):
         lanes = slice(pair * LANES, (pair + 1) * LANES)
-        value = v_ref[:, lanes].astype(jnp.float32)
+        at = pl.multiple_of((0 if own else core * (wide // 2)) + pair * LANES, LANES)
+        value = v_ref[:, pl.ds(at, LANES)].astype(jnp.float32)
         conved = convolved(value, None, conv_ref, lanes)
         right = jnp.concatenate([conved, ones], axis=1)
         right = jnp.concatenate([right, right], axis=0)
@@ -146,10 +149,10 @@
         for row in range(taps - 1):
             share = jnp.zeros((1, LANES), jnp.float32)
             for lag in range(row + 1, taps):
-                at = tokens + row - lag
-                share = share + conv_ref[lag : lag + 1, lanes] * value[at : at + 1]
-            extra = jnp.where(low_row == row, share, extra)
-            extra = jnp.where(low_row == taps - 1 + row, first_keys[row : row + 1], extra)
+                last = rows + row - lag
+                share = share + conv_ref[lag : lag + 1, lanes] * value[last : last + 1]
+            extra = jnp.where(slot == row, share, extra)
+            extra = jnp.where(slot == taps - 1 + row, first_keys[row : row + 1], extra)
         extras.append(extra)
     norms_t = norms.T
     for pair in range(PAIRS // 2):
@@ -168,8 +171,12 @@
             if padded != part:
                 rows_of.append(jnp.zeros((padded - part, LANES), jnp.float32))
             message = jnp.concatenate(rows_of + [extras[pair]], axis=0)
-            out_ref[pair * (ROWS // part) + piece] = message.astype(BF16)
-    for copy in copies[5:]:
+            chunk = pair * (ROWS // part) + piece
+            if own:
+                out_ref[chunk] = message
+            else:
+                out_ref[chunk] = (own_ref[chunk] + message).astype(BF16)
+    for copy in copies[3:]:
         copy.wait()
 
 
@@ -195,15 +202,15 @@
         mine = lane // FEAT == head + place
         first = dot(jnp.where(mine, one, 0.0).astype(BF16), extras_low, NT) + add_one
         second = dot(jnp.where(mine, two, 0.0).astype(BF16), extras_low, NT) + add_two
-        lefts.append(pltpu.roll(first * second, width - EXTRA - (taps - 1), 1))
+        lefts.append(pltpu.roll(first * second, width - BLOCK_EXTRA - (taps - 1), 1))
         rights.append(jnp.where(upper == (place == 1), extras, 0.0).astype(BF16))
     left = jnp.concatenate(lefts, axis=1)
     right = jnp.concatenate(rights, axis=0)
     column = iota(left.shape, 1) % width
-    to_chip = jnp.where(column % EXTRA < taps - 1, column // EXTRA + 1, chips)
+    to_block = jnp.where(column % BLOCK_EXTRA < taps - 1, column // BLOCK_EXTRA + 1, 2 * chips)
 
     def one_chip(chip, total):
-        seen = jnp.where(to_chip <= chip, left, 0.0).astype(BF16)
+        seen = jnp.where(to_block <= 2 * chip, left, 0.0).astype(BF16)
         result = total + dot(seen, right)
         out_ref[chip] = result[:part].astype(BF16)
         return total + parts_ref[chip].astype(jnp.float32)[:padded]
@@ -301,65 +308,75 @@
             )
 
 
-def readout_kernel(qk_ref, numer_ref, denom_ref, swa_ref, here_ref, there_ref, out_ref, past_ref):
+def readout_kernel(own, qk_ref, numer_ref, denom_ref, swa_ref, past_ref, *refs):
     core = lax.axis_index("core")
-    rows = out_ref.shape[0]
-    half = PAIRS // 2 * ROWS
-    past_ref[pl.ds(pl.multiple_of(core * half, half), half), :] = here_ref[...]
-    past_ref[pl.ds(pl.multiple_of((1 - core) * half, half), half), :] = there_ref[...]
+    half = core if own else 1 - core
+    rows = qk_ref.shape[0]
+    wide = PAIRS // 2 * LANES
+    copies = []
+    if own:
+        (out_ref,) = refs
+    else:
+        own_ref, out_hbm, out_ref, sems = refs
+        there = pl.ds(pl.multiple_of(core * wide, wide), wide)
+        copies.append(pltpu.make_async_copy(own_ref, out_hbm.at[:, there], sems.at[PAIRS // 2]))
+        copies[0].start()
     lower = iota((rows, LANES), 1) < VHEAD
-    query = qk_ref[:, : HEADS * FEAT]
-    feature = iota((HEADS * FEAT, ROWS), 1)
-    lane = iota((HEADS * FEAT, ROWS), 0)
+    query = qk_ref[:, pl.ds(pl.multiple_of(half * LANES, LANES), LANES)]
+    feature = iota((LANES, ROWS), 1)
+    lane = iota((LANES, ROWS), 0)
     one = selector(feature, lane, False, halved=True).astype(BF16)
     two = selector(feature, lane, True).astype(BF16)
     add_one, add_two = adders(iota((8, ROWS), 1)[0:1])
     norms = []
-    for pair in range(PAIRS):
+    for pair in range(PAIRS // 2):
         last = past_ref[(pair + 1) * ROWS - 16 : (pair + 1) * ROWS, :].astype(jnp.float32)
         for place in range(2):
             at = 16 - (ROWS - CONST) + 1 + 2 * place
             norm = jnp.concatenate([last[at : at + 1], last[at + 1 : at + 2, : ROWS - LANES]], axis=1)
             norms.append(jnp.broadcast_to(norm, (8, ROWS)))
-    norms = jnp.concatenate(norms, axis=0).T.astype(BF16)
+    norms = jnp.concatenate(norms + [jnp.zeros((LANES // 2, ROWS), jnp.float32)], axis=0).T.astype(BF16)
     source = iota((LANES, LANES), 0)
     target = iota((LANES, LANES), 1)
-    group_heads = 8
-    for group in range(0, HEADS, group_heads):
-        own = jnp.concatenate(
-            [
-                jnp.where(head_mask(head, query.shape), query, jnp.zeros_like(query))
-                for head in range(group, group + group_heads)
-            ],
-            axis=0,
-        )
-        high, low = hi_lo((dot(own, one) + add_one) * (dot(own, two) + add_two))
-        for at in range(group_heads // 2):
-            pair = group // 2 + at
-            lanes = slice(pair * LANES, (pair + 1) * LANES)
-            wanted = jnp.where(target < VHEAD, 16 * pair, 16 * pair + 8)
-            spread = dot(norms, jnp.where(source == wanted, 1.0, 0.0).astype(BF16)).astype(BF16)
-            right = jnp.concatenate([past_ref[pair * ROWS : (pair + 1) * ROWS, :], spread], axis=1)
-            mine = slice(2 * at * rows, (2 * at + 2) * rows)
-            result = dot(high[mine], right) + dot(low[mine], right)
-            numer = jnp.where(lower, result[:rows, :LANES], result[rows:, :LANES]) + numer_ref[:, lanes]
-            denom = jnp.where(lower, result[:rows, LANES:], result[rows:, LANES:]) + denom_ref[:, lanes]
-            out_ref[:, lanes] = (numer / denom + swa_ref[:, lanes]).astype(out_ref.dtype)
+    own_heads = [
+        jnp.where(head_mask(head, query.shape), query, jnp.zeros_like(query)) for head in range(HEADS // 2)
+    ]
+    stacked = jnp.concatenate(own_heads, axis=0)
+    high, low = hi_lo((dot(stacked, one) + add_one) * (dot(stacked, two) + add_two))
+    for pair in range(PAIRS // 2):
+        here = pl.ds(pl.multiple_of(half * wide + pair * LANES, LANES), LANES)
+        wanted = jnp.where(target < VHEAD, 16 * pair, 16 * pair + 8)
+        spread = dot(norms, jnp.where(source == wanted, 1.0, 0.0).astype(BF16)).astype(BF16)
+        right = jnp.concatenate([past_ref[pair * ROWS : (pair + 1) * ROWS, :], spread], axis=1)
+        mine = slice(2 * pair * rows, (2 * pair + 2) * rows)
+        result = dot(high[mine], right) + dot(low[mine], right)
+        numer = jnp.where(lower, result[:rows, :LANES], result[rows:, :LANES]) + numer_ref[:, here]
+        denom = jnp.where(lower, result[:rows, LANES:], result[rows:, LANES:]) + denom_ref[:, here]
+        mixed = (numer / denom + swa_ref[:, here]).astype(BF16)
+        out_ref[:, pair * LANES : (pair + 1) * LANES] = mixed
+        if not own:
+            done = out_ref.at[:, pair * LANES : (pair + 1) * LANES]
+            copies.append(pltpu.make_async_copy(done, out_hbm.at[:, here], sems.at[pair]))
+            copies[-1].start()
+    for copy in copies:
+        copy.wait()
 
 
 IN_VMEM = pl.BlockSpec(memory_space=pltpu.VMEM)
 IN_HBM = pl.BlockSpec(memory_space=pltpu.HBM)
 
 
-def call(kernel, outs, args, specs, out_specs, scratch=(), grant=16):
+def call(kernel, outs, args, specs, out_specs, scratch=()):
+    placed = [pltpu.with_memory_space_constraint(a, spec.memory_space) for a, spec in zip(args, specs)]
+    results = jax.tree.map(lambda out, spec: spec.memory_space(out.shape, out.dtype), outs, out_specs)
     return pl.pallas_call(
         kernel,
-        out_shape=outs,
+        out_shape=results,
         in_specs=specs,
         out_specs=out_specs,
         scratch_shapes=scratch,
-        compiler_params=pltpu.CompilerParams(vmem_limit_bytes=grant * 1024 * 1024),
-    )(*args)
+        compiler_params=pltpu.CompilerParams(vmem_limit_bytes=16 * 1024 * 1024),
+    )(*placed)
 
 
 def shards(lin_qk, lin_v, conv_w, swa_qkv):
@@ -374,23 +391,29 @@
         return lax.ppermute(array, "core", [(0, 1), (1, 0)])
 
     other_qk, other_v = swap(lin_qk), swap(lin_v)
-    tokens = 2 * rows
-    sums, tails = call(
-        functools.partial(state_kernel, part),
+    half_wide = lin_v.shape[1] // 2
+    own_sums, tails, conv_half = call(
+        functools.partial(state_kernel, part, True),
         [
-            shape((chips, held, LANES), BF16),
+            shape((chips, held, LANES), jnp.float32),
             shape((WINDOW + TAIL, swa_qkv.shape[1] // 3 * 2), BF16),
+            shape((taps, half_wide), jnp.float32),
         ],
-        [lin_qk, lin_v, other_qk, other_v, conv_w, swa_qkv],
-        [IN_HBM] * 6,
-        [IN_VMEM] * 2,
+        [lin_qk, lin_v, conv_w, swa_qkv],
+        [IN_HBM] * 4,
+        [IN_VMEM] * 3,
         [
-            pltpu.VMEM((tokens, LANES), BF16),
-            pltpu.VMEM((tokens, lin_v.shape[1] // 2), BF16),
-            pltpu.VMEM((taps, lin_v.shape[1] // 2), jnp.float32),
-            pltpu.SemaphoreType.DMA((7,)),
+            pltpu.VMEM((rows, LANES), BF16),
+            pltpu.VMEM((rows, half_wide), BF16),
+            pltpu.SemaphoreType.DMA((5,)),
         ],
-        grant=60,
+    )
+    sums = call(
+        functools.partial(state_kernel, part, False),
+        shape((chips, held, LANES), BF16),
+        [other_qk, other_v, conv_half, own_sums],
+        [IN_VMEM] * 4,
+        IN_VMEM,
     )
     sums, tails = lax.optimization_barrier((sums, tails))
     parts = lax.all_to_all(sums, CHIPS, 0, 0, tiled=True)
@@ -413,13 +436,20 @@
     )
     here, numer, denom, swa = lax.optimization_barrier((here, numer, denom, swa))
     there = swap(here)
+    own_out = call(
+        functools.partial(readout_kernel, True),
+        shape((rows, half_wide), BF16),
+        [lin_qk, numer, denom, swa, here],
+        [IN_VMEM] * 5,
+        IN_VMEM,
+    )
     return call(
-        readout_kernel,
+        functools.partial(readout_kernel, False),
         shape(lin_v.shape, BF16),
-        [lin_qk, numer, denom, swa, here, there],
+        [lin_qk, numer, denom, swa, there, own_out],
         [IN_VMEM] * 6,
-        IN_VMEM,
-        [pltpu.VMEM((PAIRS * ROWS, LANES), BF16)],
+        IN_HBM,
+        [pltpu.VMEM((rows, half_wide), BF16), pltpu.SemaphoreType.DMA((PAIRS // 2 + 1,))],
     )
 
 

time: 40.7 us -> 37 us (0.909)
  waiting for transfers between devices: 15.1 us -> 12 us
  local copies, waits for them, and re-layouts: 2.31 us -> 1.69 us
    ppermute x3, waiting for transfers between devices: 2.9 us -> 0.46 us  [swap(): return lax.ppermute(array, 'core', [(0, 1), (1, 0)])]
    all_to_all x1, waiting for transfers between devices: 4.54 us -> 3.84 us  [shards(): lax.all_to_all(past, CHIPS, 0, 0, tiled=True).reshape(chips * part, LANES)]
    unnamed x16 -> x12, local copies, waits for them, and re-layouts: 2.31 us -> 1.69 us
    pallas_call x4 -> x6, Pallas kernels: 8.51 us -> 8.58 us  [call(): pl.pallas_call(kernel, out_shape=results, in_specs=specs, out_specs=out_s...]
  transfers between devices with their start and end apart: 6 -> 6, of which waited for: 4 -> 4; matrix products, arithmetic and copies ran while one was open for 0% -> 0% of each run, Pallas kernels for 8% -> 16%
where the time goes in v5:
time: 37 us; the launch traced here: 36.6 us
  starting transfers between devices  14.3 us (39%)
  waiting for transfers between devices  12 us (32%)
  Pallas kernels  8.58 us (23%)
  local copies, waits for them, and re-layouts  1.69 us (5%)
    pallas_call x6, Pallas kernels, call(): pl.pallas_call(kernel, out_shape=results, in_specs=specs, out_specs=out_s...  8.58 us
    all_to_all x1, starting transfers between devices, shards(): parts = lax.all_to_all(sums, CHIPS, 0, 0, tiled=True)  8.4 us
    all_to_all x1, waiting for transfers between devices, shards(): parts = lax.all_to_all(sums, CHIPS, 0, 0, tiled=True)  7.68 us
    all_to_all x1, waiting for transfers between devices, shards(): lax.all_to_all(past, CHIPS, 0, 0, tiled=True).reshape(chips * part, LANES)  3.84 us
    all_to_all x1, starting transfers between devices, shards(): lax.all_to_all(past, CHIPS, 0, 0, tiled=True).reshape(chips * part, LANES)  3.65 us
    ppermute x1, starting transfers between devices, shards(): lax.ppermute(tails, SPLIT, [(i, i + 1) for i in range(2 * chips - 1)])  1.74 us
    unnamed x12, local copies, waits for them, and re-layouts  1.69 us
  transfers between devices with their start and end apart: 6, of which 4 were waited for; matrix products, arithmetic and copies ran while one was open for 0% of the time, Pallas kernels for 16%

profile of v5, /device:TPU:0, one launch (start us, length us, event | category | flops | bytes accessed | tf_op | source)
XLA Modules:
  0.0 36.6 jit_solution(13989742010080412631)
XLA Ops:
  0.0 0.5 %collective-permute-start.1 = (bf16[128,1024]{1,0:T(8,128)(2,1)}, bf16[128,1024]{1,0:T(8,128)(2,1)S(1)}, u32[]{:S(2)}, u32[]{:S(2)}) collective-permute-start(bf16[128,1024]{1,0:T(8,128)(2,1)} %v_ref.1), channel_id=1, source_target_pairs={{0,1},{1,0},{2,3},{3,2},{4,5},{5,4},{6,7},{7,6},{8,9},{9,8},{10,11... | collective-permute-start | bytes 786440 | tf_op jit(solution)/shard_map/ppermute | solution.py:391
  0.5 0.1 collective-permute-start
  0.5 1.4 %shard_map.46 = (f32[16,48,128]{2,1,0:T(8,128)S(1)}, bf16[80,2048]{1,0:T(8,128)(2,1)S(1)}, f32[3,512]{1,0:T(4,128)S(1)}) custom-call(bf16[128,512]{1,0:T(8,128)(2,1)} %qk_ref.5, bf16[128,1024]{1,0:T(8,128)(2,1)} %v_ref.1, f32[3,1024]{1,0:T(4,128)} %conv_ref.1, bf16[128,3072]{1,0:T(8,128)(2,1)} %swa_ref.1), custom_call_target="tpu_custom_call" | custom-call | tf_op jit(solution)/shard_map/pallas_call | solution.py:372
  1.9 0.1 collective-permute-done.refs_0_.other_qk_ref
  2.0 0.0 collective-permute-done.1.refs_1_.other_v_ref
  2.0 0.0 copy-start.2
  2.0 1.2 %shard_map.47 = bf16[16,48,128]{2,1,0:T(8,128)(2,1)} custom-call(bf16[128,512]{1,0:T(8,128)(2,1)S(1)} %collective-permute-done.refs_0_.other_qk_ref, bf16[128,1024]{1,0:T(8,128)(2,1)S(1)} %collective-permute-done.1.refs_1_.other_v_ref, f32[3,512]{1,0:T(4,128)S(1)} %get-tuple-element.17.refs_2_, f32[16,48,128]{2,1,0:T(8,128)S(1)} %get-tuple-element.18.refs_3_), custom_call_target="tpu_custom_call" | custom-call | tf_op jit(solution)/shard_map/pallas_call | solution.py:372
  3.2 0.0 copy-start
  3.2 8.4 %all-to-all-start = ((bf16[16,48,128]{2,1,0:T(8,128)(2,1)}), bf16[16,48,128]{2,1,0:T(8,128)(2,1)S(1)}, u32[]{:S(2)}, u32[]{:S(2)}) async-start(bf16[16,48,128]{2,1,0:T(8,128)(2,1)} %shard_map.47), calls=%async_computation | async-start | bytes 393216 | tf_op jit(solution)/shard_map/all_to_all | solution.py:419
  11.6 1.7 %collective-permute-start.2 = (bf16[80,2048]{1,0:T(8,128)(2,1)S(1)}, bf16[80,2048]{1,0:T(8,128)(2,1)S(1)}, u32[]{:S(2)}, u32[]{:S(2)}) collective-permute-start(bf16[80,2048]{1,0:T(8,128)(2,1)S(1)} %get-tuple-element.21), channel_id=1, source_target_pairs={{0,1},{1,2},{2,3},{3,4},{4,5},{5,6},{6,7},{7,8},{8,9},{9,10},{10,1... | collective-permute-start | bytes 983048 | tf_op jit(solution)/shard_map/ppermute | solution.py:420
  13.3 7.7 %all-to-all-done.parts_ref = bf16[16,48,128]{2,1,0:T(8,128)(2,1)S(1)} async-done(((bf16[16,48,128]{2,1,0:T(8,128)(2,1)}), bf16[16,48,128]{2,1,0:T(8,128)(2,1)S(1)}, u32[]{:S(2)}, u32[]{:S(2)}) %all-to-all-start) | async-done | bytes 196640 | tf_op jit(solution)/shard_map/all_to_all | solution.py:419
  21.0 1.2 %shard_map.48 = bf16[16,40,128]{2,1,0:T(8,128)(2,1)} custom-call(bf16[16,48,128]{2,1,0:T(8,128)(2,1)S(1)} %all-to-all-done.parts_ref), custom_call_target="tpu_custom_call" | custom-call | tf_op jit(solution)/shard_map/pallas_call | solution.py:372
  22.2 0.0 copy-start.1
  22.2 0.0 copy-start.5
  22.2 3.6 %all-to-all-start.1 = ((bf16[16,40,128]{2,1,0:T(8,128)(2,1)}), bf16[16,40,128]{2,1,0:T(8,128)(2,1)S(1)}, u32[]{:S(2)}, u32[]{:S(2)}) async-start(bf16[16,40,128]{2,1,0:T(8,128)(2,1)} %shard_map.48), calls=%async_computation.1 | async-start | bytes 327680 | tf_op jit(solution)/shard_map/all_to_all | solution.py:428
  25.9 0.0 collective-permute-done.2.tails_ref
  25.9 0.0 copy-start.3
  25.9 0.7 %copy-done.3 = bf16[80,2048]{1,0:T(8,128)(2,1)} copy-done((bf16[80,2048]{1,0:T(8,128)(2,1)}, bf16[80,2048]{1,0:T(8,128)(2,1)S(1)}, u32[]{:S(2)}) %copy-start.3) | copy-done | bytes 327704
  26.6 0.0 copy-done.2
  26.6 0.0 copy-done
  26.6 0.0 copy-done.1
  26.6 0.0 copy-done.5
  26.6 0.0 copy-start.4
  26.6 1.0 %copy-done.4 = bf16[80,2048]{1,0:T(8,128)(2,1)S(1)} copy-done((bf16[80,2048]{1,0:T(8,128)(2,1)S(1)}, bf16[80,2048]{1,0:T(8,128)(2,1)}, u32[]{:S(2)}) %copy-start.4) | copy-done | bytes 327704
  27.6 2.1 %shard_map.49 = (f32[128,1024]{1,0:T(8,128)S(1)}, f32[128,1024]{1,0:T(8,128)S(1)}, f32[128,1024]{1,0:T(8,128)S(1)}) custom-call(bf16[128,512]{1,0:T(8,128)(2,1)S(1)} %copy-done.1, bf16[128,1024]{1,0:T(8,128)(2,1)S(1)} %copy-done.2, f32[3,1024]{1,0:T(4,128)S(1)} %copy-done.5, bf16[128,3072]{1,0:T(8,128)(2,1)S(1)} %copy-done, bf16[80,2048]{1,0:T(8,128)(2,1)S(1)} %copy-done.4, ...), custom_call_target="tpu_custom_call" | custom-call | tf_op jit(solution)/shard_map/pallas_call | solution.py:372
  29.7 3.8 %all-to-all-done.1 = bf16[16,40,128]{2,1,0:T(8,128)(2,1)S(1)} async-done(((bf16[16,40,128]{2,1,0:T(8,128)(2,1)}), bf16[16,40,128]{2,1,0:T(8,128)(2,1)S(1)}, u32[]{:S(2)}, u32[]{:S(2)}) %all-to-all-start.1) | async-done | bytes 163872 | tf_op jit(solution)/shard_map/all_to_all | solution.py:428
  33.6 0.0 collective-permute-start.3
  33.6 1.0 %shard_map.50.refs_0_ = bf16[128,512]{1,0:T(8,128)(2,1)S(1)} custom-call(bf16[128,512]{1,0:T(8,128)(2,1)S(1)} %copy-done.1, f32[128,1024]{1,0:T(8,128)S(1)} %get-tuple-element.25.numer_ref, f32[128,1024]{1,0:T(8,128)S(1)} %get-tuple-element.26.denom_ref, f32[128,1024]{1,0:T(8,128)S(1)} %get-tuple-element.27.swa_ref, bf16[640,128]{1,0:T(8,128)(2,1)S(1)} %bitcast.2), custom_call_target="tpu_custom_call" | custom-call | tf_op jit(solution)/shard_map/pallas_call | solution.py:372
  34.6 0.4 %collective-permute-done.3.past_ref = bf16[640,128]{1,0:T(8,128)(2,1)S(1)} collective-permute-done((bf16[640,128]{1,0:T(8,128)(2,1)S(1)}, bf16[640,128]{1,0:T(8,128)(2,1)S(1)}, u32[]{:S(2)}, u32[]{:S(2)}) %collective-permute-start.3) | collective-permute-done | bytes 163872 | tf_op jit(solution)/shard_map/ppermute | solution.py:391
  35.0 1.7 %shard_map.51 = bf16[128,1024]{1,0:T(8,128)(2,1)} custom-call(bf16[128,512]{1,0:T(8,128)(2,1)S(1)} %copy-done.1, f32[128,1024]{1,0:T(8,128)S(1)} %get-tuple-element.25.numer_ref, f32[128,1024]{1,0:T(8,128)S(1)} %get-tuple-element.26.denom_ref, f32[128,1024]{1,0:T(8,128)S(1)} %get-tuple-element.27.swa_ref, ...), custom_call_target="tpu_custom_call" | custom-call | tf_op jit(solution)/shard_map/pallas_call | solution.py:372
Async XLA Ops:
  0.0 2.0 %collective-permute-start.1 = (bf16[128,1024]{1,0:T(8,128)(2,1)}, bf16[128,1024]{1,0:T(8,128)(2,1)S(1)}, u32[]{:S(2)}, u32[]{:S(2)}) collective-permute-start(bf16[128,1024]{1,0:T(8,128)(2,1)} %v_ref.1), channel_id=1, source_target_pairs={{0,1},{1,0},{2,3},{3,2},{4,5},{5,4},{6,7},{7,6},{8,9},{9,8},{10,11... | collective-permute-start | bytes 786440 | tf_op jit(solution)/shard_map/ppermute | solution.py:391
  0.5 1.6 %collective-permute-start = (bf16[128,512]{1,0:T(8,128)(2,1)}, bf16[128,512]{1,0:T(8,128)(2,1)S(1)}, u32[]{:S(2)}, u32[]{:S(2)}) collective-permute-start(bf16[128,512]{1,0:T(8,128)(2,1)} %qk_ref.5), channel_id=1, source_target_pairs={{0,1},{1,0},{2,3},{3,2},{4,5},{5,4},{6,7},{7,6},{8,9},{9,8},{10,11... | collective-permute-start | bytes 393224 | tf_op jit(solution)/shard_map/ppermute | solution.py:391
  2.0 24.6 %copy-start.2 = (bf16[128,1024]{1,0:T(8,128)(2,1)S(1)}, bf16[128,1024]{1,0:T(8,128)(2,1)}, u32[]{:S(2)}) copy-start(bf16[128,1024]{1,0:T(8,128)(2,1)} %v_ref.1) | copy-start | bytes 786436
  3.2 23.4 %copy-start = (bf16[128,3072]{1,0:T(8,128)(2,1)S(1)}, bf16[128,3072]{1,0:T(8,128)(2,1)}, u32[]{:S(2)}) copy-start(bf16[128,3072]{1,0:T(8,128)(2,1)} %swa_ref.1) | copy-start | bytes 2359300
  3.2 17.8 %all-to-all-start = ((bf16[16,48,128]{2,1,0:T(8,128)(2,1)}), bf16[16,48,128]{2,1,0:T(8,128)(2,1)S(1)}, u32[]{:S(2)}, u32[]{:S(2)}) async-start(bf16[16,48,128]{2,1,0:T(8,128)(2,1)} %shard_map.47), calls=%async_computation | async-start | bytes 393216 | tf_op jit(solution)/shard_map/all_to_all | solution.py:419
  11.6 14.3 %collective-permute-start.2 = (bf16[80,2048]{1,0:T(8,128)(2,1)S(1)}, bf16[80,2048]{1,0:T(8,128)(2,1)S(1)}, u32[]{:S(2)}, u32[]{:S(2)}) collective-permute-start(bf16[80,2048]{1,0:T(8,128)(2,1)S(1)} %get-tuple-element.21), channel_id=1, source_target_pairs={{0,1},{1,2},{2,3},{3,4},{4,5},{5,6},{6,7},{7,8},{8,9},{9,10},{10,1... | collective-permute-start | bytes 983048 | tf_op jit(solution)/shard_map/ppermute | solution.py:420
  22.2 4.4 %copy-start.1 = (bf16[128,512]{1,0:T(8,128)(2,1)S(1)}, bf16[128,512]{1,0:T(8,128)(2,1)}, u32[]{:S(2)}) copy-start(bf16[128,512]{1,0:T(8,128)(2,1)} %qk_ref.5) | copy-start | bytes 393220
  22.2 4.4 %copy-start.5 = (f32[3,1024]{1,0:T(4,128)S(1)}, f32[3,1024]{1,0:T(4,128)}, u32[]{:S(2)}) copy-start(f32[3,1024]{1,0:T(4,128)} %conv_ref.1) | copy-start | bytes 36868
  22.2 11.3 %all-to-all-start.1 = ((bf16[16,40,128]{2,1,0:T(8,128)(2,1)}), bf16[16,40,128]{2,1,0:T(8,128)(2,1)S(1)}, u32[]{:S(2)}, u32[]{:S(2)}) async-start(bf16[16,40,128]{2,1,0:T(8,128)(2,1)} %shard_map.48), calls=%async_computation.1 | async-start | bytes 327680 | tf_op jit(solution)/shard_map/all_to_all | solution.py:428
  25.9 0.7 %copy-start.3 = (bf16[80,2048]{1,0:T(8,128)(2,1)}, bf16[80,2048]{1,0:T(8,128)(2,1)S(1)}, u32[]{:S(2)}) copy-start(bf16[80,2048]{1,0:T(8,128)(2,1)S(1)} %collective-permute-done.2.tails_ref) | copy-start | bytes 983044
  26.6 1.0 %copy-start.4 = (bf16[80,2048]{1,0:T(8,128)(2,1)S(1)}, bf16[80,2048]{1,0:T(8,128)(2,1)}, u32[]{:S(2)}) copy-start(bf16[80,2048]{1,0:T(8,128)(2,1)} %copy-done.3) | copy-start | bytes 983044
  33.6 1.4 %collective-permute-start.3 = (bf16[640,128]{1,0:T(8,128)(2,1)S(1)}, bf16[640,128]{1,0:T(8,128)(2,1)S(1)}, u32[]{:S(2)}, u32[]{:S(2)}) collective-permute-start(bf16[640,128]{1,0:T(8,128)(2,1)S(1)} %bitcast.1), channel_id=1, source_target_pairs={{0,1},{1,0},{2,3},{3,2},{4,5},{5,4},{6,7},{7,6},{8,9},{9,8},{10,11... | collective-permute-start | bytes 491528 | tf_op jit(solution)/shard_map/ppermute | solution.py:391

commit v6 on v5

--- a/solution.py
+++ b/solution.py
@@ -15,9 +15,7 @@
 SWA_HEAD = 128
 WINDOW = 64
 
-AXES = ("ctxouter", "ctxinner")
-SPLIT = ("outer", "z", "core")
-CHIPS = ("outer", "z")
+BLOCK = "block"
 LANES = 128
 PAIRS = HEADS // 2
 QUADS = FEAT * (FEAT + 1) // 2
@@ -84,7 +82,7 @@
 
 
 def state_kernel(part, own, *refs):
-    core = lax.axis_index("core")
+    core = lax.axis_index(BLOCK) % 2
     if own:
         qk_hbm, v_hbm, conv_hbm, swa_hbm, out_ref, tails_ref, conv_ref, key_ref, v_ref, sems = refs
         rows, wide = v_hbm.shape
@@ -185,15 +183,17 @@
     part = out_ref.shape[1]
     padded = held - EXTRA
     width = chips * EXTRA
-    chip, core = lax.axis_index(CHIPS), lax.axis_index("core")
-    start = core * (ROWS * PAIRS // 2) + chip * part
+    block = lax.axis_index(BLOCK)
+    start = block % 2 * (ROWS * PAIRS // 2) + (chips - 1 - block // 2) * part
     head = start // ROWS * 2 % (LANES // FEAT)
     feature = start % ROWS + iota((padded, LANES), 0)
     lane = iota((padded, LANES), 1)
     one = selector(feature, lane, False)
     two = selector(feature, lane, True)
     add_one, add_two = adders(feature[:, 0:1])
-    extras = parts_ref[:, padded:, :].astype(jnp.float32).reshape(width, LANES)
+    extras = jnp.concatenate(
+        [parts_ref[chips - 1 - chip].astype(jnp.float32)[padded:] for chip in range(chips)], axis=0
+    )
     extras_low = extras.astype(BF16)
     upper = iota((width, LANES), 1) >= VHEAD
     lefts = []
@@ -212,8 +212,8 @@
     def one_chip(chip, total):
         seen = jnp.where(to_block <= 2 * chip, left, 0.0).astype(BF16)
         result = total + dot(seen, right)
-        out_ref[chip] = result[:part].astype(BF16)
-        return total + parts_ref[chip].astype(jnp.float32)[:padded]
+        out_ref[chips - 1 - chip] = result[:part].astype(BF16)
+        return total + parts_ref[chips - 1 - chip].astype(jnp.float32)[:padded]
 
     total = jnp.zeros((padded, LANES), jnp.float32)
     if chips <= 32:
@@ -230,9 +230,9 @@
     rows = v_ref.shape[0]
     taps = conv_ref.shape[0]
     width = HEADS * FEAT
-    core = lax.axis_index("core")
+    core = lax.axis_index(BLOCK) % 2
     second = core == 1
-    first_block = (lax.axis_index(CHIPS) == 0) & (core == 0)
+    first_block = lax.axis_index(BLOCK) == 0
     query = qk_ref[:, :width]
     key = qk_ref[:, width : 2 * width]
     lower = iota((rows, LANES), 1) < VHEAD
@@ -309,7 +309,7 @@
 
 
 def readout_kernel(own, qk_ref, numer_ref, denom_ref, swa_ref, past_ref, *refs):
-    core = lax.axis_index("core")
+    core = lax.axis_index(BLOCK) % 2
     half = core if own else 1 - core
     rows = qk_ref.shape[0]
     wide = PAIRS // 2 * LANES
@@ -382,13 +382,17 @@
 def shards(lin_qk, lin_v, conv_w, swa_qkv):
     rows = lin_qk.shape[0]
     taps = conv_w.shape[0]
-    chips = lax.axis_size("outer") * lax.axis_size("z")
+    chips = lax.axis_size(BLOCK) // 2
     part = PAIRS // 2 * ROWS // chips
     held = (part + 7) // 8 * 8 + EXTRA
     shape = jax.ShapeDtypeStruct
 
     def swap(array):
-        return lax.ppermute(array, "core", [(0, 1), (1, 0)])
+        return lax.ppermute(array, BLOCK, [(i, i ^ 1) for i in range(2 * chips)])
+
+    def exchange(array):
+        groups = [list(range(core, 2 * chips, 2))[::-1] for core in range(2)]
+        return lax.all_to_all(array, BLOCK, 0, 0, axis_index_groups=groups, tiled=True)
 
     other_qk, other_v = swap(lin_qk), swap(lin_v)
     half_wide = lin_v.shape[1] // 2
@@ -416,8 +420,8 @@
         IN_VMEM,
     )
     sums, tails = lax.optimization_barrier((sums, tails))
-    parts = lax.all_to_all(sums, CHIPS, 0, 0, tiled=True)
-    tails = lax.ppermute(tails, SPLIT, [(i, i + 1) for i in range(2 * chips - 1)])
+    parts = exchange(sums)
+    tails = lax.ppermute(tails, BLOCK, [(i, i + 1) for i in range(2 * chips - 1)])
     past = call(
         functools.partial(prefix_kernel, taps),
         shape((chips, part, LANES), BF16),
@@ -425,7 +429,7 @@
         [IN_VMEM],
         IN_VMEM,
     )
-    here = lax.all_to_all(past, CHIPS, 0, 0, tiled=True).reshape(chips * part, LANES)
+    here = exchange(past).reshape(chips * part, LANES)
     wide = shape(lin_v.shape, jnp.float32)
     numer, denom, swa = call(
         local_kernel,
@@ -454,12 +458,11 @@
 
 
 def solution(mesh):
-    outer, inner = mesh.shape["ctxouter"], mesh.shape["ctxinner"]
-    split = jax.sharding.Mesh(mesh.devices.reshape(outer, inner // 2, 2), SPLIT)
+    blocks = jax.sharding.Mesh(mesh.devices.reshape(-1), (BLOCK,))
     return jax.shard_map(
         shards,
-        mesh=split,
-        in_specs=(P(SPLIT, None), P(SPLIT, None), P(), P(SPLIT, None)),
-        out_specs=P(SPLIT, None),
+        mesh=blocks,
+        in_specs=(P(BLOCK, None), P(BLOCK, None), P(), P(BLOCK, None)),
+        out_specs=P(BLOCK, None),
         check_vma=False,
     )

time: 37 us -> 36.4 us (0.984)
  waiting for transfers between devices: 12 us -> 4.55 us
  starting transfers between devices: 14.3 us -> 21.2 us
    all_to_all x2, waiting for transfers between devices: 11.5 us -> 4.09 us  [exchange(): lax.all_to_all(array, BLOCK, 0, 0, axis_index_groups=groups, tiled=True)]
    all_to_all x2, starting transfers between devices: 12.1 us -> 18.9 us  [exchange(): lax.all_to_all(array, BLOCK, 0, 0, axis_index_groups=groups, tiled=True)]
where the time goes in v6:
time: 36.4 us; the launch traced here: 36.1 us
  starting transfers between devices  21.2 us (58%)
  Pallas kernels  8.6 us (24%)
  waiting for transfers between devices  4.55 us (12%)
  local copies, waits for them, and re-layouts  1.69 us (5%)
    all_to_all x2, starting transfers between devices, exchange(): lax.all_to_all(array, BLOCK, 0, 0, axis_index_groups=groups, tiled=True)  18.9 us
    pallas_call x6, Pallas kernels, call(): pl.pallas_call(kernel, out_shape=results, in_specs=specs, out_specs=out_s...  8.6 us
    all_to_all x2, waiting for transfers between devices, exchange(): lax.all_to_all(array, BLOCK, 0, 0, axis_index_groups=groups, tiled=True)  4.09 us
    ppermute x1, starting transfers between devices, shards(): lax.ppermute(tails, BLOCK, [(i, i + 1) for i in range(2 * chips - 1)])  1.72 us
    unnamed x12, local copies, waits for them, and re-layouts  1.69 us
  transfers between devices with their start and end apart: 6, of which 4 were waited for; matrix products, arithmetic and copies ran while one was open for 0% of the time, Pallas kernels for 16%

profile of v6, /device:TPU:0, one launch (start us, length us, event | category | flops | bytes accessed | tf_op | source)
XLA Modules:
  0.0 36.1 jit_solution(6919657582432734341)
XLA Ops:
  0.0 0.5 %collective-permute-start.1 = (bf16[128,1024]{1,0:T(8,128)(2,1)}, bf16[128,1024]{1,0:T(8,128)(2,1)S(1)}, u32[]{:S(2)}, u32[]{:S(2)}) collective-permute-start(bf16[128,1024]{1,0:T(8,128)(2,1)} %v_ref.1), channel_id=1, source_target_pairs={{0,1},{1,0},{2,3},{3,2},{4,5},{5,4},{6,7},{7,6},{8,9},{9,8},{10,11... | collective-permute-start | bytes 786440 | tf_op jit(solution)/shard_map/ppermute | solution.py:391
  0.5 0.1 collective-permute-start
  0.5 1.4 %shard_map.46 = (f32[16,48,128]{2,1,0:T(8,128)S(1)}, bf16[80,2048]{1,0:T(8,128)(2,1)S(1)}, f32[3,512]{1,0:T(4,128)S(1)}) custom-call(bf16[128,512]{1,0:T(8,128)(2,1)} %qk_ref.5, bf16[128,1024]{1,0:T(8,128)(2,1)} %v_ref.1, f32[3,1024]{1,0:T(4,128)} %conv_ref.1, bf16[128,3072]{1,0:T(8,128)(2,1)} %swa_ref.1), custom_call_target="tpu_custom_call" | custom-call | tf_op jit(solution)/shard_map/pallas_call | solution.py:372
  1.9 0.1 collective-permute-done.refs_0_.other_qk_ref
  2.0 0.0 collective-permute-done.1.refs_1_.other_v_ref
  2.0 0.0 copy-start.2
  2.0 1.2 %shard_map.47 = bf16[16,48,128]{2,1,0:T(8,128)(2,1)} custom-call(bf16[128,512]{1,0:T(8,128)(2,1)S(1)} %collective-permute-done.refs_0_.other_qk_ref, bf16[128,1024]{1,0:T(8,128)(2,1)S(1)} %collective-permute-done.1.refs_1_.other_v_ref, f32[3,512]{1,0:T(4,128)S(1)} %get-tuple-element.17.refs_2_, f32[16,48,128]{2,1,0:T(8,128)S(1)} %get-tuple-element.18.refs_3_), custom_call_target="tpu_custom_call" | custom-call | tf_op jit(solution)/shard_map/pallas_call | solution.py:372
  3.2 0.0 copy-start
  3.2 10.4 %all-to-all-start = ((bf16[16,48,128]{2,1,0:T(8,128)(2,1)}), bf16[16,48,128]{2,1,0:T(8,128)(2,1)S(1)}, u32[]{:S(2)}, u32[]{:S(2)}) async-start(bf16[16,48,128]{2,1,0:T(8,128)(2,1)} %shard_map.47), calls=%async_computation | async-start | bytes 393216 | tf_op jit(solution)/shard_map/all_to_all | solution.py:395
  13.6 1.7 %collective-permute-start.2 = (bf16[80,2048]{1,0:T(8,128)(2,1)S(1)}, bf16[80,2048]{1,0:T(8,128)(2,1)S(1)}, u32[]{:S(2)}, u32[]{:S(2)}) collective-permute-start(bf16[80,2048]{1,0:T(8,128)(2,1)S(1)} %get-tuple-element.21), channel_id=1, source_target_pairs={{0,1},{1,2},{2,3},{3,4},{4,5},{5,6},{6,7},{7,8},{8,9},{9,10},{10,1... | collective-permute-start | bytes 983048 | tf_op jit(solution)/shard_map/ppermute | solution.py:424
  15.4 3.9 %all-to-all-done.parts_ref = bf16[16,48,128]{2,1,0:T(8,128)(2,1)S(1)} async-done(((bf16[16,48,128]{2,1,0:T(8,128)(2,1)}), bf16[16,48,128]{2,1,0:T(8,128)(2,1)S(1)}, u32[]{:S(2)}, u32[]{:S(2)}) %all-to-all-start) | async-done | bytes 196640 | tf_op jit(solution)/shard_map/all_to_all | solution.py:395
  19.2 1.2 %shard_map.48 = bf16[16,40,128]{2,1,0:T(8,128)(2,1)} custom-call(bf16[16,48,128]{2,1,0:T(8,128)(2,1)S(1)} %all-to-all-done.parts_ref), custom_call_target="tpu_custom_call" | custom-call | tf_op jit(solution)/shard_map/pallas_call | solution.py:372
  20.4 0.0 copy-start.1
  20.5 0.0 copy-start.5
  20.5 8.5 %all-to-all-start.1 = ((bf16[16,40,128]{2,1,0:T(8,128)(2,1)}), bf16[16,40,128]{2,1,0:T(8,128)(2,1)S(1)}, u32[]{:S(2)}, u32[]{:S(2)}) async-start(bf16[16,40,128]{2,1,0:T(8,128)(2,1)} %shard_map.48), calls=%async_computation.1 | async-start | bytes 327680 | tf_op jit(solution)/shard_map/all_to_all | solution.py:395
  29.0 0.0 collective-permute-done.2.tails_ref
  29.0 0.0 copy-start.3
  29.0 0.7 %copy-done.3 = bf16[80,2048]{1,0:T(8,128)(2,1)} copy-done((bf16[80,2048]{1,0:T(8,128)(2,1)}, bf16[80,2048]{1,0:T(8,128)(2,1)S(1)}, u32[]{:S(2)}) %copy-start.3) | copy-done | bytes 327704
  29.7 0.0 copy-done.2
  29.7 0.0 copy-done
  29.7 0.0 copy-done.1
  29.7 0.0 copy-done.5
  29.7 0.0 copy-start.4
  29.7 1.0 %copy-done.4 = bf16[80,2048]{1,0:T(8,128)(2,1)S(1)} copy-done((bf16[80,2048]{1,0:T(8,128)(2,1)S(1)}, bf16[80,2048]{1,0:T(8,128)(2,1)}, u32[]{:S(2)}) %copy-start.4) | copy-done | bytes 327704
  30.7 2.1 %shard_map.49 = (f32[128,1024]{1,0:T(8,128)S(1)}, f32[128,1024]{1,0:T(8,128)S(1)}, f32[128,1024]{1,0:T(8,128)S(1)}) custom-call(bf16[128,512]{1,0:T(8,128)(2,1)S(1)} %copy-done.1, bf16[128,1024]{1,0:T(8,128)(2,1)S(1)} %copy-done.2, f32[3,1024]{1,0:T(4,128)S(1)} %copy-done.5, bf16[128,3072]{1,0:T(8,128)(2,1)S(1)} %copy-done, bf16[80,2048]{1,0:T(8,128)(2,1)S(1)} %copy-done.4, ...), custom_call_target="tpu_custom_call" | custom-call | tf_op jit(solution)/shard_map/pallas_call | solution.py:372
  32.8 0.2 all-to-all-done.1
  33.0 0.0 collective-permute-start.3
  33.0 1.0 %shard_map.50.refs_0_ = bf16[128,512]{1,0:T(8,128)(2,1)S(1)} custom-call(bf16[128,512]{1,0:T(8,128)(2,1)S(1)} %copy-done.1, f32[128,1024]{1,0:T(8,128)S(1)} %get-tuple-element.25.numer_ref, f32[128,1024]{1,0:T(8,128)S(1)} %get-tuple-element.26.denom_ref, f32[128,1024]{1,0:T(8,128)S(1)} %get-tuple-element.27.swa_ref, bf16[640,128]{1,0:T(8,128)(2,1)S(1)} %bitcast.2), custom_call_target="tpu_custom_call" | custom-call | tf_op jit(solution)/shard_map/pallas_call | solution.py:372
  34.0 0.4 %collective-permute-done.3.past_ref = bf16[640,128]{1,0:T(8,128)(2,1)S(1)} collective-permute-done((bf16[640,128]{1,0:T(8,128)(2,1)S(1)}, bf16[640,128]{1,0:T(8,128)(2,1)S(1)}, u32[]{:S(2)}, u32[]{:S(2)}) %collective-permute-start.3) | collective-permute-done | bytes 163872 | tf_op jit(solution)/shard_map/ppermute | solution.py:391
  34.4 1.7 %shard_map.51 = bf16[128,1024]{1,0:T(8,128)(2,1)} custom-call(bf16[128,512]{1,0:T(8,128)(2,1)S(1)} %copy-done.1, f32[128,1024]{1,0:T(8,128)S(1)} %get-tuple-element.25.numer_ref, f32[128,1024]{1,0:T(8,128)S(1)} %get-tuple-element.26.denom_ref, f32[128,1024]{1,0:T(8,128)S(1)} %get-tuple-element.27.swa_ref, ...), custom_call_target="tpu_custom_call" | custom-call | tf_op jit(solution)/shard_map/pallas_call | solution.py:372
Async XLA Ops:
  0.0 2.0 %collective-permute-start.1 = (bf16[128,1024]{1,0:T(8,128)(2,1)}, bf16[128,1024]{1,0:T(8,128)(2,1)S(1)}, u32[]{:S(2)}, u32[]{:S(2)}) collective-permute-start(bf16[128,1024]{1,0:T(8,128)(2,1)} %v_ref.1), channel_id=1, source_target_pairs={{0,1},{1,0},{2,3},{3,2},{4,5},{5,4},{6,7},{7,6},{8,9},{9,8},{10,11... | collective-permute-start | bytes 786440 | tf_op jit(solution)/shard_map/ppermute | solution.py:391
  0.5 1.6 %collective-permute-start = (bf16[128,512]{1,0:T(8,128)(2,1)}, bf16[128,512]{1,0:T(8,128)(2,1)S(1)}, u32[]{:S(2)}, u32[]{:S(2)}) collective-permute-start(bf16[128,512]{1,0:T(8,128)(2,1)} %qk_ref.5), channel_id=1, source_target_pairs={{0,1},{1,0},{2,3},{3,2},{4,5},{5,4},{6,7},{7,6},{8,9},{9,8},{10,11... | collective-permute-start | bytes 393224 | tf_op jit(solution)/shard_map/ppermute | solution.py:391
  2.0 27.7 %copy-start.2 = (bf16[128,1024]{1,0:T(8,128)(2,1)S(1)}, bf16[128,1024]{1,0:T(8,128)(2,1)}, u32[]{:S(2)}) copy-start(bf16[128,1024]{1,0:T(8,128)(2,1)} %v_ref.1) | copy-start | bytes 786436
  3.2 26.5 %copy-start = (bf16[128,3072]{1,0:T(8,128)(2,1)S(1)}, bf16[128,3072]{1,0:T(8,128)(2,1)}, u32[]{:S(2)}) copy-start(bf16[128,3072]{1,0:T(8,128)(2,1)} %swa_ref.1) | copy-start | bytes 2359300
  3.2 16.1 %all-to-all-start = ((bf16[16,48,128]{2,1,0:T(8,128)(2,1)}), bf16[16,48,128]{2,1,0:T(8,128)(2,1)S(1)}, u32[]{:S(2)}, u32[]{:S(2)}) async-start(bf16[16,48,128]{2,1,0:T(8,128)(2,1)} %shard_map.47), calls=%async_computation | async-start | bytes 393216 | tf_op jit(solution)/shard_map/all_to_all | solution.py:395
  13.6 15.3 %collective-permute-start.2 = (bf16[80,2048]{1,0:T(8,128)(2,1)S(1)}, bf16[80,2048]{1,0:T(8,128)(2,1)S(1)}, u32[]{:S(2)}, u32[]{:S(2)}) collective-permute-start(bf16[80,2048]{1,0:T(8,128)(2,1)S(1)} %get-tuple-element.21), channel_id=1, source_target_pairs={{0,1},{1,2},{2,3},{3,4},{4,5},{5,6},{6,7},{7,8},{8,9},{9,10},{10,1... | collective-permute-start | bytes 983048 | tf_op jit(solution)/shard_map/ppermute | solution.py:424
  20.4 9.2 %copy-start.1 = (bf16[128,512]{1,0:T(8,128)(2,1)S(1)}, bf16[128,512]{1,0:T(8,128)(2,1)}, u32[]{:S(2)}) copy-start(bf16[128,512]{1,0:T(8,128)(2,1)} %qk_ref.5) | copy-start | bytes 393220
  20.5 9.2 %copy-start.5 = (f32[3,1024]{1,0:T(4,128)S(1)}, f32[3,1024]{1,0:T(4,128)}, u32[]{:S(2)}) copy-start(f32[3,1024]{1,0:T(4,128)} %conv_ref.1) | copy-start | bytes 36868
  20.5 12.5 %all-to-all-start.1 = ((bf16[16,40,128]{2,1,0:T(8,128)(2,1)}), bf16[16,40,128]{2,1,0:T(8,128)(2,1)S(1)}, u32[]{:S(2)}, u32[]{:S(2)}) async-start(bf16[16,40,128]{2,1,0:T(8,128)(2,1)} %shard_map.48), calls=%async_computation.1 | async-start | bytes 327680 | tf_op jit(solution)/shard_map/all_to_all | solution.py:395
  29.0 0.7 %copy-start.3 = (bf16[80,2048]{1,0:T(8,128)(2,1)}, bf16[80,2048]{1,0:T(8,128)(2,1)S(1)}, u32[]{:S(2)}) copy-start(bf16[80,2048]{1,0:T(8,128)(2,1)S(1)} %collective-permute-done.2.tails_ref) | copy-start | bytes 983044
  29.7 1.0 %copy-start.4 = (bf16[80,2048]{1,0:T(8,128)(2,1)S(1)}, bf16[80,2048]{1,0:T(8,128)(2,1)}, u32[]{:S(2)}) copy-start(bf16[80,2048]{1,0:T(8,128)(2,1)} %copy-done.3) | copy-start | bytes 983044
  33.0 1.4 %collective-permute-start.3 = (bf16[640,128]{1,0:T(8,128)(2,1)S(1)}, bf16[640,128]{1,0:T(8,128)(2,1)S(1)}, u32[]{:S(2)}, u32[]{:S(2)}) collective-permute-start(bf16[640,128]{1,0:T(8,128)(2,1)S(1)} %bitcast.1), channel_id=1, source_target_pairs={{0,1},{1,0},{2,3},{3,2},{4,5},{5,4},{6,7},{7,6},{8,9},{9,8},{10,11... | collective-permute-start | bytes 491528 | tf_op jit(solution)/shard_map/ppermute | solution.py:391

commit v7 on v6

--- a/solution.py
+++ b/solution.py
@@ -16,6 +16,7 @@
 WINDOW = 64
 
 BLOCK = "block"
+ORDER_SEED = 24
 LANES = 128
 PAIRS = HEADS // 2
 QUADS = FEAT * (FEAT + 1) // 2
@@ -56,6 +57,10 @@
     first = jnp.where(feature == CONST, 1.0, 0.0)
     second = jnp.where((feature >= QUADS) & (feature <= CONST), 1.0, 0.0)
     return first, second
+
+
+def group_order(chips):
+    return [int(chip) for chip in np.random.RandomState(ORDER_SEED).permutation(chips)]
 
 
 def head_mask(head, shape):
@@ -184,7 +189,9 @@
     padded = held - EXTRA
     width = chips * EXTRA
     block = lax.axis_index(BLOCK)
-    start = block % 2 * (ROWS * PAIRS // 2) + (chips - 1 - block // 2) * part
+    places = list(np.argsort(group_order(chips)))
+    place = sum(jnp.where(block // 2 == chip, int(at), 0) for chip, at in enumerate(places))
+    start = block % 2 * (ROWS * PAIRS // 2) + place * part
     head = start // ROWS * 2 % (LANES // FEAT)
     feature = start % ROWS + iota((padded, LANES), 0)
     lane = iota((padded, LANES), 1)
@@ -192,7 +199,7 @@
     two = selector(feature, lane, True)
     add_one, add_two = adders(feature[:, 0:1])
     extras = jnp.concatenate(
-        [parts_ref[chips - 1 - chip].astype(jnp.float32)[padded:] for chip in range(chips)], axis=0
+        [parts_ref[int(at)].astype(jnp.float32)[padded:] for at in places], axis=0
     )
     extras_low = extras.astype(BF16)
     upper = iota((width, LANES), 1) >= VHEAD
@@ -209,18 +216,11 @@
     column = iota(left.shape, 1) % width
     to_block = jnp.where(column % BLOCK_EXTRA < taps - 1, column // BLOCK_EXTRA + 1, 2 * chips)
 
-    def one_chip(chip, total):
+    total = jnp.zeros((padded, LANES), jnp.float32)
+    for chip, at in enumerate(places):
         seen = jnp.where(to_block <= 2 * chip, left, 0.0).astype(BF16)
-        result = total + dot(seen, right)
-        out_ref[chips - 1 - chip] = result[:part].astype(BF16)
-        return total + parts_ref[chips - 1 - chip].astype(jnp.float32)[:padded]
-
-    total = jnp.zeros((padded, LANES), jnp.float32)
-    if chips <= 32:
-        for chip in range(chips):
-            total = one_chip(chip, total)
-    else:
-        lax.fori_loop(0, chips, one_chip, total)
+        out_ref[int(at)] = (total + dot(seen, right))[:part].astype(BF16)
+        total = total + parts_ref[int(at)].astype(jnp.float32)[:padded]
 
 
 def local_kernel(
@@ -391,7 +391,7 @@
         return lax.ppermute(array, BLOCK, [(i, i ^ 1) for i in range(2 * chips)])
 
     def exchange(array):
-        groups = [list(range(core, 2 * chips, 2))[::-1] for core in range(2)]
+        groups = [[2 * chip + core for chip in group_order(chips)] for core in range(2)]
         return lax.all_to_all(array, BLOCK, 0, 0, axis_index_groups=groups, tiled=True)
 
     other_qk, other_v = swap(lin_qk), swap(lin_v)

time: 36.4 us -> 33.8 us (0.929)
  starting transfers between devices: 21.2 us -> 17.4 us
  waiting for transfers between devices: 4.55 us -> 5.71 us
    all_to_all x2, starting transfers between devices: 18.9 us -> 15.5 us  [exchange(): lax.all_to_all(array, BLOCK, 0, 0, axis_index_groups=groups, tiled=True)]
    all_to_all x2, waiting for transfers between devices: 4.09 us -> 5.26 us  [exchange(): lax.all_to_all(array, BLOCK, 0, 0, axis_index_groups=groups, tiled=True)]
  transfers between devices with their start and end apart: 6 -> 6, of which waited for: 4 -> 4; matrix products, arithmetic and copies ran while one was open for 0% -> 0% of each run, Pallas kernels for 16% -> 17%
where the time goes in v7:
time: 33.8 us; the launch traced here: 33.5 us
  starting transfers between devices  17.4 us (51%)
  Pallas kernels  8.61 us (25%)
  waiting for transfers between devices  5.71 us (17%)
  local copies, waits for them, and re-layouts  1.69 us (5%)
    all_to_all x2, starting transfers between devices, exchange(): lax.all_to_all(array, BLOCK, 0, 0, axis_index_groups=groups, tiled=True)  15.5 us
    pallas_call x6, Pallas kernels, call(): pl.pallas_call(kernel, out_shape=results, in_specs=specs, out_specs=out_s...  8.61 us
    all_to_all x2, waiting for transfers between devices, exchange(): lax.all_to_all(array, BLOCK, 0, 0, axis_index_groups=groups, tiled=True)  5.26 us
    unnamed x12, local copies, waits for them, and re-layouts  1.69 us
    ppermute x1, starting transfers between devices, shards(): lax.ppermute(tails, BLOCK, [(i, i + 1) for i in range(2 * chips - 1)])  1.44 us
  transfers between devices with their start and end apart: 6, of which 4 were waited for; matrix products, arithmetic and copies ran while one was open for 0% of the time, Pallas kernels for 17%

profile of v7, /device:TPU:0, one launch (start us, length us, event | category | flops | bytes accessed | tf_op | source)
XLA Modules:
  0.0 33.5 jit_solution(17099557363046430104)
XLA Ops:
  0.0 0.5 %collective-permute-start.1 = (bf16[128,1024]{1,0:T(8,128)(2,1)}, bf16[128,1024]{1,0:T(8,128)(2,1)S(1)}, u32[]{:S(2)}, u32[]{:S(2)}) collective-permute-start(bf16[128,1024]{1,0:T(8,128)(2,1)} %v_ref.1), channel_id=1, source_target_pairs={{0,1},{1,0},{2,3},{3,2},{4,5},{5,4},{6,7},{7,6},{8,9},{9,8},{10,11... | collective-permute-start | bytes 786440 | tf_op jit(solution)/shard_map/ppermute | solution.py:391
  0.5 0.1 collective-permute-start
  0.5 1.4 %shard_map.46 = (f32[16,48,128]{2,1,0:T(8,128)S(1)}, bf16[80,2048]{1,0:T(8,128)(2,1)S(1)}, f32[3,512]{1,0:T(4,128)S(1)}) custom-call(bf16[128,512]{1,0:T(8,128)(2,1)} %qk_ref.5, bf16[128,1024]{1,0:T(8,128)(2,1)} %v_ref.1, f32[3,1024]{1,0:T(4,128)} %conv_ref.1, bf16[128,3072]{1,0:T(8,128)(2,1)} %swa_ref.1), custom_call_target="tpu_custom_call" | custom-call | tf_op jit(solution)/shard_map/pallas_call | solution.py:372
  1.9 0.1 collective-permute-done.refs_0_.other_qk_ref
  2.0 0.0 collective-permute-done.1.refs_1_.other_v_ref
  2.0 0.0 copy-start.2
  2.0 1.2 %shard_map.47 = bf16[16,48,128]{2,1,0:T(8,128)(2,1)} custom-call(bf16[128,512]{1,0:T(8,128)(2,1)S(1)} %collective-permute-done.refs_0_.other_qk_ref, bf16[128,1024]{1,0:T(8,128)(2,1)S(1)} %collective-permute-done.1.refs_1_.other_v_ref, f32[3,512]{1,0:T(4,128)S(1)} %get-tuple-element.17.refs_2_, f32[16,48,128]{2,1,0:T(8,128)S(1)} %get-tuple-element.18.refs_3_), custom_call_target="tpu_custom_call" | custom-call | tf_op jit(solution)/shard_map/pallas_call | solution.py:372
  3.2 0.0 copy-start
  3.2 8.9 %all-to-all-start = ((bf16[16,48,128]{2,1,0:T(8,128)(2,1)}), bf16[16,48,128]{2,1,0:T(8,128)(2,1)S(1)}, u32[]{:S(2)}, u32[]{:S(2)}) async-start(bf16[16,48,128]{2,1,0:T(8,128)(2,1)} %shard_map.47), calls=%async_computation | async-start | bytes 393216 | tf_op jit(solution)/shard_map/all_to_all | solution.py:395
  12.1 1.4 %collective-permute-start.2 = (bf16[80,2048]{1,0:T(8,128)(2,1)S(1)}, bf16[80,2048]{1,0:T(8,128)(2,1)S(1)}, u32[]{:S(2)}, u32[]{:S(2)}) collective-permute-start(bf16[80,2048]{1,0:T(8,128)(2,1)S(1)} %get-tuple-element.21), channel_id=1, source_target_pairs={{0,1},{1,2},{2,3},{3,4},{4,5},{5,6},{6,7},{7,8},{8,9},{9,10},{10,1... | collective-permute-start | bytes 983048 | tf_op jit(solution)/shard_map/ppermute | solution.py:424
  13.5 4.1 %all-to-all-done.parts_ref = bf16[16,48,128]{2,1,0:T(8,128)(2,1)S(1)} async-done(((bf16[16,48,128]{2,1,0:T(8,128)(2,1)}), bf16[16,48,128]{2,1,0:T(8,128)(2,1)S(1)}, u32[]{:S(2)}, u32[]{:S(2)}) %all-to-all-start) | async-done | bytes 196640 | tf_op jit(solution)/shard_map/all_to_all | solution.py:395
  17.6 1.2 %shard_map.48 = bf16[16,40,128]{2,1,0:T(8,128)(2,1)} custom-call(bf16[16,48,128]{2,1,0:T(8,128)(2,1)S(1)} %all-to-all-done.parts_ref), custom_call_target="tpu_custom_call" | custom-call | tf_op jit(solution)/shard_map/pallas_call | solution.py:372
  18.9 0.0 copy-start.1
  18.9 0.0 copy-start.5
  18.9 6.6 %all-to-all-start.1 = ((bf16[16,40,128]{2,1,0:T(8,128)(2,1)}), bf16[16,40,128]{2,1,0:T(8,128)(2,1)S(1)}, u32[]{:S(2)}, u32[]{:S(2)}) async-start(bf16[16,40,128]{2,1,0:T(8,128)(2,1)} %shard_map.48), calls=%async_computation.1 | async-start | bytes 327680 | tf_op jit(solution)/shard_map/all_to_all | solution.py:395
  25.4 0.0 collective-permute-done.2.tails_ref
  25.4 0.0 copy-start.3
  25.4 0.7 %copy-done.3 = bf16[80,2048]{1,0:T(8,128)(2,1)} copy-done((bf16[80,2048]{1,0:T(8,128)(2,1)}, bf16[80,2048]{1,0:T(8,128)(2,1)S(1)}, u32[]{:S(2)}) %copy-start.3) | copy-done | bytes 327704
  26.2 0.0 copy-done.2
  26.2 0.0 copy-done
  26.2 0.0 copy-done.1
  26.2 0.0 copy-done.5
  26.2 0.0 copy-start.4
  26.2 1.0 %copy-done.4 = bf16[80,2048]{1,0:T(8,128)(2,1)S(1)} copy-done((bf16[80,2048]{1,0:T(8,128)(2,1)S(1)}, bf16[80,2048]{1,0:T(8,128)(2,1)}, u32[]{:S(2)}) %copy-start.4) | copy-done | bytes 327704
  27.1 2.1 %shard_map.49 = (f32[128,1024]{1,0:T(8,128)S(1)}, f32[128,1024]{1,0:T(8,128)S(1)}, f32[128,1024]{1,0:T(8,128)S(1)}) custom-call(bf16[128,512]{1,0:T(8,128)(2,1)S(1)} %copy-done.1, bf16[128,1024]{1,0:T(8,128)(2,1)S(1)} %copy-done.2, f32[3,1024]{1,0:T(4,128)S(1)} %copy-done.5, bf16[128,3072]{1,0:T(8,128)(2,1)S(1)} %copy-done, bf16[80,2048]{1,0:T(8,128)(2,1)S(1)} %copy-done.4, ...), custom_call_target="tpu_custom_call" | custom-call | tf_op jit(solution)/shard_map/pallas_call | solution.py:372
  29.3 1.1 %all-to-all-done.1 = bf16[16,40,128]{2,1,0:T(8,128)(2,1)S(1)} async-done(((bf16[16,40,128]{2,1,0:T(8,128)(2,1)}), bf16[16,40,128]{2,1,0:T(8,128)(2,1)S(1)}, u32[]{:S(2)}, u32[]{:S(2)}) %all-to-all-start.1) | async-done | bytes 163872 | tf_op jit(solution)/shard_map/all_to_all | solution.py:395
  30.4 0.0 collective-permute-start.3
  30.4 1.0 %shard_map.50.refs_0_ = bf16[128,512]{1,0:T(8,128)(2,1)S(1)} custom-call(bf16[128,512]{1,0:T(8,128)(2,1)S(1)} %copy-done.1, f32[128,1024]{1,0:T(8,128)S(1)} %get-tuple-element.25.numer_ref, f32[128,1024]{1,0:T(8,128)S(1)} %get-tuple-element.26.denom_ref, f32[128,1024]{1,0:T(8,128)S(1)} %get-tuple-element.27.swa_ref, bf16[640,128]{1,0:T(8,128)(2,1)S(1)} %bitcast.2), custom_call_target="tpu_custom_call" | custom-call | tf_op jit(solution)/shard_map/pallas_call | solution.py:372
  31.4 0.4 %collective-permute-done.3.past_ref = bf16[640,128]{1,0:T(8,128)(2,1)S(1)} collective-permute-done((bf16[640,128]{1,0:T(8,128)(2,1)S(1)}, bf16[640,128]{1,0:T(8,128)(2,1)S(1)}, u32[]{:S(2)}, u32[]{:S(2)}) %collective-permute-start.3) | collective-permute-done | bytes 163872 | tf_op jit(solution)/shard_map/ppermute | solution.py:391
  31.8 1.7 %shard_map.51 = bf16[128,1024]{1,0:T(8,128)(2,1)} custom-call(bf16[128,512]{1,0:T(8,128)(2,1)S(1)} %copy-done.1, f32[128,1024]{1,0:T(8,128)S(1)} %get-tuple-element.25.numer_ref, f32[128,1024]{1,0:T(8,128)S(1)} %get-tuple-element.26.denom_ref, f32[128,1024]{1,0:T(8,128)S(1)} %get-tuple-element.27.swa_ref, ...), custom_call_target="tpu_custom_call" | custom-call | tf_op jit(solution)/shard_map/pallas_call | solution.py:372
Async XLA Ops:
  0.0 2.0 %collective-permute-start.1 = (bf16[128,1024]{1,0:T(8,128)(2,1)}, bf16[128,1024]{1,0:T(8,128)(2,1)S(1)}, u32[]{:S(2)}, u32[]{:S(2)}) collective-permute-start(bf16[128,1024]{1,0:T(8,128)(2,1)} %v_ref.1), channel_id=1, source_target_pairs={{0,1},{1,0},{2,3},{3,2},{4,5},{5,4},{6,7},{7,6},{8,9},{9,8},{10,11... | collective-permute-start | bytes 786440 | tf_op jit(solution)/shard_map/ppermute | solution.py:391
  0.5 1.6 %collective-permute-start = (bf16[128,512]{1,0:T(8,128)(2,1)}, bf16[128,512]{1,0:T(8,128)(2,1)S(1)}, u32[]{:S(2)}, u32[]{:S(2)}) collective-permute-start(bf16[128,512]{1,0:T(8,128)(2,1)} %qk_ref.5), channel_id=1, source_target_pairs={{0,1},{1,0},{2,3},{3,2},{4,5},{5,4},{6,7},{7,6},{8,9},{9,8},{10,11... | collective-permute-start | bytes 393224 | tf_op jit(solution)/shard_map/ppermute | solution.py:391
  2.0 24.1 %copy-start.2 = (bf16[128,1024]{1,0:T(8,128)(2,1)S(1)}, bf16[128,1024]{1,0:T(8,128)(2,1)}, u32[]{:S(2)}) copy-start(bf16[128,1024]{1,0:T(8,128)(2,1)} %v_ref.1) | copy-start | bytes 786436
  3.2 23.0 %copy-start = (bf16[128,3072]{1,0:T(8,128)(2,1)S(1)}, bf16[128,3072]{1,0:T(8,128)(2,1)}, u32[]{:S(2)}) copy-start(bf16[128,3072]{1,0:T(8,128)(2,1)} %swa_ref.1) | copy-start | bytes 2359300
  3.2 14.5 %all-to-all-start = ((bf16[16,48,128]{2,1,0:T(8,128)(2,1)}), bf16[16,48,128]{2,1,0:T(8,128)(2,1)S(1)}, u32[]{:S(2)}, u32[]{:S(2)}) async-start(bf16[16,48,128]{2,1,0:T(8,128)(2,1)} %shard_map.47), calls=%async_computation | async-start | bytes 393216 | tf_op jit(solution)/shard_map/all_to_all | solution.py:395
  12.1 13.4 %collective-permute-start.2 = (bf16[80,2048]{1,0:T(8,128)(2,1)S(1)}, bf16[80,2048]{1,0:T(8,128)(2,1)S(1)}, u32[]{:S(2)}, u32[]{:S(2)}) collective-permute-start(bf16[80,2048]{1,0:T(8,128)(2,1)S(1)} %get-tuple-element.21), channel_id=1, source_target_pairs={{0,1},{1,2},{2,3},{3,4},{4,5},{5,6},{6,7},{7,8},{8,9},{9,10},{10,1... | collective-permute-start | bytes 983048 | tf_op jit(solution)/shard_map/ppermute | solution.py:424
  18.9 7.3 %copy-start.1 = (bf16[128,512]{1,0:T(8,128)(2,1)S(1)}, bf16[128,512]{1,0:T(8,128)(2,1)}, u32[]{:S(2)}) copy-start(bf16[128,512]{1,0:T(8,128)(2,1)} %qk_ref.5) | copy-start | bytes 393220
  18.9 7.3 %copy-start.5 = (f32[3,1024]{1,0:T(4,128)S(1)}, f32[3,1024]{1,0:T(4,128)}, u32[]{:S(2)}) copy-start(f32[3,1024]{1,0:T(4,128)} %conv_ref.1) | copy-start | bytes 36868
  18.9 11.5 %all-to-all-start.1 = ((bf16[16,40,128]{2,1,0:T(8,128)(2,1)}), bf16[16,40,128]{2,1,0:T(8,128)(2,1)S(1)}, u32[]{:S(2)}, u32[]{:S(2)}) async-start(bf16[16,40,128]{2,1,0:T(8,128)(2,1)} %shard_map.48), calls=%async_computation.1 | async-start | bytes 327680 | tf_op jit(solution)/shard_map/all_to_all | solution.py:395
  25.4 0.7 %copy-start.3 = (bf16[80,2048]{1,0:T(8,128)(2,1)}, bf16[80,2048]{1,0:T(8,128)(2,1)S(1)}, u32[]{:S(2)}) copy-start(bf16[80,2048]{1,0:T(8,128)(2,1)S(1)} %collective-permute-done.2.tails_ref) | copy-start | bytes 983044
  26.2 1.0 %copy-start.4 = (bf16[80,2048]{1,0:T(8,128)(2,1)S(1)}, bf16[80,2048]{1,0:T(8,128)(2,1)}, u32[]{:S(2)}) copy-start(bf16[80,2048]{1,0:T(8,128)(2,1)} %copy-done.3) | copy-start | bytes 983044
  30.4 1.4 %collective-permute-start.3 = (bf16[640,128]{1,0:T(8,128)(2,1)S(1)}, bf16[640,128]{1,0:T(8,128)(2,1)S(1)}, u32[]{:S(2)}, u32[]{:S(2)}) collective-permute-start(bf16[640,128]{1,0:T(8,128)(2,1)S(1)} %bitcast.1), channel_id=1, source_target_pairs={{0,1},{1,0},{2,3},{3,2},{4,5},{5,4},{6,7},{7,6},{8,9},{9,8},{10,11... | collective-permute-start | bytes 491528 | tf_op jit(solution)/shard_map/ppermute | solution.py:391

commit v8 on v7

--- a/solution.py
+++ b/solution.py
@@ -16,7 +16,7 @@
 WINDOW = 64
 
 BLOCK = "block"
-ORDER_SEED = 24
+ORDER_SEED = 81
 LANES = 128
 PAIRS = HEADS // 2
 QUADS = FEAT * (FEAT + 1) // 2

time: 33.8 us -> 33 us (0.976)
  starting transfers between devices: 17.4 us -> 16.7 us
    all_to_all x2, starting transfers between devices: 15.5 us -> 14.8 us  [exchange(): lax.all_to_all(array, BLOCK, 0, 0, axis_index_groups=groups, tiled=True)]
  transfers between devices with their start and end apart: 6 -> 6, of which waited for: 4 -> 4; matrix products, arithmetic and copies ran while one was open for 0% -> 0% of each run, Pallas kernels for 17% -> 18%
where the time goes in v8:
time: 33 us; the launch traced here: 32.7 us
  starting transfers between devices  16.7 us (51%)
  Pallas kernels  8.6 us (26%)
  waiting for transfers between devices  5.6 us (17%)
  local copies, waits for them, and re-layouts  1.69 us (5%)
    all_to_all x2, starting transfers between devices, exchange(): lax.all_to_all(array, BLOCK, 0, 0, axis_index_groups=groups, tiled=True)  14.8 us
    pallas_call x6, Pallas kernels, call(): pl.pallas_call(kernel, out_shape=results, in_specs=specs, out_specs=out_s...  8.6 us
    all_to_all x2, waiting for transfers between devices, exchange(): lax.all_to_all(array, BLOCK, 0, 0, axis_index_groups=groups, tiled=True)  5.14 us
    unnamed x12, local copies, waits for them, and re-layouts  1.69 us
    ppermute x1, starting transfers between devices, shards(): lax.ppermute(tails, BLOCK, [(i, i + 1) for i in range(2 * chips - 1)])  1.44 us
  transfers between devices with their start and end apart: 6, of which 4 were waited for; matrix products, arithmetic and copies ran while one was open for 0% of the time, Pallas kernels for 18%

profile of v8, /device:TPU:0, one launch (start us, length us, event | category | flops | bytes accessed | tf_op | source)
XLA Modules:
  0.0 32.7 jit_solution(8012062939256183048)
XLA Ops:
  0.0 0.5 %collective-permute-start.1 = (bf16[128,1024]{1,0:T(8,128)(2,1)}, bf16[128,1024]{1,0:T(8,128)(2,1)S(1)}, u32[]{:S(2)}, u32[]{:S(2)}) collective-permute-start(bf16[128,1024]{1,0:T(8,128)(2,1)} %v_ref.1), channel_id=1, source_target_pairs={{0,1},{1,0},{2,3},{3,2},{4,5},{5,4},{6,7},{7,6},{8,9},{9,8},{10,11... | collective-permute-start | bytes 786440 | tf_op jit(solution)/shard_map/ppermute | solution.py:391
  0.5 0.1 collective-permute-start
  0.5 1.4 %shard_map.46 = (f32[16,48,128]{2,1,0:T(8,128)S(1)}, bf16[80,2048]{1,0:T(8,128)(2,1)S(1)}, f32[3,512]{1,0:T(4,128)S(1)}) custom-call(bf16[128,512]{1,0:T(8,128)(2,1)} %qk_ref.5, bf16[128,1024]{1,0:T(8,128)(2,1)} %v_ref.1, f32[3,1024]{1,0:T(4,128)} %conv_ref.1, bf16[128,3072]{1,0:T(8,128)(2,1)} %swa_ref.1), custom_call_target="tpu_custom_call" | custom-call | tf_op jit(solution)/shard_map/pallas_call | solution.py:372
  1.9 0.1 collective-permute-done.refs_0_.other_qk_ref
  2.0 0.0 collective-permute-done.1.refs_1_.other_v_ref
  2.0 0.0 copy-start.2
  2.0 1.2 %shard_map.47 = bf16[16,48,128]{2,1,0:T(8,128)(2,1)} custom-call(bf16[128,512]{1,0:T(8,128)(2,1)S(1)} %collective-permute-done.refs_0_.other_qk_ref, bf16[128,1024]{1,0:T(8,128)(2,1)S(1)} %collective-permute-done.1.refs_1_.other_v_ref, f32[3,512]{1,0:T(4,128)S(1)} %get-tuple-element.17.refs_2_, f32[16,48,128]{2,1,0:T(8,128)S(1)} %get-tuple-element.18.refs_3_), custom_call_target="tpu_custom_call" | custom-call | tf_op jit(solution)/shard_map/pallas_call | solution.py:372
  3.2 0.0 copy-start
  3.2 8.9 %all-to-all-start = ((bf16[16,48,128]{2,1,0:T(8,128)(2,1)}), bf16[16,48,128]{2,1,0:T(8,128)(2,1)S(1)}, u32[]{:S(2)}, u32[]{:S(2)}) async-start(bf16[16,48,128]{2,1,0:T(8,128)(2,1)} %shard_map.47), calls=%async_computation | async-start | bytes 393216 | tf_op jit(solution)/shard_map/all_to_all | solution.py:395
  12.1 1.4 %collective-permute-start.2 = (bf16[80,2048]{1,0:T(8,128)(2,1)S(1)}, bf16[80,2048]{1,0:T(8,128)(2,1)S(1)}, u32[]{:S(2)}, u32[]{:S(2)}) collective-permute-start(bf16[80,2048]{1,0:T(8,128)(2,1)S(1)} %get-tuple-element.21), channel_id=1, source_target_pairs={{0,1},{1,2},{2,3},{3,4},{4,5},{5,6},{6,7},{7,8},{8,9},{9,10},{10,1... | collective-permute-start | bytes 983048 | tf_op jit(solution)/shard_map/ppermute | solution.py:424
  13.5 4.5 %all-to-all-done.parts_ref = bf16[16,48,128]{2,1,0:T(8,128)(2,1)S(1)} async-done(((bf16[16,48,128]{2,1,0:T(8,128)(2,1)}), bf16[16,48,128]{2,1,0:T(8,128)(2,1)S(1)}, u32[]{:S(2)}, u32[]{:S(2)}) %all-to-all-start) | async-done | bytes 196640 | tf_op jit(solution)/shard_map/all_to_all | solution.py:395
  18.1 1.2 %shard_map.48 = bf16[16,40,128]{2,1,0:T(8,128)(2,1)} custom-call(bf16[16,48,128]{2,1,0:T(8,128)(2,1)S(1)} %all-to-all-done.parts_ref), custom_call_target="tpu_custom_call" | custom-call | tf_op jit(solution)/shard_map/pallas_call | solution.py:372
  19.3 0.0 copy-start.1
  19.3 0.0 copy-start.5
  19.3 5.9 %all-to-all-start.1 = ((bf16[16,40,128]{2,1,0:T(8,128)(2,1)}), bf16[16,40,128]{2,1,0:T(8,128)(2,1)S(1)}, u32[]{:S(2)}, u32[]{:S(2)}) async-start(bf16[16,40,128]{2,1,0:T(8,128)(2,1)} %shard_map.48), calls=%async_computation.1 | async-start | bytes 327680 | tf_op jit(solution)/shard_map/all_to_all | solution.py:395
  25.2 0.0 collective-permute-done.2.tails_ref
  25.2 0.0 copy-start.3
  25.2 0.7 %copy-done.3 = bf16[80,2048]{1,0:T(8,128)(2,1)} copy-done((bf16[80,2048]{1,0:T(8,128)(2,1)}, bf16[80,2048]{1,0:T(8,128)(2,1)S(1)}, u32[]{:S(2)}) %copy-start.3) | copy-done | bytes 327704
  25.9 0.0 copy-done.2
  25.9 0.0 copy-done
  25.9 0.0 copy-done.1
  25.9 0.0 copy-done.5
  25.9 0.0 copy-start.4
  25.9 1.0 %copy-done.4 = bf16[80,2048]{1,0:T(8,128)(2,1)S(1)} copy-done((bf16[80,2048]{1,0:T(8,128)(2,1)S(1)}, bf16[80,2048]{1,0:T(8,128)(2,1)}, u32[]{:S(2)}) %copy-start.4) | copy-done | bytes 327704
  26.9 2.1 %shard_map.49 = (f32[128,1024]{1,0:T(8,128)S(1)}, f32[128,1024]{1,0:T(8,128)S(1)}, f32[128,1024]{1,0:T(8,128)S(1)}) custom-call(bf16[128,512]{1,0:T(8,128)(2,1)S(1)} %copy-done.1, bf16[128,1024]{1,0:T(8,128)(2,1)S(1)} %copy-done.2, f32[3,1024]{1,0:T(4,128)S(1)} %copy-done.5, bf16[128,3072]{1,0:T(8,128)(2,1)S(1)} %copy-done, bf16[80,2048]{1,0:T(8,128)(2,1)S(1)} %copy-done.4, ...), custom_call_target="tpu_custom_call" | custom-call | tf_op jit(solution)/shard_map/pallas_call | solution.py:372
  29.0 0.6 %all-to-all-done.1 = bf16[16,40,128]{2,1,0:T(8,128)(2,1)S(1)} async-done(((bf16[16,40,128]{2,1,0:T(8,128)(2,1)}), bf16[16,40,128]{2,1,0:T(8,128)(2,1)S(1)}, u32[]{:S(2)}, u32[]{:S(2)}) %all-to-all-start.1) | async-done | bytes 163872 | tf_op jit(solution)/shard_map/all_to_all | solution.py:395
  29.6 0.0 collective-permute-start.3
  29.6 1.0 %shard_map.50.refs_0_ = bf16[128,512]{1,0:T(8,128)(2,1)S(1)} custom-call(bf16[128,512]{1,0:T(8,128)(2,1)S(1)} %copy-done.1, f32[128,1024]{1,0:T(8,128)S(1)} %get-tuple-element.25.numer_ref, f32[128,1024]{1,0:T(8,128)S(1)} %get-tuple-element.26.denom_ref, f32[128,1024]{1,0:T(8,128)S(1)} %get-tuple-element.27.swa_ref, bf16[640,128]{1,0:T(8,128)(2,1)S(1)} %bitcast.2), custom_call_target="tpu_custom_call" | custom-call | tf_op jit(solution)/shard_map/pallas_call | solution.py:372
  30.6 0.4 %collective-permute-done.3.past_ref = bf16[640,128]{1,0:T(8,128)(2,1)S(1)} collective-permute-done((bf16[640,128]{1,0:T(8,128)(2,1)S(1)}, bf16[640,128]{1,0:T(8,128)(2,1)S(1)}, u32[]{:S(2)}, u32[]{:S(2)}) %collective-permute-start.3) | collective-permute-done | bytes 163872 | tf_op jit(solution)/shard_map/ppermute | solution.py:391
  31.0 1.7 %shard_map.51 = bf16[128,1024]{1,0:T(8,128)(2,1)} custom-call(bf16[128,512]{1,0:T(8,128)(2,1)S(1)} %copy-done.1, f32[128,1024]{1,0:T(8,128)S(1)} %get-tuple-element.25.numer_ref, f32[128,1024]{1,0:T(8,128)S(1)} %get-tuple-element.26.denom_ref, f32[128,1024]{1,0:T(8,128)S(1)} %get-tuple-element.27.swa_ref, ...), custom_call_target="tpu_custom_call" | custom-call | tf_op jit(solution)/shard_map/pallas_call | solution.py:372
Async XLA Ops:
  0.0 2.0 %collective-permute-start.1 = (bf16[128,1024]{1,0:T(8,128)(2,1)}, bf16[128,1024]{1,0:T(8,128)(2,1)S(1)}, u32[]{:S(2)}, u32[]{:S(2)}) collective-permute-start(bf16[128,1024]{1,0:T(8,128)(2,1)} %v_ref.1), channel_id=1, source_target_pairs={{0,1},{1,0},{2,3},{3,2},{4,5},{5,4},{6,7},{7,6},{8,9},{9,8},{10,11... | collective-permute-start | bytes 786440 | tf_op jit(solution)/shard_map/ppermute | solution.py:391
  0.5 1.6 %collective-permute-start = (bf16[128,512]{1,0:T(8,128)(2,1)}, bf16[128,512]{1,0:T(8,128)(2,1)S(1)}, u32[]{:S(2)}, u32[]{:S(2)}) collective-permute-start(bf16[128,512]{1,0:T(8,128)(2,1)} %qk_ref.5), channel_id=1, source_target_pairs={{0,1},{1,0},{2,3},{3,2},{4,5},{5,4},{6,7},{7,6},{8,9},{9,8},{10,11... | collective-permute-start | bytes 393224 | tf_op jit(solution)/shard_map/ppermute | solution.py:391
  2.0 23.9 %copy-start.2 = (bf16[128,1024]{1,0:T(8,128)(2,1)S(1)}, bf16[128,1024]{1,0:T(8,128)(2,1)}, u32[]{:S(2)}) copy-start(bf16[128,1024]{1,0:T(8,128)(2,1)} %v_ref.1) | copy-start | bytes 786436
  3.2 22.7 %copy-start = (bf16[128,3072]{1,0:T(8,128)(2,1)S(1)}, bf16[128,3072]{1,0:T(8,128)(2,1)}, u32[]{:S(2)}) copy-start(bf16[128,3072]{1,0:T(8,128)(2,1)} %swa_ref.1) | copy-start | bytes 2359300
  3.2 14.9 %all-to-all-start = ((bf16[16,48,128]{2,1,0:T(8,128)(2,1)}), bf16[16,48,128]{2,1,0:T(8,128)(2,1)S(1)}, u32[]{:S(2)}, u32[]{:S(2)}) async-start(bf16[16,48,128]{2,1,0:T(8,128)(2,1)} %shard_map.47), calls=%async_computation | async-start | bytes 393216 | tf_op jit(solution)/shard_map/all_to_all | solution.py:395
  12.1 13.1 %collective-permute-start.2 = (bf16[80,2048]{1,0:T(8,128)(2,1)S(1)}, bf16[80,2048]{1,0:T(8,128)(2,1)S(1)}, u32[]{:S(2)}, u32[]{:S(2)}) collective-permute-start(bf16[80,2048]{1,0:T(8,128)(2,1)S(1)} %get-tuple-element.21), channel_id=1, source_target_pairs={{0,1},{1,2},{2,3},{3,4},{4,5},{5,6},{6,7},{7,8},{8,9},{9,10},{10,1... | collective-permute-start | bytes 983048 | tf_op jit(solution)/shard_map/ppermute | solution.py:424
  19.3 6.6 %copy-start.1 = (bf16[128,512]{1,0:T(8,128)(2,1)S(1)}, bf16[128,512]{1,0:T(8,128)(2,1)}, u32[]{:S(2)}) copy-start(bf16[128,512]{1,0:T(8,128)(2,1)} %qk_ref.5) | copy-start | bytes 393220
  19.3 6.6 %copy-start.5 = (f32[3,1024]{1,0:T(4,128)S(1)}, f32[3,1024]{1,0:T(4,128)}, u32[]{:S(2)}) copy-start(f32[3,1024]{1,0:T(4,128)} %conv_ref.1) | copy-start | bytes 36868
  19.3 10.3 %all-to-all-start.1 = ((bf16[16,40,128]{2,1,0:T(8,128)(2,1)}), bf16[16,40,128]{2,1,0:T(8,128)(2,1)S(1)}, u32[]{:S(2)}, u32[]{:S(2)}) async-start(bf16[16,40,128]{2,1,0:T(8,128)(2,1)} %shard_map.48), calls=%async_computation.1 | async-start | bytes 327680 | tf_op jit(solution)/shard_map/all_to_all | solution.py:395
  25.2 0.7 %copy-start.3 = (bf16[80,2048]{1,0:T(8,128)(2,1)}, bf16[80,2048]{1,0:T(8,128)(2,1)S(1)}, u32[]{:S(2)}) copy-start(bf16[80,2048]{1,0:T(8,128)(2,1)S(1)} %collective-permute-done.2.tails_ref) | copy-start | bytes 983044
  25.9 1.0 %copy-start.4 = (bf16[80,2048]{1,0:T(8,128)(2,1)S(1)}, bf16[80,2048]{1,0:T(8,128)(2,1)}, u32[]{:S(2)}) copy-start(bf16[80,2048]{1,0:T(8,128)(2,1)} %copy-done.3) | copy-start | bytes 983044
  29.6 1.4 %collective-permute-start.3 = (bf16[640,128]{1,0:T(8,128)(2,1)S(1)}, bf16[640,128]{1,0:T(8,128)(2,1)S(1)}, u32[]{:S(2)}, u32[]{:S(2)}) collective-permute-start(bf16[640,128]{1,0:T(8,128)(2,1)S(1)} %bitcast.1), channel_id=1, source_target_pairs={{0,1},{1,0},{2,3},{3,2},{4,5},{5,4},{6,7},{7,6},{8,9},{9,8},{10,11... | collective-permute-start | bytes 491528 | tf_op jit(solution)/shard_map/ppermute | solution.py:391

commit v9 on v8

--- a/solution.py
+++ b/solution.py
@@ -203,23 +203,27 @@
     )
     extras_low = extras.astype(BF16)
     upper = iota((width, LANES), 1) >= VHEAD
+    heads = [lane // FEAT == head + place for place in range(2)]
+    factors = [jnp.where(mine, factor, 0.0) for factor in (one, two) for mine in heads]
+    products = dot(jnp.concatenate(factors, axis=0).astype(BF16), extras_low, NT)
     lefts = []
     rights = []
-    for place in range(2):
-        mine = lane // FEAT == head + place
-        first = dot(jnp.where(mine, one, 0.0).astype(BF16), extras_low, NT) + add_one
-        second = dot(jnp.where(mine, two, 0.0).astype(BF16), extras_low, NT) + add_two
+    for side in range(2):
+        first = products[side * padded : (side + 1) * padded] + add_one
+        second = products[(side + 2) * padded : (side + 3) * padded] + add_two
         lefts.append(pltpu.roll(first * second, width - BLOCK_EXTRA - (taps - 1), 1))
-        rights.append(jnp.where(upper == (place == 1), extras, 0.0).astype(BF16))
+        rights.append(jnp.where(upper == (side == 1), extras, 0.0).astype(BF16))
     left = jnp.concatenate(lefts, axis=1)
     right = jnp.concatenate(rights, axis=0)
     column = iota(left.shape, 1) % width
     to_block = jnp.where(column % BLOCK_EXTRA < taps - 1, column // BLOCK_EXTRA + 1, 2 * chips)
 
+    seen = [jnp.where(to_block <= 2 * chip, left, 0.0).astype(BF16) for chip in range(chips)]
+    added = dot(jnp.concatenate(seen, axis=0), right)
     total = jnp.zeros((padded, LANES), jnp.float32)
     for chip, at in enumerate(places):
-        seen = jnp.where(to_block <= 2 * chip, left, 0.0).astype(BF16)
-        out_ref[int(at)] = (total + dot(seen, right))[:part].astype(BF16)
+        result = total + added[chip * padded : (chip + 1) * padded]
+        out_ref[int(at)] = result[:part].astype(BF16)
         total = total + parts_ref[int(at)].astype(jnp.float32)[:padded]
 
 

time: 33 us -> 33 us (level)
  no operation moved by 1% of the time
where the time goes in v9:
time: 33 us; the launch traced here: 32.6 us
  starting transfers between devices  16.7 us (51%)
  Pallas kernels  8.58 us (26%)
  waiting for transfers between devices  5.6 us (17%)
  local copies, waits for them, and re-layouts  1.69 us (5%)
    all_to_all x2, starting transfers between devices, exchange(): lax.all_to_all(array, BLOCK, 0, 0, axis_index_groups=groups, tiled=True)  14.8 us
    pallas_call x6, Pallas kernels, call(): pl.pallas_call(kernel, out_shape=results, in_specs=specs, out_specs=out_s...  8.58 us
    all_to_all x2, waiting for transfers between devices, exchange(): lax.all_to_all(array, BLOCK, 0, 0, axis_index_groups=groups, tiled=True)  5.14 us
    unnamed x12, local copies, waits for them, and re-layouts  1.69 us
    ppermute x1, starting transfers between devices, shards(): lax.ppermute(tails, BLOCK, [(i, i + 1) for i in range(2 * chips - 1)])  1.44 us
  transfers between devices with their start and end apart: 6, of which 4 were waited for; matrix products, arithmetic and copies ran while one was open for 0% of the time, Pallas kernels for 18%

profile of v9, /device:TPU:0, one launch (start us, length us, event | category | flops | bytes accessed | tf_op | source)
XLA Modules:
  0.0 32.6 jit_solution(17668333772244788226)
XLA Ops:
  0.0 0.5 %collective-permute-start.1 = (bf16[128,1024]{1,0:T(8,128)(2,1)}, bf16[128,1024]{1,0:T(8,128)(2,1)S(1)}, u32[]{:S(2)}, u32[]{:S(2)}) collective-permute-start(bf16[128,1024]{1,0:T(8,128)(2,1)} %v_ref.1), channel_id=1, source_target_pairs={{0,1},{1,0},{2,3},{3,2},{4,5},{5,4},{6,7},{7,6},{8,9},{9,8},{10,11... | collective-permute-start | bytes 786440 | tf_op jit(solution)/shard_map/ppermute | solution.py:395
  0.5 0.1 collective-permute-start
  0.5 1.4 %shard_map.46 = (f32[16,48,128]{2,1,0:T(8,128)S(1)}, bf16[80,2048]{1,0:T(8,128)(2,1)S(1)}, f32[3,512]{1,0:T(4,128)S(1)}) custom-call(bf16[128,512]{1,0:T(8,128)(2,1)} %qk_ref.5, bf16[128,1024]{1,0:T(8,128)(2,1)} %v_ref.1, f32[3,1024]{1,0:T(4,128)} %conv_ref.1, bf16[128,3072]{1,0:T(8,128)(2,1)} %swa_ref.1), custom_call_target="tpu_custom_call" | custom-call | tf_op jit(solution)/shard_map/pallas_call | solution.py:376
  1.9 0.1 collective-permute-done.refs_0_.other_qk_ref
  2.0 0.0 collective-permute-done.1.refs_1_.other_v_ref
  2.0 0.0 copy-start.2
  2.0 1.2 %shard_map.47 = bf16[16,48,128]{2,1,0:T(8,128)(2,1)} custom-call(bf16[128,512]{1,0:T(8,128)(2,1)S(1)} %collective-permute-done.refs_0_.other_qk_ref, bf16[128,1024]{1,0:T(8,128)(2,1)S(1)} %collective-permute-done.1.refs_1_.other_v_ref, f32[3,512]{1,0:T(4,128)S(1)} %get-tuple-element.17.refs_2_, f32[16,48,128]{2,1,0:T(8,128)S(1)} %get-tuple-element.18.refs_3_), custom_call_target="tpu_custom_call" | custom-call | tf_op jit(solution)/shard_map/pallas_call | solution.py:376
  3.2 0.0 copy-start
  3.2 8.9 %all-to-all-start = ((bf16[16,48,128]{2,1,0:T(8,128)(2,1)}), bf16[16,48,128]{2,1,0:T(8,128)(2,1)S(1)}, u32[]{:S(2)}, u32[]{:S(2)}) async-start(bf16[16,48,128]{2,1,0:T(8,128)(2,1)} %shard_map.47), calls=%async_computation | async-start | bytes 393216 | tf_op jit(solution)/shard_map/all_to_all | solution.py:399
  12.1 1.4 %collective-permute-start.2 = (bf16[80,2048]{1,0:T(8,128)(2,1)S(1)}, bf16[80,2048]{1,0:T(8,128)(2,1)S(1)}, u32[]{:S(2)}, u32[]{:S(2)}) collective-permute-start(bf16[80,2048]{1,0:T(8,128)(2,1)S(1)} %get-tuple-element.21), channel_id=1, source_target_pairs={{0,1},{1,2},{2,3},{3,4},{4,5},{5,6},{6,7},{7,8},{8,9},{9,10},{10,1... | collective-permute-start | bytes 983048 | tf_op jit(solution)/shard_map/ppermute | solution.py:428
  13.5 4.5 %all-to-all-done.parts_ref = bf16[16,48,128]{2,1,0:T(8,128)(2,1)S(1)} async-done(((bf16[16,48,128]{2,1,0:T(8,128)(2,1)}), bf16[16,48,128]{2,1,0:T(8,128)(2,1)S(1)}, u32[]{:S(2)}, u32[]{:S(2)}) %all-to-all-start) | async-done | bytes 196640 | tf_op jit(solution)/shard_map/all_to_all | solution.py:399
  18.1 1.2 %shard_map.48 = bf16[16,40,128]{2,1,0:T(8,128)(2,1)} custom-call(bf16[16,48,128]{2,1,0:T(8,128)(2,1)S(1)} %all-to-all-done.parts_ref), custom_call_target="tpu_custom_call" | custom-call | tf_op jit(solution)/shard_map/pallas_call | solution.py:376
  19.3 0.0 copy-start.1
  19.3 0.0 copy-start.5
  19.3 5.9 %all-to-all-start.1 = ((bf16[16,40,128]{2,1,0:T(8,128)(2,1)}), bf16[16,40,128]{2,1,0:T(8,128)(2,1)S(1)}, u32[]{:S(2)}, u32[]{:S(2)}) async-start(bf16[16,40,128]{2,1,0:T(8,128)(2,1)} %shard_map.48), calls=%async_computation.1 | async-start | bytes 327680 | tf_op jit(solution)/shard_map/all_to_all | solution.py:399
  25.1 0.0 collective-permute-done.2.tails_ref
  25.1 0.0 copy-start.3
  25.2 0.7 %copy-done.3 = bf16[80,2048]{1,0:T(8,128)(2,1)} copy-done((bf16[80,2048]{1,0:T(8,128)(2,1)}, bf16[80,2048]{1,0:T(8,128)(2,1)S(1)}, u32[]{:S(2)}) %copy-start.3) | copy-done | bytes 327704
  25.9 0.0 copy-done.2
  25.9 0.0 copy-done
  25.9 0.0 copy-done.1
  25.9 0.0 copy-done.5
  25.9 0.0 copy-start.4
  25.9 1.0 %copy-done.4 = bf16[80,2048]{1,0:T(8,128)(2,1)S(1)} copy-done((bf16[80,2048]{1,0:T(8,128)(2,1)S(1)}, bf16[80,2048]{1,0:T(8,128)(2,1)}, u32[]{:S(2)}) %copy-start.4) | copy-done | bytes 327704
  26.9 2.1 %shard_map.49 = (f32[128,1024]{1,0:T(8,128)S(1)}, f32[128,1024]{1,0:T(8,128)S(1)}, f32[128,1024]{1,0:T(8,128)S(1)}) custom-call(bf16[128,512]{1,0:T(8,128)(2,1)S(1)} %copy-done.1, bf16[128,1024]{1,0:T(8,128)(2,1)S(1)} %copy-done.2, f32[3,1024]{1,0:T(4,128)S(1)} %copy-done.5, bf16[128,3072]{1,0:T(8,128)(2,1)S(1)} %copy-done, bf16[80,2048]{1,0:T(8,128)(2,1)S(1)} %copy-done.4, ...), custom_call_target="tpu_custom_call" | custom-call | tf_op jit(solution)/shard_map/pallas_call | solution.py:376
  29.0 0.6 %all-to-all-done.1 = bf16[16,40,128]{2,1,0:T(8,128)(2,1)S(1)} async-done(((bf16[16,40,128]{2,1,0:T(8,128)(2,1)}), bf16[16,40,128]{2,1,0:T(8,128)(2,1)S(1)}, u32[]{:S(2)}, u32[]{:S(2)}) %all-to-all-start.1) | async-done | bytes 163872 | tf_op jit(solution)/shard_map/all_to_all | solution.py:399
  29.6 0.0 collective-permute-start.3
  29.6 1.0 %shard_map.50.refs_0_ = bf16[128,512]{1,0:T(8,128)(2,1)S(1)} custom-call(bf16[128,512]{1,0:T(8,128)(2,1)S(1)} %copy-done.1, f32[128,1024]{1,0:T(8,128)S(1)} %get-tuple-element.25.numer_ref, f32[128,1024]{1,0:T(8,128)S(1)} %get-tuple-element.26.denom_ref, f32[128,1024]{1,0:T(8,128)S(1)} %get-tuple-element.27.swa_ref, bf16[640,128]{1,0:T(8,128)(2,1)S(1)} %bitcast.2), custom_call_target="tpu_custom_call" | custom-call | tf_op jit(solution)/shard_map/pallas_call | solution.py:376
  30.6 0.4 %collective-permute-done.3.past_ref = bf16[640,128]{1,0:T(8,128)(2,1)S(1)} collective-permute-done((bf16[640,128]{1,0:T(8,128)(2,1)S(1)}, bf16[640,128]{1,0:T(8,128)(2,1)S(1)}, u32[]{:S(2)}, u32[]{:S(2)}) %collective-permute-start.3) | collective-permute-done | bytes 163872 | tf_op jit(solution)/shard_map/ppermute | solution.py:395
  31.0 1.7 %shard_map.51 = bf16[128,1024]{1,0:T(8,128)(2,1)} custom-call(bf16[128,512]{1,0:T(8,128)(2,1)S(1)} %copy-done.1, f32[128,1024]{1,0:T(8,128)S(1)} %get-tuple-element.25.numer_ref, f32[128,1024]{1,0:T(8,128)S(1)} %get-tuple-element.26.denom_ref, f32[128,1024]{1,0:T(8,128)S(1)} %get-tuple-element.27.swa_ref, ...), custom_call_target="tpu_custom_call" | custom-call | tf_op jit(solution)/shard_map/pallas_call | solution.py:376
Async XLA Ops:
  0.0 2.0 %collective-permute-start.1 = (bf16[128,1024]{1,0:T(8,128)(2,1)}, bf16[128,1024]{1,0:T(8,128)(2,1)S(1)}, u32[]{:S(2)}, u32[]{:S(2)}) collective-permute-start(bf16[128,1024]{1,0:T(8,128)(2,1)} %v_ref.1), channel_id=1, source_target_pairs={{0,1},{1,0},{2,3},{3,2},{4,5},{5,4},{6,7},{7,6},{8,9},{9,8},{10,11... | collective-permute-start | bytes 786440 | tf_op jit(solution)/shard_map/ppermute | solution.py:395
  0.5 1.6 %collective-permute-start = (bf16[128,512]{1,0:T(8,128)(2,1)}, bf16[128,512]{1,0:T(8,128)(2,1)S(1)}, u32[]{:S(2)}, u32[]{:S(2)}) collective-permute-start(bf16[128,512]{1,0:T(8,128)(2,1)} %qk_ref.5), channel_id=1, source_target_pairs={{0,1},{1,0},{2,3},{3,2},{4,5},{5,4},{6,7},{7,6},{8,9},{9,8},{10,11... | collective-permute-start | bytes 393224 | tf_op jit(solution)/shard_map/ppermute | solution.py:395
  2.0 23.8 %copy-start.2 = (bf16[128,1024]{1,0:T(8,128)(2,1)S(1)}, bf16[128,1024]{1,0:T(8,128)(2,1)}, u32[]{:S(2)}) copy-start(bf16[128,1024]{1,0:T(8,128)(2,1)} %v_ref.1) | copy-start | bytes 786436
  3.2 22.7 %copy-start = (bf16[128,3072]{1,0:T(8,128)(2,1)S(1)}, bf16[128,3072]{1,0:T(8,128)(2,1)}, u32[]{:S(2)}) copy-start(bf16[128,3072]{1,0:T(8,128)(2,1)} %swa_ref.1) | copy-start | bytes 2359300
  3.2 14.9 %all-to-all-start = ((bf16[16,48,128]{2,1,0:T(8,128)(2,1)}), bf16[16,48,128]{2,1,0:T(8,128)(2,1)S(1)}, u32[]{:S(2)}, u32[]{:S(2)}) async-start(bf16[16,48,128]{2,1,0:T(8,128)(2,1)} %shard_map.47), calls=%async_computation | async-start | bytes 393216 | tf_op jit(solution)/shard_map/all_to_all | solution.py:399
  12.1 13.1 %collective-permute-start.2 = (bf16[80,2048]{1,0:T(8,128)(2,1)S(1)}, bf16[80,2048]{1,0:T(8,128)(2,1)S(1)}, u32[]{:S(2)}, u32[]{:S(2)}) collective-permute-start(bf16[80,2048]{1,0:T(8,128)(2,1)S(1)} %get-tuple-element.21), channel_id=1, source_target_pairs={{0,1},{1,2},{2,3},{3,4},{4,5},{5,6},{6,7},{7,8},{8,9},{9,10},{10,1... | collective-permute-start | bytes 983048 | tf_op jit(solution)/shard_map/ppermute | solution.py:428
  19.3 6.6 %copy-start.1 = (bf16[128,512]{1,0:T(8,128)(2,1)S(1)}, bf16[128,512]{1,0:T(8,128)(2,1)}, u32[]{:S(2)}) copy-start(bf16[128,512]{1,0:T(8,128)(2,1)} %qk_ref.5) | copy-start | bytes 393220
  19.3 6.6 %copy-start.5 = (f32[3,1024]{1,0:T(4,128)S(1)}, f32[3,1024]{1,0:T(4,128)}, u32[]{:S(2)}) copy-start(f32[3,1024]{1,0:T(4,128)} %conv_ref.1) | copy-start | bytes 36868
  19.3 10.3 %all-to-all-start.1 = ((bf16[16,40,128]{2,1,0:T(8,128)(2,1)}), bf16[16,40,128]{2,1,0:T(8,128)(2,1)S(1)}, u32[]{:S(2)}, u32[]{:S(2)}) async-start(bf16[16,40,128]{2,1,0:T(8,128)(2,1)} %shard_map.48), calls=%async_computation.1 | async-start | bytes 327680 | tf_op jit(solution)/shard_map/all_to_all | solution.py:399
  25.1 0.7 %copy-start.3 = (bf16[80,2048]{1,0:T(8,128)(2,1)}, bf16[80,2048]{1,0:T(8,128)(2,1)S(1)}, u32[]{:S(2)}) copy-start(bf16[80,2048]{1,0:T(8,128)(2,1)S(1)} %collective-permute-done.2.tails_ref) | copy-start | bytes 983044
  25.9 1.0 %copy-start.4 = (bf16[80,2048]{1,0:T(8,128)(2,1)S(1)}, bf16[80,2048]{1,0:T(8,128)(2,1)}, u32[]{:S(2)}) copy-start(bf16[80,2048]{1,0:T(8,128)(2,1)} %copy-done.3) | copy-start | bytes 983044
  29.6 1.4 %collective-permute-start.3 = (bf16[640,128]{1,0:T(8,128)(2,1)S(1)}, bf16[640,128]{1,0:T(8,128)(2,1)S(1)}, u32[]{:S(2)}, u32[]{:S(2)}) collective-permute-start(bf16[640,128]{1,0:T(8,128)(2,1)S(1)} %bitcast.1), channel_id=1, source_target_pairs={{0,1},{1,0},{2,3},{3,2},{4,5},{5,4},{6,7},{7,6},{8,9},{9,8},{10,11... | collective-permute-start | bytes 491528 | tf_op jit(solution)/shard_map/ppermute | solution.py:395

commit v10 on v9

--- a/solution.py
+++ b/solution.py
@@ -340,8 +340,9 @@
             norm = jnp.concatenate([last[at : at + 1], last[at + 1 : at + 2, : ROWS - LANES]], axis=1)
             norms.append(jnp.broadcast_to(norm, (8, ROWS)))
     norms = jnp.concatenate(norms + [jnp.zeros((LANES // 2, ROWS), jnp.float32)], axis=0).T.astype(BF16)
-    source = iota((LANES, LANES), 0)
-    target = iota((LANES, LANES), 1)
+    source = iota((LANES, wide), 0)
+    target = iota((LANES, wide), 1)
+    spreads = dot(norms, jnp.where(source == target // VHEAD * 8, 1.0, 0.0).astype(BF16)).astype(BF16)
     own_heads = [
         jnp.where(head_mask(head, query.shape), query, jnp.zeros_like(query)) for head in range(HEADS // 2)
     ]
@@ -349,8 +350,7 @@
     high, low = hi_lo((dot(stacked, one) + add_one) * (dot(stacked, two) + add_two))
     for pair in range(PAIRS // 2):
         here = pl.ds(pl.multiple_of(half * wide + pair * LANES, LANES), LANES)
-        wanted = jnp.where(target < VHEAD, 16 * pair, 16 * pair + 8)
-        spread = dot(norms, jnp.where(source == wanted, 1.0, 0.0).astype(BF16)).astype(BF16)
+        spread = spreads[:, pair * LANES : (pair + 1) * LANES]
         right = jnp.concatenate([past_ref[pair * ROWS : (pair + 1) * ROWS, :], spread], axis=1)
         mine = slice(2 * pair * rows, (2 * pair + 2) * rows)
         result = dot(high[mine], right) + dot(low[mine], right)

time: 33 us -> 32.8 us (level)
  Pallas kernels: 8.58 us -> 8.22 us
    pallas_call x6, Pallas kernels: 8.58 us -> 8.22 us  [call(): pl.pallas_call(kernel, out_shape=results, in_specs=specs, out_specs=out_s...]
  transfers between devices with their start and end apart: 6 -> 6, of which waited for: 4 -> 4; matrix products, arithmetic and copies ran while one was open for 0% -> 0% of each run, Pallas kernels for 18% -> 17%
where the time goes in v10:
time: 32.8 us; the launch traced here: 32.5 us
  starting transfers between devices  16.7 us (51%)
  Pallas kernels  8.22 us (25%)
  waiting for transfers between devices  5.78 us (18%)
  local copies, waits for them, and re-layouts  1.69 us (5%)
    all_to_all x2, starting transfers between devices, exchange(): lax.all_to_all(array, BLOCK, 0, 0, axis_index_groups=groups, tiled=True)  14.8 us
    pallas_call x6, Pallas kernels, call(): pl.pallas_call(kernel, out_shape=results, in_specs=specs, out_specs=out_s...  8.22 us
    all_to_all x2, waiting for transfers between devices, exchange(): lax.all_to_all(array, BLOCK, 0, 0, axis_index_groups=groups, tiled=True)  5.14 us
    unnamed x12, local copies, waits for them, and re-layouts  1.69 us
    ppermute x1, starting transfers between devices, shards(): lax.ppermute(tails, BLOCK, [(i, i + 1) for i in range(2 * chips - 1)])  1.44 us
  transfers between devices with their start and end apart: 6, of which 4 were waited for; matrix products, arithmetic and copies ran while one was open for 0% of the time, Pallas kernels for 17%

profile of v10, /device:TPU:0, one launch (start us, length us, event | category | flops | bytes accessed | tf_op | source)
XLA Modules:
  0.0 32.5 jit_solution(2775970043213108473)
XLA Ops:
  0.0 0.5 %collective-permute-start.1 = (bf16[128,1024]{1,0:T(8,128)(2,1)}, bf16[128,1024]{1,0:T(8,128)(2,1)S(1)}, u32[]{:S(2)}, u32[]{:S(2)}) collective-permute-start(bf16[128,1024]{1,0:T(8,128)(2,1)} %v_ref.1), channel_id=1, source_target_pairs={{0,1},{1,0},{2,3},{3,2},{4,5},{5,4},{6,7},{7,6},{8,9},{9,8},{10,11... | collective-permute-start | bytes 786440 | tf_op jit(solution)/shard_map/ppermute | solution.py:395
  0.5 0.1 collective-permute-start
  0.5 1.4 %shard_map.46 = (f32[16,48,128]{2,1,0:T(8,128)S(1)}, bf16[80,2048]{1,0:T(8,128)(2,1)S(1)}, f32[3,512]{1,0:T(4,128)S(1)}) custom-call(bf16[128,512]{1,0:T(8,128)(2,1)} %qk_ref.5, bf16[128,1024]{1,0:T(8,128)(2,1)} %v_ref.1, f32[3,1024]{1,0:T(4,128)} %conv_ref.1, bf16[128,3072]{1,0:T(8,128)(2,1)} %swa_ref.1), custom_call_target="tpu_custom_call" | custom-call | tf_op jit(solution)/shard_map/pallas_call | solution.py:376
  1.9 0.1 collective-permute-done.refs_0_.other_qk_ref
  2.0 0.0 collective-permute-done.1.refs_1_.other_v_ref
  2.0 0.0 copy-start.2
  2.0 1.2 %shard_map.47 = bf16[16,48,128]{2,1,0:T(8,128)(2,1)} custom-call(bf16[128,512]{1,0:T(8,128)(2,1)S(1)} %collective-permute-done.refs_0_.other_qk_ref, bf16[128,1024]{1,0:T(8,128)(2,1)S(1)} %collective-permute-done.1.refs_1_.other_v_ref, f32[3,512]{1,0:T(4,128)S(1)} %get-tuple-element.17.refs_2_, f32[16,48,128]{2,1,0:T(8,128)S(1)} %get-tuple-element.18.refs_3_), custom_call_target="tpu_custom_call" | custom-call | tf_op jit(solution)/shard_map/pallas_call | solution.py:376
  3.2 0.0 copy-start
  3.2 8.9 %all-to-all-start = ((bf16[16,48,128]{2,1,0:T(8,128)(2,1)}), bf16[16,48,128]{2,1,0:T(8,128)(2,1)S(1)}, u32[]{:S(2)}, u32[]{:S(2)}) async-start(bf16[16,48,128]{2,1,0:T(8,128)(2,1)} %shard_map.47), calls=%async_computation | async-start | bytes 393216 | tf_op jit(solution)/shard_map/all_to_all | solution.py:399
  12.1 1.4 %collective-permute-start.2 = (bf16[80,2048]{1,0:T(8,128)(2,1)S(1)}, bf16[80,2048]{1,0:T(8,128)(2,1)S(1)}, u32[]{:S(2)}, u32[]{:S(2)}) collective-permute-start(bf16[80,2048]{1,0:T(8,128)(2,1)S(1)} %get-tuple-element.21), channel_id=1, source_target_pairs={{0,1},{1,2},{2,3},{3,4},{4,5},{5,6},{6,7},{7,8},{8,9},{9,10},{10,1... | collective-permute-start | bytes 983048 | tf_op jit(solution)/shard_map/ppermute | solution.py:428
  13.5 4.5 %all-to-all-done.parts_ref = bf16[16,48,128]{2,1,0:T(8,128)(2,1)S(1)} async-done(((bf16[16,48,128]{2,1,0:T(8,128)(2,1)}), bf16[16,48,128]{2,1,0:T(8,128)(2,1)S(1)}, u32[]{:S(2)}, u32[]{:S(2)}) %all-to-all-start) | async-done | bytes 196640 | tf_op jit(solution)/shard_map/all_to_all | solution.py:399
  18.1 1.2 %shard_map.48 = bf16[16,40,128]{2,1,0:T(8,128)(2,1)} custom-call(bf16[16,48,128]{2,1,0:T(8,128)(2,1)S(1)} %all-to-all-done.parts_ref), custom_call_target="tpu_custom_call" | custom-call | tf_op jit(solution)/shard_map/pallas_call | solution.py:376
  19.3 0.0 copy-start.1
  19.3 0.0 copy-start.5
  19.3 5.9 %all-to-all-start.1 = ((bf16[16,40,128]{2,1,0:T(8,128)(2,1)}), bf16[16,40,128]{2,1,0:T(8,128)(2,1)S(1)}, u32[]{:S(2)}, u32[]{:S(2)}) async-start(bf16[16,40,128]{2,1,0:T(8,128)(2,1)} %shard_map.48), calls=%async_computation.1 | async-start | bytes 327680 | tf_op jit(solution)/shard_map/all_to_all | solution.py:399
  25.1 0.0 collective-permute-done.2.tails_ref
  25.1 0.0 copy-start.3
  25.2 0.7 %copy-done.3 = bf16[80,2048]{1,0:T(8,128)(2,1)} copy-done((bf16[80,2048]{1,0:T(8,128)(2,1)}, bf16[80,2048]{1,0:T(8,128)(2,1)S(1)}, u32[]{:S(2)}) %copy-start.3) | copy-done | bytes 327704
  25.9 0.0 copy-done.2
  25.9 0.0 copy-done
  25.9 0.0 copy-done.1
  25.9 0.0 copy-done.5
  25.9 0.0 copy-start.4
  25.9 1.0 %copy-done.4 = bf16[80,2048]{1,0:T(8,128)(2,1)S(1)} copy-done((bf16[80,2048]{1,0:T(8,128)(2,1)S(1)}, bf16[80,2048]{1,0:T(8,128)(2,1)}, u32[]{:S(2)}) %copy-start.4) | copy-done | bytes 327704
  26.9 2.1 %shard_map.49 = (f32[128,1024]{1,0:T(8,128)S(1)}, f32[128,1024]{1,0:T(8,128)S(1)}, f32[128,1024]{1,0:T(8,128)S(1)}) custom-call(bf16[128,512]{1,0:T(8,128)(2,1)S(1)} %copy-done.1, bf16[128,1024]{1,0:T(8,128)(2,1)S(1)} %copy-done.2, f32[3,1024]{1,0:T(4,128)S(1)} %copy-done.5, bf16[128,3072]{1,0:T(8,128)(2,1)S(1)} %copy-done, bf16[80,2048]{1,0:T(8,128)(2,1)S(1)} %copy-done.4, ...), custom_call_target="tpu_custom_call" | custom-call | tf_op jit(solution)/shard_map/pallas_call | solution.py:376
  29.0 0.6 %all-to-all-done.1 = bf16[16,40,128]{2,1,0:T(8,128)(2,1)S(1)} async-done(((bf16[16,40,128]{2,1,0:T(8,128)(2,1)}), bf16[16,40,128]{2,1,0:T(8,128)(2,1)S(1)}, u32[]{:S(2)}, u32[]{:S(2)}) %all-to-all-start.1) | async-done | bytes 163872 | tf_op jit(solution)/shard_map/all_to_all | solution.py:399
  29.6 0.0 collective-permute-start.3
  29.6 0.8 %shard_map.50.refs_0_ = bf16[128,512]{1,0:T(8,128)(2,1)S(1)} custom-call(bf16[128,512]{1,0:T(8,128)(2,1)S(1)} %copy-done.1, f32[128,1024]{1,0:T(8,128)S(1)} %get-tuple-element.25.numer_ref, f32[128,1024]{1,0:T(8,128)S(1)} %get-tuple-element.26.denom_ref, f32[128,1024]{1,0:T(8,128)S(1)} %get-tuple-element.27.swa_ref, bf16[640,128]{1,0:T(8,128)(2,1)S(1)} %bitcast.2), custom_call_target="tpu_custom_call" | custom-call | tf_op jit(solution)/shard_map/pallas_call | solution.py:376
  30.4 0.6 %collective-permute-done.3.past_ref = bf16[640,128]{1,0:T(8,128)(2,1)S(1)} collective-permute-done((bf16[640,128]{1,0:T(8,128)(2,1)S(1)}, bf16[640,128]{1,0:T(8,128)(2,1)S(1)}, u32[]{:S(2)}, u32[]{:S(2)}) %collective-permute-start.3) | collective-permute-done | bytes 163872 | tf_op jit(solution)/shard_map/ppermute | solution.py:395
  31.0 1.5 %shard_map.51 = bf16[128,1024]{1,0:T(8,128)(2,1)} custom-call(bf16[128,512]{1,0:T(8,128)(2,1)S(1)} %copy-done.1, f32[128,1024]{1,0:T(8,128)S(1)} %get-tuple-element.25.numer_ref, f32[128,1024]{1,0:T(8,128)S(1)} %get-tuple-element.26.denom_ref, f32[128,1024]{1,0:T(8,128)S(1)} %get-tuple-element.27.swa_ref, ...), custom_call_target="tpu_custom_call" | custom-call | tf_op jit(solution)/shard_map/pallas_call | solution.py:376
Async XLA Ops:
  0.0 2.0 %collective-permute-start.1 = (bf16[128,1024]{1,0:T(8,128)(2,1)}, bf16[128,1024]{1,0:T(8,128)(2,1)S(1)}, u32[]{:S(2)}, u32[]{:S(2)}) collective-permute-start(bf16[128,1024]{1,0:T(8,128)(2,1)} %v_ref.1), channel_id=1, source_target_pairs={{0,1},{1,0},{2,3},{3,2},{4,5},{5,4},{6,7},{7,6},{8,9},{9,8},{10,11... | collective-permute-start | bytes 786440 | tf_op jit(solution)/shard_map/ppermute | solution.py:395
  0.5 1.6 %collective-permute-start = (bf16[128,512]{1,0:T(8,128)(2,1)}, bf16[128,512]{1,0:T(8,128)(2,1)S(1)}, u32[]{:S(2)}, u32[]{:S(2)}) collective-permute-start(bf16[128,512]{1,0:T(8,128)(2,1)} %qk_ref.5), channel_id=1, source_target_pairs={{0,1},{1,0},{2,3},{3,2},{4,5},{5,4},{6,7},{7,6},{8,9},{9,8},{10,11... | collective-permute-start | bytes 393224 | tf_op jit(solution)/shard_map/ppermute | solution.py:395
  2.0 23.8 %copy-start.2 = (bf16[128,1024]{1,0:T(8,128)(2,1)S(1)}, bf16[128,1024]{1,0:T(8,128)(2,1)}, u32[]{:S(2)}) copy-start(bf16[128,1024]{1,0:T(8,128)(2,1)} %v_ref.1) | copy-start | bytes 786436
  3.2 22.7 %copy-start = (bf16[128,3072]{1,0:T(8,128)(2,1)S(1)}, bf16[128,3072]{1,0:T(8,128)(2,1)}, u32[]{:S(2)}) copy-start(bf16[128,3072]{1,0:T(8,128)(2,1)} %swa_ref.1) | copy-start | bytes 2359300
  3.2 14.9 %all-to-all-start = ((bf16[16,48,128]{2,1,0:T(8,128)(2,1)}), bf16[16,48,128]{2,1,0:T(8,128)(2,1)S(1)}, u32[]{:S(2)}, u32[]{:S(2)}) async-start(bf16[16,48,128]{2,1,0:T(8,128)(2,1)} %shard_map.47), calls=%async_computation | async-start | bytes 393216 | tf_op jit(solution)/shard_map/all_to_all | solution.py:399
  12.1 13.1 %collective-permute-start.2 = (bf16[80,2048]{1,0:T(8,128)(2,1)S(1)}, bf16[80,2048]{1,0:T(8,128)(2,1)S(1)}, u32[]{:S(2)}, u32[]{:S(2)}) collective-permute-start(bf16[80,2048]{1,0:T(8,128)(2,1)S(1)} %get-tuple-element.21), channel_id=1, source_target_pairs={{0,1},{1,2},{2,3},{3,4},{4,5},{5,6},{6,7},{7,8},{8,9},{9,10},{10,1... | collective-permute-start | bytes 983048 | tf_op jit(solution)/shard_map/ppermute | solution.py:428
  19.3 6.6 %copy-start.1 = (bf16[128,512]{1,0:T(8,128)(2,1)S(1)}, bf16[128,512]{1,0:T(8,128)(2,1)}, u32[]{:S(2)}) copy-start(bf16[128,512]{1,0:T(8,128)(2,1)} %qk_ref.5) | copy-start | bytes 393220
  19.3 6.6 %copy-start.5 = (f32[3,1024]{1,0:T(4,128)S(1)}, f32[3,1024]{1,0:T(4,128)}, u32[]{:S(2)}) copy-start(f32[3,1024]{1,0:T(4,128)} %conv_ref.1) | copy-start | bytes 36868
  19.3 10.3 %all-to-all-start.1 = ((bf16[16,40,128]{2,1,0:T(8,128)(2,1)}), bf16[16,40,128]{2,1,0:T(8,128)(2,1)S(1)}, u32[]{:S(2)}, u32[]{:S(2)}) async-start(bf16[16,40,128]{2,1,0:T(8,128)(2,1)} %shard_map.48), calls=%async_computation.1 | async-start | bytes 327680 | tf_op jit(solution)/shard_map/all_to_all | solution.py:399
  25.1 0.7 %copy-start.3 = (bf16[80,2048]{1,0:T(8,128)(2,1)}, bf16[80,2048]{1,0:T(8,128)(2,1)S(1)}, u32[]{:S(2)}) copy-start(bf16[80,2048]{1,0:T(8,128)(2,1)S(1)} %collective-permute-done.2.tails_ref) | copy-start | bytes 983044
  25.9 1.0 %copy-start.4 = (bf16[80,2048]{1,0:T(8,128)(2,1)S(1)}, bf16[80,2048]{1,0:T(8,128)(2,1)}, u32[]{:S(2)}) copy-start(bf16[80,2048]{1,0:T(8,128)(2,1)} %copy-done.3) | copy-start | bytes 983044
  29.6 1.4 %collective-permute-start.3 = (bf16[640,128]{1,0:T(8,128)(2,1)S(1)}, bf16[640,128]{1,0:T(8,128)(2,1)S(1)}, u32[]{:S(2)}, u32[]{:S(2)}) collective-permute-start(bf16[640,128]{1,0:T(8,128)(2,1)S(1)} %bitcast.1), channel_id=1, source_target_pairs={{0,1},{1,0},{2,3},{3,2},{4,5},{5,4},{6,7},{7,6},{8,9},{9,8},{10,11... | collective-permute-start | bytes 491528 | tf_op jit(solution)/shard_map/ppermute | solution.py:395
